TPU v7x, 32 devices: a whole 2x2x4 slice. The times are simulated.
32 devices in a mesh: row: 4 (over z), col: 8 (over y, x, core).
Axes of the slice: x: 2, y: 2, z: 4, core: 2. Of those that a mesh axis runs over, the one named last changes fastest.
Arguments:
- feature: bfloat16 [64, 32, 1024], P(None, 'row', 'col'), may hold values from -6 to 6
- cotangent: bfloat16 [64, 32, 1024], P(None, 'row', 'col'), may hold values from -6 to 6
- order_weight: bfloat16 [6, 64, 64], replicated, may hold values from -0.75 to 0.75
- pixel_mask: int32 [32, 1024], P('row', 'col'), may hold values 0 or 1
Outputs:
- grad_feature: bfloat16 [64, 32, 1024], P(None, 'row', 'col')
- grad_order: float32 [6, 64, 64], replicated
Inputs may be any that keep to these rules, and one draw needn't show every extreme that they name: `pixel_mask`: 1 where a pixel is observed, 0 where it is masked.
All inputs are finite; a program needn't handle non-finite values. No bound on the sum of `pixel_mask` on one device may be relied on, other than what follows from the above.
Results may differ from a plain program's by a relative error of at most 0.0054.
Values may be sent and summed in bfloat16 or wider, within the bound.
No kernel may reach another device: no remote copies, remote signals or barrier semaphores. Data moves between devices by JAX's collectives and lax.ppermute only.
A program may use at most 64 MiB of HBM per device.

v0:
```python
import math

import jax
import jax.numpy as jnp
from jax import lax
from jax.sharding import PartitionSpec as P


def with_halo(cells, sides, width):
    for axis, dim in sides:
        count = lax.axis_size(axis)
        ends = count - 1
        head = lax.slice_in_dim(cells, 0, width, axis=dim)
        tail = lax.slice_in_dim(cells, cells.shape[dim] - width, cells.shape[dim], axis=dim)
        cells = jnp.concatenate(
            [
                lax.ppermute(tail, axis, [(i, (i + 1) % count) for i in range(ends)]),
                cells,
                lax.ppermute(head, axis, [((i + 1) % count, i) for i in range(ends)]),
            ],
            axis=dim,
        )
    return cells


def neighbour_sum(u):
    row_sums = u[..., :-2, :] + u[..., 1:-1, :] + u[..., 2:, :]
    box = row_sums[..., :-2] + row_sums[..., 1:-1] + row_sums[..., 2:]
    return box - u[..., 1:-1, 1:-1]


def trim_rim(v, have, want):
    off = have - want
    return v[..., off : v.shape[-2] - off, off : v.shape[-1] - off]


def body(feature, cotangent, order_weight, pixel_mask):
    orders = order_weight.shape[0]
    mask_wide = with_halo(pixel_mask, (("row", 0), ("col", 1)), 6)
    mask_float = mask_wide.astype(jnp.float32)
    mask_inner = trim_rim(mask_float, 6, 5)
    degree = mask_inner * neighbour_sum(mask_float)
    scales = mask_inner / jnp.sqrt(jnp.maximum(degree, 1.0))

    def apply_laplacian(v, reach):
        weighted = trim_rim(scales, 5, reach) * v.astype(jnp.float32)
        return -trim_rim(scales, 5, reach - 1) * neighbour_sum(weighted)

    def mix(k, source):
        return jnp.einsum(
            "io,ohw->ihw", order_weight[k], source, preferred_element_type=jnp.float32
        )

    def cycle_one(v):
        return with_halo(v, (("row", 1), ("col", 2)), 1)

    cheb_terms = [feature, apply_laplacian(cycle_one(feature), 1).astype(jnp.bfloat16)]
    for k in range(2, orders):
        fresh = 2.0 * apply_laplacian(cycle_one(cheb_terms[k - 1]), 1) - cheb_terms[k - 2].astype(
            jnp.float32
        )
        cheb_terms.append(fresh.astype(jnp.bfloat16))
    adj_next = mix(orders - 1, cotangent).astype(jnp.bfloat16)
    adj_after = None
    for k in range(orders - 2, 0, -1):
        update = mix(k, cotangent) + 2.0 * apply_laplacian(cycle_one(adj_next), 1)
        if adj_after is not None:
            update = update - adj_after.astype(jnp.float32)
        adj_after, adj_next = (adj_next, update.astype(jnp.bfloat16))
    grad_feature = (
        mix(0, cotangent) + apply_laplacian(cycle_one(adj_next), 1) - adj_after.astype(jnp.float32)
    ).astype(jnp.bfloat16)
    partial_grads = jnp.stack(
        [
            jnp.einsum("ihw,ohw->io", t, cotangent, preferred_element_type=jnp.float32)
            for t in cheb_terms
        ]
    )
    summed = lax.psum(partial_grads, ("row", "col"))
    pixel_count = feature.shape[1] * feature.shape[2] * lax.axis_size("row") * lax.axis_size("col")
    grad_order = summed / math.sqrt(pixel_count)
    return (grad_feature, grad_order)


def solution(mesh):
    placed = (P(None, "row", "col"), P(None, "row", "col"), P(), P("row", "col"))
    return jax.shard_map(
        body, mesh=mesh, in_specs=placed, out_specs=(P(None, "row", "col"), P()), check_vma=False
    )
```

profile of v0, /device:TPU:0, one launch (start us, length us, event | category | flops | bytes accessed | tf_op | source)
XLA Modules:
  0.0 310.6 jit_solution(14759283237119570238)
XLA Ops:
  7.2 0.8 fusion.95
  8.0 4.9 %collective-permute-start = (s32[6,128]{1,0:T(8,128)S(1)}, s32[6,128]{1,0:T(8,128)S(1)}, u32[]{:S(2)}, u32[]{:S(2)}) collective-permute-start(s32[6,128]{1,0:T(8,128)S(1)} %get-tuple-element.50), channel_id=1, source_target_pairs={{0,8},{8,16},{16,24},{1,9},{9,17},{17,25},{2,10},{10,18},{18,26},{... | collective-permute-start | bytes 9224 | tf_op jit(solution)/shard_map/ppermute | solution.py:17
  12.9 1.3 collective-permute-start.1
  14.3 4.2 %collective-permute-done.1 = s32[6,128]{1,0:T(8,128)S(1)} collective-permute-done((s32[6,128]{1,0:T(8,128)S(1)}, s32[6,128]{1,0:T(8,128)S(1)}, u32[]{:S(2)}, u32[]{:S(2)}) %collective-permute-start.1) | collective-permute-done | bytes 3104 | tf_op jit(solution)/shard_map/ppermute | solution.py:19
  18.5 1.3 collective-permute-start.2
  19.8 1.3 collective-permute-start.3
  21.1 1.0 fusion.88
  22.2 3.5 %collective-permute-start.24 = (bf16[64,1,128]{2,0,1:T(8,128)(2,1)S(1)}, bf16[64,1,128]{2,0,1:T(8,128)(2,1)S(1)}, u32[]{:S(2)}, u32[]{:S(2)}) collective-permute-start(bf16[64,1,128]{2,0,1:T(8,128)(2,1)S(1)} %copy.52), channel_id=1, source_target_pairs={{0,8},{8,16},{16,24},{1,9},{9,17},{17,25},{2,10},{10,18},{18,26},{... | collective-permute-start | bytes 49160 | tf_op jit(solution)/shard_map/ppermute | solution.py:17
  25.7 1.3 collective-permute-start.25
  27.2 0.8 copy-done.1
  28.0 3.3 %collective-permute-done.25 = bf16[64,1,128]{2,0,1:T(8,128)(2,1)S(1)} collective-permute-done((bf16[64,1,128]{2,0,1:T(8,128)(2,1)S(1)}, bf16[64,1,128]{2,0,1:T(8,128)(2,1)S(1)}, u32[]{:S(2)}, u32[]{:S(2)}) %collective-permute-start.25) | collective-permute-done | bytes 16416 | tf_op jit(solution)/shard_map/ppermute | solution.py:19
  31.4 3.3 %collective-permute-start.26 = (bf16[64,10,1]{2,0,1:T(8,128)(2,1)S(1)}, bf16[64,10,1]{2,0,1:T(8,128)(2,1)S(1)}, u32[]{:S(2)}, u32[]{:S(2)}) collective-permute-start(bf16[64,10,1]{2,0,1:T(8,128)(2,1)S(1)} %get-tuple-element.12), channel_id=1, source_target_pairs={{0,1},{1,2},{2,3},{3,4},{4,5},{5,6},{6,7},{8,9},{9,10},{10,11},{11... | collective-permute-start | bytes 3848 | tf_op jit(solution)/shard_map/ppermute | solution.py:17
  34.8 1.3 collective-permute-start.27
  36.2 4.5 %collective-permute-done.27 = bf16[64,10,1]{2,0,1:T(8,128)(2,1)S(1)} collective-permute-done((bf16[64,10,1]{2,0,1:T(8,128)(2,1)S(1)}, bf16[64,10,1]{2,0,1:T(8,128)(2,1)S(1)}, u32[]{:S(2)}, u32[]{:S(2)}) %collective-permute-start.27) | collective-permute-done | bytes 1312 | tf_op jit(solution)/shard_map/ppermute | solution.py:19
  41.3 3.5 %collective-permute-start.28 = (bf16[64,1,128]{2,0,1:T(8,128)(2,1)S(1)}, bf16[64,1,128]{2,0,1:T(8,128)(2,1)S(1)}, u32[]{:S(2)}, u32[]{:S(2)}) collective-permute-start(bf16[64,1,128]{2,0,1:T(8,128)(2,1)S(1)} %get-tuple-element.30), channel_id=1, source_target_pairs={{0,8},{8,16},{16,24},{1,9},{9,17},{17,25},{2,10},{10,18},{18,26},{... | collective-permute-start | bytes 49160 | tf_op jit(solution)/shard_map/ppermute | solution.py:17
  44.8 1.3 collective-permute-start.29
  46.2 4.2 %collective-permute-done.29 = bf16[64,1,128]{2,0,1:T(8,128)(2,1)S(1)} collective-permute-done((bf16[64,1,128]{2,0,1:T(8,128)(2,1)S(1)}, bf16[64,1,128]{2,0,1:T(8,128)(2,1)S(1)}, u32[]{:S(2)}, u32[]{:S(2)}) %collective-permute-start.29) | collective-permute-done | bytes 16416 | tf_op jit(solution)/shard_map/ppermute | solution.py:19
  50.6 4.3 %collective-permute-start.30 = (bf16[64,10,1]{2,0,1:T(8,128)(2,1)S(1)}, bf16[64,10,1]{2,0,1:T(8,128)(2,1)S(1)}, u32[]{:S(2)}, u32[]{:S(2)}) collective-permute-start(bf16[64,10,1]{2,0,1:T(8,128)(2,1)S(1)} %get-tuple-element.10), channel_id=1, source_target_pairs={{0,1},{1,2},{2,3},{3,4},{4,5},{5,6},{6,7},{8,9},{9,10},{10,11},{11... | collective-permute-start | bytes 3848 | tf_op jit(solution)/shard_map/ppermute | solution.py:17
  54.9 1.3 collective-permute-start.31
  56.5 2.6 collective-permute-done.31
  59.6 1.9 collective-permute-start.32
  61.5 1.3 collective-permute-start.33
  62.8 4.5 %collective-permute-start.4 = (bf16[64,1,128]{2,0,1:T(8,128)(2,1)S(1)}, bf16[64,1,128]{2,0,1:T(8,128)(2,1)S(1)}, u32[]{:S(2)}, u32[]{:S(2)}) collective-permute-start(bf16[64,1,128]{2,0,1:T(8,128)(2,1)S(1)} %get-tuple-element.42), channel_id=1, source_target_pairs={{0,8},{8,16},{16,24},{1,9},{9,17},{17,25},{2,10},{10,18},{18,26},{... | collective-permute-start | bytes 49160 | tf_op jit(solution)/shard_map/ppermute | solution.py:17
  67.4 1.3 collective-permute-start.5
  68.9 5.7 %collective-permute-start.34 = (bf16[64,10,1]{2,0,1:T(8,128)(2,1)S(1)}, bf16[64,10,1]{2,0,1:T(8,128)(2,1)S(1)}, u32[]{:S(2)}, u32[]{:S(2)}) collective-permute-start(bf16[64,10,1]{2,0,1:T(8,128)(2,1)S(1)} %get-tuple-element.8), channel_id=1, source_target_pairs={{0,1},{1,2},{2,3},{3,4},{4,5},{5,6},{6,7},{8,9},{9,10},{10,11},{11... | collective-permute-start | bytes 3848 | tf_op jit(solution)/shard_map/ppermute | solution.py:17
  74.6 1.3 collective-permute-start.35
  76.0 2.1 collective-permute-done.35
  78.7 4.5 %collective-permute-start.36 = (bf16[64,1,128]{2,0,1:T(8,128)(2,1)S(1)}, bf16[64,1,128]{2,0,1:T(8,128)(2,1)S(1)}, u32[]{:S(2)}, u32[]{:S(2)}) collective-permute-start(bf16[64,1,128]{2,0,1:T(8,128)(2,1)S(1)} %get-tuple-element.26), channel_id=1, source_target_pairs={{0,8},{8,16},{16,24},{1,9},{9,17},{17,25},{2,10},{10,18},{18,26},{... | collective-permute-start | bytes 49160 | tf_op jit(solution)/shard_map/ppermute | solution.py:17
  83.2 1.3 collective-permute-start.37
  84.6 6.4 %collective-permute-start.6 = (bf16[64,10,1]{2,0,1:T(8,128)(2,1)S(1)}, bf16[64,10,1]{2,0,1:T(8,128)(2,1)S(1)}, u32[]{:S(2)}, u32[]{:S(2)}) collective-permute-start(bf16[64,10,1]{2,0,1:T(8,128)(2,1)S(1)} %get-tuple-element.22), channel_id=1, source_target_pairs={{0,1},{1,2},{2,3},{3,4},{4,5},{5,6},{6,7},{8,9},{9,10},{10,11},{11... | collective-permute-start | bytes 3848 | tf_op jit(solution)/shard_map/ppermute | solution.py:17
  91.0 1.3 collective-permute-start.7
  92.5 3.0 collective-permute-start.38
  95.5 1.3 collective-permute-start.39
  97.1 4.3 %collective-permute-done.39 = bf16[64,10,1]{2,0,1:T(8,128)(2,1)S(1)} collective-permute-done((bf16[64,10,1]{2,0,1:T(8,128)(2,1)S(1)}, bf16[64,10,1]{2,0,1:T(8,128)(2,1)S(1)}, u32[]{:S(2)}, u32[]{:S(2)}) %collective-permute-start.39) | collective-permute-done | bytes 1312 | tf_op jit(solution)/shard_map/ppermute | solution.py:19
  102.1 4.3 %collective-permute-start.40 = (bf16[64,1,128]{2,0,1:T(8,128)(2,1)S(1)}, bf16[64,1,128]{2,0,1:T(8,128)(2,1)S(1)}, u32[]{:S(2)}, u32[]{:S(2)}) collective-permute-start(bf16[64,1,128]{2,0,1:T(8,128)(2,1)S(1)} %get-tuple-element.24), channel_id=1, source_target_pairs={{0,8},{8,16},{16,24},{1,9},{9,17},{17,25},{2,10},{10,18},{18,26},{... | collective-permute-start | bytes 49160 | tf_op jit(solution)/shard_map/ppermute | solution.py:17
  106.4 1.3 collective-permute-start.41
  108.0 4.5 %collective-permute-start.8 = (bf16[64,1,128]{2,0,1:T(8,128)(2,1)S(1)}, bf16[64,1,128]{2,0,1:T(8,128)(2,1)S(1)}, u32[]{:S(2)}, u32[]{:S(2)}) collective-permute-start(bf16[64,1,128]{2,0,1:T(8,128)(2,1)S(1)} %get-tuple-element.40), channel_id=1, source_target_pairs={{0,8},{8,16},{16,24},{1,9},{9,17},{17,25},{2,10},{10,18},{18,26},{... | collective-permute-start | bytes 49160 | tf_op jit(solution)/shard_map/ppermute | solution.py:17
  112.6 1.3 collective-permute-start.9
  114.1 5.4 %collective-permute-start.42 = (bf16[64,10,1]{2,0,1:T(8,128)(2,1)S(1)}, bf16[64,10,1]{2,0,1:T(8,128)(2,1)S(1)}, u32[]{:S(2)}, u32[]{:S(2)}) collective-permute-start(bf16[64,10,1]{2,0,1:T(8,128)(2,1)S(1)} %get-tuple-element.4), channel_id=1, source_target_pairs={{0,1},{1,2},{2,3},{3,4},{4,5},{5,6},{6,7},{8,9},{9,10},{10,11},{11... | collective-permute-start | bytes 3848 | tf_op jit(solution)/shard_map/ppermute | solution.py:17
  119.4 1.3 collective-permute-start.43
  120.9 3.2 %collective-permute-start.10 = (bf16[64,10,1]{2,0,1:T(8,128)(2,1)S(1)}, bf16[64,10,1]{2,0,1:T(8,128)(2,1)S(1)}, u32[]{:S(2)}, u32[]{:S(2)}) collective-permute-start(bf16[64,10,1]{2,0,1:T(8,128)(2,1)S(1)} %get-tuple-element.20), channel_id=1, source_target_pairs={{0,1},{1,2},{2,3},{3,4},{4,5},{5,6},{6,7},{8,9},{9,10},{10,11},{11... | collective-permute-start | bytes 3848 | tf_op jit(solution)/shard_map/ppermute | solution.py:17
  124.1 1.3 collective-permute-start.11
  125.6 4.1 %collective-permute-done.11 = bf16[64,10,1]{2,0,1:T(8,128)(2,1)S(1)} collective-permute-done((bf16[64,10,1]{2,0,1:T(8,128)(2,1)S(1)}, bf16[64,10,1]{2,0,1:T(8,128)(2,1)S(1)}, u32[]{:S(2)}, u32[]{:S(2)}) %collective-permute-start.11) | collective-permute-done | bytes 1312 | tf_op jit(solution)/shard_map/ppermute | solution.py:19
  130.5 4.3 %collective-permute-start.12 = (bf16[64,1,128]{2,0,1:T(8,128)(2,1)S(1)}, bf16[64,1,128]{2,0,1:T(8,128)(2,1)S(1)}, u32[]{:S(2)}, u32[]{:S(2)}) collective-permute-start(bf16[64,1,128]{2,0,1:T(8,128)(2,1)S(1)} %get-tuple-element.38), channel_id=1, source_target_pairs={{0,8},{8,16},{16,24},{1,9},{9,17},{17,25},{2,10},{10,18},{18,26},{... | collective-permute-start | bytes 49160 | tf_op jit(solution)/shard_map/ppermute | solution.py:17
  134.8 1.3 collective-permute-start.13
  136.3 4.1 %collective-permute-done.13 = bf16[64,1,128]{2,0,1:T(8,128)(2,1)S(1)} collective-permute-done((bf16[64,1,128]{2,0,1:T(8,128)(2,1)S(1)}, bf16[64,1,128]{2,0,1:T(8,128)(2,1)S(1)}, u32[]{:S(2)}, u32[]{:S(2)}) %collective-permute-start.13) | collective-permute-done | bytes 16416 | tf_op jit(solution)/shard_map/ppermute | solution.py:19
  140.6 5.3 %collective-permute-start.14 = (bf16[64,10,1]{2,0,1:T(8,128)(2,1)S(1)}, bf16[64,10,1]{2,0,1:T(8,128)(2,1)S(1)}, u32[]{:S(2)}, u32[]{:S(2)}) collective-permute-start(bf16[64,10,1]{2,0,1:T(8,128)(2,1)S(1)} %get-tuple-element.18), channel_id=1, source_target_pairs={{0,1},{1,2},{2,3},{3,4},{4,5},{5,6},{6,7},{8,9},{9,10},{10,11},{11... | collective-permute-start | bytes 3848 | tf_op jit(solution)/shard_map/ppermute | solution.py:17
  145.9 1.3 collective-permute-start.15
  147.4 2.6 collective-permute-done.15
  150.6 1.9 collective-permute-start.16
  152.5 1.3 collective-permute-start.17
  154.0 4.1 %collective-permute-done.17 = bf16[64,1,128]{2,0,1:T(8,128)(2,1)S(1)} collective-permute-done((bf16[64,1,128]{2,0,1:T(8,128)(2,1)S(1)}, bf16[64,1,128]{2,0,1:T(8,128)(2,1)S(1)}, u32[]{:S(2)}, u32[]{:S(2)}) %collective-permute-start.17) | collective-permute-done | bytes 16416 | tf_op jit(solution)/shard_map/ppermute | solution.py:19
  158.3 5.2 %collective-permute-start.18 = (bf16[64,10,1]{2,0,1:T(8,128)(2,1)S(1)}, bf16[64,10,1]{2,0,1:T(8,128)(2,1)S(1)}, u32[]{:S(2)}, u32[]{:S(2)}) collective-permute-start(bf16[64,10,1]{2,0,1:T(8,128)(2,1)S(1)} %get-tuple-element.16), channel_id=1, source_target_pairs={{0,1},{1,2},{2,3},{3,4},{4,5},{5,6},{6,7},{8,9},{9,10},{10,11},{11... | collective-permute-start | bytes 3848 | tf_op jit(solution)/shard_map/ppermute | solution.py:17
  163.6 1.3 collective-permute-start.19
  164.9 2.7 collective-permute-done.19
  168.2 1.9 collective-permute-start.20
  170.1 1.3 collective-permute-start.21
  171.8 0.7 copy-done.2
  172.6 3.2 %collective-permute-done.21 = bf16[64,1,128]{2,0,1:T(8,128)(2,1)S(1)} collective-permute-done((bf16[64,1,128]{2,0,1:T(8,128)(2,1)S(1)}, bf16[64,1,128]{2,0,1:T(8,128)(2,1)S(1)}, u32[]{:S(2)}, u32[]{:S(2)}) %collective-permute-start.21) | collective-permute-done | bytes 16416 | tf_op jit(solution)/shard_map/ppermute | solution.py:19
  175.9 5.2 %collective-permute-start.22 = (bf16[64,10,1]{2,0,1:T(8,128)(2,1)S(1)}, bf16[64,10,1]{2,0,1:T(8,128)(2,1)S(1)}, u32[]{:S(2)}, u32[]{:S(2)}) collective-permute-start(bf16[64,10,1]{2,0,1:T(8,128)(2,1)S(1)} %get-tuple-element.14), channel_id=1, source_target_pairs={{0,1},{1,2},{2,3},{3,4},{4,5},{5,6},{6,7},{8,9},{9,10},{10,11},{11... | collective-permute-start | bytes 3848 | tf_op jit(solution)/shard_map/ppermute | solution.py:17
  181.2 1.3 collective-permute-start.23
  182.5 118.3 %all-reduce.2.cloned.1.call-done = f32[6,64,64]{2,1,0:T(8,128)} async-done(((f32[6,64,64]{2,1,0:T(8,128)}), f32[6,64,64]{2,1,0:T(8,128)}) %all-reduce.2.cloned.1.call-update) | async-done | bytes 98320 | tf_op jit(solution)/shard_map/psum | solution.py:79
  300.8 1.6 broadcast_multiply_fusion
  303.0 0.7 copy.23
  (115 shorter events, 8.8 us)
Async XLA Ops:
  7.2 49.1 %copy-start = (bf16[64,8,128]{2,1,0:T(8,128)(2,1)S(1)}, bf16[64,8,128]{2,1,0:T(8,128)(2,1)}, u32[]{:S(2)}) copy-start(bf16[64,8,128]{2,1,0:T(8,128)(2,1)} %param.5) | copy-start | bytes 393220
  7.2 293.6 %all-reduce.2.cloned.1.call-start = ((), (), s32[]{:S(2)}) async-start(), calls=%async_computation | async-start | bytes 393216 | tf_op jit(solution)/shard_map/psum | solution.py:79
  7.2 11.2 %copy-start.4 = (s32[8,128]{1,0:T(8,128)S(1)}, s32[8,128]{1,0:T(8,128)}, u32[]{:S(2)}) copy-start(s32[8,128]{1,0:T(8,128)} %param.7) | copy-start | bytes 12292
  8.0 6.2 %collective-permute-start = (s32[6,128]{1,0:T(8,128)S(1)}, s32[6,128]{1,0:T(8,128)S(1)}, u32[]{:S(2)}, u32[]{:S(2)}) collective-permute-start(s32[6,128]{1,0:T(8,128)S(1)} %get-tuple-element.50), channel_id=1, source_target_pairs={{0,8},{8,16},{16,24},{1,9},{9,17},{17,25},{2,10},{10,18},{18,26},{... | collective-permute-start | bytes 9224 | tf_op jit(solution)/shard_map/ppermute | solution.py:17
  12.9 5.5 %collective-permute-start.1 = (s32[6,128]{1,0:T(8,128)S(1)}, s32[6,128]{1,0:T(8,128)S(1)}, u32[]{:S(2)}, u32[]{:S(2)}) collective-permute-start(s32[6,128]{1,0:T(8,128)S(1)} %get-tuple-element.51), channel_id=1, source_target_pairs={{8,0},{16,8},{24,16},{9,1},{17,9},{25,17},{10,2},{18,10},{26,18},{... | collective-permute-start | bytes 9224 | tf_op jit(solution)/shard_map/ppermute | solution.py:19
  18.5 8.4 %collective-permute-start.2 = (s32[20,6]{1,0:T(8,128)S(1)}, s32[20,6]{1,0:T(8,128)S(1)}, u32[]{:S(2)}, u32[]{:S(2)}) collective-permute-start(s32[20,6]{1,0:T(8,128)S(1)} %get-tuple-element.48), channel_id=1, source_target_pairs={{0,1},{1,2},{2,3},{3,4},{4,5},{5,6},{6,7},{8,9},{9,10},{10,11},{11... | collective-permute-start | bytes 1448 | tf_op jit(solution)/shard_map/ppermute | solution.py:17
  19.8 7.2 %collective-permute-start.3 = (s32[20,6]{1,0:T(8,128)S(1)}, s32[20,6]{1,0:T(8,128)S(1)}, u32[]{:S(2)}, u32[]{:S(2)}) collective-permute-start(s32[20,6]{1,0:T(8,128)S(1)} %get-tuple-element.49), channel_id=1, source_target_pairs={{1,0},{2,1},{3,2},{4,3},{5,4},{6,5},{7,6},{9,8},{10,9},{11,10},{12... | collective-permute-start | bytes 1448 | tf_op jit(solution)/shard_map/ppermute | solution.py:19
  22.2 5.1 %collective-permute-start.24 = (bf16[64,1,128]{2,0,1:T(8,128)(2,1)S(1)}, bf16[64,1,128]{2,0,1:T(8,128)(2,1)S(1)}, u32[]{:S(2)}, u32[]{:S(2)}) collective-permute-start(bf16[64,1,128]{2,0,1:T(8,128)(2,1)S(1)} %copy.52), channel_id=1, source_target_pairs={{0,8},{8,16},{16,24},{1,9},{9,17},{17,25},{2,10},{10,18},{18,26},{... | collective-permute-start | bytes 49160 | tf_op jit(solution)/shard_map/ppermute | solution.py:17
  25.7 5.6 %collective-permute-start.25 = (bf16[64,1,128]{2,0,1:T(8,128)(2,1)S(1)}, bf16[64,1,128]{2,0,1:T(8,128)(2,1)S(1)}, u32[]{:S(2)}, u32[]{:S(2)}) collective-permute-start(bf16[64,1,128]{2,0,1:T(8,128)(2,1)S(1)} %copy.53), channel_id=1, source_target_pairs={{8,0},{16,8},{24,16},{9,1},{17,9},{25,17},{10,2},{18,10},{26,18},{... | collective-permute-start | bytes 49160 | tf_op jit(solution)/shard_map/ppermute | solution.py:19
  27.1 0.9 copy-start.1
  31.4 4.8 %collective-permute-start.26 = (bf16[64,10,1]{2,0,1:T(8,128)(2,1)S(1)}, bf16[64,10,1]{2,0,1:T(8,128)(2,1)S(1)}, u32[]{:S(2)}, u32[]{:S(2)}) collective-permute-start(bf16[64,10,1]{2,0,1:T(8,128)(2,1)S(1)} %get-tuple-element.12), channel_id=1, source_target_pairs={{0,1},{1,2},{2,3},{3,4},{4,5},{5,6},{6,7},{8,9},{9,10},{10,11},{11... | collective-permute-start | bytes 3848 | tf_op jit(solution)/shard_map/ppermute | solution.py:17
  34.8 5.9 %collective-permute-start.27 = (bf16[64,10,1]{2,0,1:T(8,128)(2,1)S(1)}, bf16[64,10,1]{2,0,1:T(8,128)(2,1)S(1)}, u32[]{:S(2)}, u32[]{:S(2)}) collective-permute-start(bf16[64,10,1]{2,0,1:T(8,128)(2,1)S(1)} %get-tuple-element.13), channel_id=1, source_target_pairs={{1,0},{2,1},{3,2},{4,3},{5,4},{6,5},{7,6},{9,8},{10,9},{11,10},{12... | collective-permute-start | bytes 3848 | tf_op jit(solution)/shard_map/ppermute | solution.py:19
  41.3 4.9 %collective-permute-start.28 = (bf16[64,1,128]{2,0,1:T(8,128)(2,1)S(1)}, bf16[64,1,128]{2,0,1:T(8,128)(2,1)S(1)}, u32[]{:S(2)}, u32[]{:S(2)}) collective-permute-start(bf16[64,1,128]{2,0,1:T(8,128)(2,1)S(1)} %get-tuple-element.30), channel_id=1, source_target_pairs={{0,8},{8,16},{16,24},{1,9},{9,17},{17,25},{2,10},{10,18},{18,26},{... | collective-permute-start | bytes 49160 | tf_op jit(solution)/shard_map/ppermute | solution.py:17
  44.8 5.6 %collective-permute-start.29 = (bf16[64,1,128]{2,0,1:T(8,128)(2,1)S(1)}, bf16[64,1,128]{2,0,1:T(8,128)(2,1)S(1)}, u32[]{:S(2)}, u32[]{:S(2)}) collective-permute-start(bf16[64,1,128]{2,0,1:T(8,128)(2,1)S(1)} %get-tuple-element.31), channel_id=1, source_target_pairs={{8,0},{16,8},{24,16},{9,1},{17,9},{25,17},{10,2},{18,10},{26,18},{... | collective-permute-start | bytes 49160 | tf_op jit(solution)/shard_map/ppermute | solution.py:19
  50.5 5.8 %copy-start.3 = (bf16[6,64,64]{2,1,0:T(8,128)(2,1)S(1)}, bf16[6,64,64]{2,1,0:T(8,128)(2,1)}, u32[]{:S(2)}) copy-start(bf16[6,64,64]{2,1,0:T(8,128)(2,1)} %param.6) | copy-start | bytes 147460
  50.6 5.8 %collective-permute-start.30 = (bf16[64,10,1]{2,0,1:T(8,128)(2,1)S(1)}, bf16[64,10,1]{2,0,1:T(8,128)(2,1)S(1)}, u32[]{:S(2)}, u32[]{:S(2)}) collective-permute-start(bf16[64,10,1]{2,0,1:T(8,128)(2,1)S(1)} %get-tuple-element.10), channel_id=1, source_target_pairs={{0,1},{1,2},{2,3},{3,4},{4,5},{5,6},{6,7},{8,9},{9,10},{10,11},{11... | collective-permute-start | bytes 3848 | tf_op jit(solution)/shard_map/ppermute | solution.py:17
  54.9 4.1 %collective-permute-start.31 = (bf16[64,10,1]{2,0,1:T(8,128)(2,1)S(1)}, bf16[64,10,1]{2,0,1:T(8,128)(2,1)S(1)}, u32[]{:S(2)}, u32[]{:S(2)}) collective-permute-start(bf16[64,10,1]{2,0,1:T(8,128)(2,1)S(1)} %get-tuple-element.11), channel_id=1, source_target_pairs={{1,0},{2,1},{3,2},{4,3},{5,4},{6,5},{7,6},{9,8},{10,9},{11,10},{12... | collective-permute-start | bytes 3848 | tf_op jit(solution)/shard_map/ppermute | solution.py:19
  59.6 9.1 %collective-permute-start.32 = (bf16[64,1,128]{2,0,1:T(8,128)(2,1)S(1)}, bf16[64,1,128]{2,0,1:T(8,128)(2,1)S(1)}, u32[]{:S(2)}, u32[]{:S(2)}) collective-permute-start(bf16[64,1,128]{2,0,1:T(8,128)(2,1)S(1)} %get-tuple-element.28), channel_id=1, source_target_pairs={{0,8},{8,16},{16,24},{1,9},{9,17},{17,25},{2,10},{10,18},{18,26},{... | collective-permute-start | bytes 49160 | tf_op jit(solution)/shard_map/ppermute | solution.py:17
  61.5 7.2 %collective-permute-start.33 = (bf16[64,1,128]{2,0,1:T(8,128)(2,1)S(1)}, bf16[64,1,128]{2,0,1:T(8,128)(2,1)S(1)}, u32[]{:S(2)}, u32[]{:S(2)}) collective-permute-start(bf16[64,1,128]{2,0,1:T(8,128)(2,1)S(1)} %get-tuple-element.29), channel_id=1, source_target_pairs={{8,0},{16,8},{24,16},{9,1},{17,9},{25,17},{10,2},{18,10},{26,18},{... | collective-permute-start | bytes 49160 | tf_op jit(solution)/shard_map/ppermute | solution.py:19
  62.8 13.1 %collective-permute-start.4 = (bf16[64,1,128]{2,0,1:T(8,128)(2,1)S(1)}, bf16[64,1,128]{2,0,1:T(8,128)(2,1)S(1)}, u32[]{:S(2)}, u32[]{:S(2)}) collective-permute-start(bf16[64,1,128]{2,0,1:T(8,128)(2,1)S(1)} %get-tuple-element.42), channel_id=1, source_target_pairs={{0,8},{8,16},{16,24},{1,9},{9,17},{17,25},{2,10},{10,18},{18,26},{... | collective-permute-start | bytes 49160 | tf_op jit(solution)/shard_map/ppermute | solution.py:17
  67.4 8.5 %collective-permute-start.5 = (bf16[64,1,128]{2,0,1:T(8,128)(2,1)S(1)}, bf16[64,1,128]{2,0,1:T(8,128)(2,1)S(1)}, u32[]{:S(2)}, u32[]{:S(2)}) collective-permute-start(bf16[64,1,128]{2,0,1:T(8,128)(2,1)S(1)} %get-tuple-element.43), channel_id=1, source_target_pairs={{8,0},{16,8},{24,16},{9,1},{17,9},{25,17},{10,2},{18,10},{26,18},{... | collective-permute-start | bytes 49160 | tf_op jit(solution)/shard_map/ppermute | solution.py:19
  68.9 7.1 %collective-permute-start.34 = (bf16[64,10,1]{2,0,1:T(8,128)(2,1)S(1)}, bf16[64,10,1]{2,0,1:T(8,128)(2,1)S(1)}, u32[]{:S(2)}, u32[]{:S(2)}) collective-permute-start(bf16[64,10,1]{2,0,1:T(8,128)(2,1)S(1)} %get-tuple-element.8), channel_id=1, source_target_pairs={{0,1},{1,2},{2,3},{3,4},{4,5},{5,6},{6,7},{8,9},{9,10},{10,11},{11... | collective-permute-start | bytes 3848 | tf_op jit(solution)/shard_map/ppermute | solution.py:17
  74.6 3.5 %collective-permute-start.35 = (bf16[64,10,1]{2,0,1:T(8,128)(2,1)S(1)}, bf16[64,10,1]{2,0,1:T(8,128)(2,1)S(1)}, u32[]{:S(2)}, u32[]{:S(2)}) collective-permute-start(bf16[64,10,1]{2,0,1:T(8,128)(2,1)S(1)} %get-tuple-element.9), channel_id=1, source_target_pairs={{1,0},{2,1},{3,2},{4,3},{5,4},{6,5},{7,6},{9,8},{10,9},{11,10},{12... | collective-permute-start | bytes 3848 | tf_op jit(solution)/shard_map/ppermute | solution.py:19
  78.7 13.7 %collective-permute-start.36 = (bf16[64,1,128]{2,0,1:T(8,128)(2,1)S(1)}, bf16[64,1,128]{2,0,1:T(8,128)(2,1)S(1)}, u32[]{:S(2)}, u32[]{:S(2)}) collective-permute-start(bf16[64,1,128]{2,0,1:T(8,128)(2,1)S(1)} %get-tuple-element.26), channel_id=1, source_target_pairs={{0,8},{8,16},{16,24},{1,9},{9,17},{17,25},{2,10},{10,18},{18,26},{... | collective-permute-start | bytes 49160 | tf_op jit(solution)/shard_map/ppermute | solution.py:17
  83.2 9.1 %collective-permute-start.37 = (bf16[64,1,128]{2,0,1:T(8,128)(2,1)S(1)}, bf16[64,1,128]{2,0,1:T(8,128)(2,1)S(1)}, u32[]{:S(2)}, u32[]{:S(2)}) collective-permute-start(bf16[64,1,128]{2,0,1:T(8,128)(2,1)S(1)} %get-tuple-element.27), channel_id=1, source_target_pairs={{8,0},{16,8},{24,16},{9,1},{17,9},{25,17},{10,2},{18,10},{26,18},{... | collective-permute-start | bytes 49160 | tf_op jit(solution)/shard_map/ppermute | solution.py:19
  84.6 12.4 %collective-permute-start.6 = (bf16[64,10,1]{2,0,1:T(8,128)(2,1)S(1)}, bf16[64,10,1]{2,0,1:T(8,128)(2,1)S(1)}, u32[]{:S(2)}, u32[]{:S(2)}) collective-permute-start(bf16[64,10,1]{2,0,1:T(8,128)(2,1)S(1)} %get-tuple-element.22), channel_id=1, source_target_pairs={{0,1},{1,2},{2,3},{3,4},{4,5},{5,6},{6,7},{8,9},{9,10},{10,11},{11... | collective-permute-start | bytes 3848 | tf_op jit(solution)/shard_map/ppermute | solution.py:17
  91.0 6.0 %collective-permute-start.7 = (bf16[64,10,1]{2,0,1:T(8,128)(2,1)S(1)}, bf16[64,10,1]{2,0,1:T(8,128)(2,1)S(1)}, u32[]{:S(2)}, u32[]{:S(2)}) collective-permute-start(bf16[64,10,1]{2,0,1:T(8,128)(2,1)S(1)} %get-tuple-element.23), channel_id=1, source_target_pairs={{1,0},{2,1},{3,2},{4,3},{5,4},{6,5},{7,6},{9,8},{10,9},{11,10},{12... | collective-permute-start | bytes 3848 | tf_op jit(solution)/shard_map/ppermute | solution.py:19
  92.5 4.5 %collective-permute-start.38 = (bf16[64,10,1]{2,0,1:T(8,128)(2,1)S(1)}, bf16[64,10,1]{2,0,1:T(8,128)(2,1)S(1)}, u32[]{:S(2)}, u32[]{:S(2)}) collective-permute-start(bf16[64,10,1]{2,0,1:T(8,128)(2,1)S(1)} %get-tuple-element.6), channel_id=1, source_target_pairs={{0,1},{1,2},{2,3},{3,4},{4,5},{5,6},{6,7},{8,9},{9,10},{10,11},{11... | collective-permute-start | bytes 3848 | tf_op jit(solution)/shard_map/ppermute | solution.py:17
  95.5 5.8 %collective-permute-start.39 = (bf16[64,10,1]{2,0,1:T(8,128)(2,1)S(1)}, bf16[64,10,1]{2,0,1:T(8,128)(2,1)S(1)}, u32[]{:S(2)}, u32[]{:S(2)}) collective-permute-start(bf16[64,10,1]{2,0,1:T(8,128)(2,1)S(1)} %get-tuple-element.7), channel_id=1, source_target_pairs={{1,0},{2,1},{3,2},{4,3},{5,4},{6,5},{7,6},{9,8},{10,9},{11,10},{12... | collective-permute-start | bytes 3848 | tf_op jit(solution)/shard_map/ppermute | solution.py:19
  102.1 11.8 %collective-permute-start.40 = (bf16[64,1,128]{2,0,1:T(8,128)(2,1)S(1)}, bf16[64,1,128]{2,0,1:T(8,128)(2,1)S(1)}, u32[]{:S(2)}, u32[]{:S(2)}) collective-permute-start(bf16[64,1,128]{2,0,1:T(8,128)(2,1)S(1)} %get-tuple-element.24), channel_id=1, source_target_pairs={{0,8},{8,16},{16,24},{1,9},{9,17},{17,25},{2,10},{10,18},{18,26},{... | collective-permute-start | bytes 49160 | tf_op jit(solution)/shard_map/ppermute | solution.py:17
  106.4 7.5 %collective-permute-start.41 = (bf16[64,1,128]{2,0,1:T(8,128)(2,1)S(1)}, bf16[64,1,128]{2,0,1:T(8,128)(2,1)S(1)}, u32[]{:S(2)}, u32[]{:S(2)}) collective-permute-start(bf16[64,1,128]{2,0,1:T(8,128)(2,1)S(1)} %get-tuple-element.25), channel_id=1, source_target_pairs={{8,0},{16,8},{24,16},{9,1},{17,9},{25,17},{10,2},{18,10},{26,18},{... | collective-permute-start | bytes 49160 | tf_op jit(solution)/shard_map/ppermute | solution.py:19
  108.0 12.7 %collective-permute-start.8 = (bf16[64,1,128]{2,0,1:T(8,128)(2,1)S(1)}, bf16[64,1,128]{2,0,1:T(8,128)(2,1)S(1)}, u32[]{:S(2)}, u32[]{:S(2)}) collective-permute-start(bf16[64,1,128]{2,0,1:T(8,128)(2,1)S(1)} %get-tuple-element.40), channel_id=1, source_target_pairs={{0,8},{8,16},{16,24},{1,9},{9,17},{17,25},{2,10},{10,18},{18,26},{... | collective-permute-start | bytes 49160 | tf_op jit(solution)/shard_map/ppermute | solution.py:17
  112.6 8.2 %collective-permute-start.9 = (bf16[64,1,128]{2,0,1:T(8,128)(2,1)S(1)}, bf16[64,1,128]{2,0,1:T(8,128)(2,1)S(1)}, u32[]{:S(2)}, u32[]{:S(2)}) collective-permute-start(bf16[64,1,128]{2,0,1:T(8,128)(2,1)S(1)} %get-tuple-element.41), channel_id=1, source_target_pairs={{8,0},{16,8},{24,16},{9,1},{17,9},{25,17},{10,2},{18,10},{26,18},{... | collective-permute-start | bytes 49160 | tf_op jit(solution)/shard_map/ppermute | solution.py:19
  114.1 11.5 %collective-permute-start.42 = (bf16[64,10,1]{2,0,1:T(8,128)(2,1)S(1)}, bf16[64,10,1]{2,0,1:T(8,128)(2,1)S(1)}, u32[]{:S(2)}, u32[]{:S(2)}) collective-permute-start(bf16[64,10,1]{2,0,1:T(8,128)(2,1)S(1)} %get-tuple-element.4), channel_id=1, source_target_pairs={{0,1},{1,2},{2,3},{3,4},{4,5},{5,6},{6,7},{8,9},{9,10},{10,11},{11... | collective-permute-start | bytes 3848 | tf_op jit(solution)/shard_map/ppermute | solution.py:17
  119.4 6.2 %collective-permute-start.43 = (bf16[64,10,1]{2,0,1:T(8,128)(2,1)S(1)}, bf16[64,10,1]{2,0,1:T(8,128)(2,1)S(1)}, u32[]{:S(2)}, u32[]{:S(2)}) collective-permute-start(bf16[64,10,1]{2,0,1:T(8,128)(2,1)S(1)} %get-tuple-element.5), channel_id=1, source_target_pairs={{1,0},{2,1},{3,2},{4,3},{5,4},{6,5},{7,6},{9,8},{10,9},{11,10},{12... | collective-permute-start | bytes 3848 | tf_op jit(solution)/shard_map/ppermute | solution.py:19
  120.9 4.7 %collective-permute-start.10 = (bf16[64,10,1]{2,0,1:T(8,128)(2,1)S(1)}, bf16[64,10,1]{2,0,1:T(8,128)(2,1)S(1)}, u32[]{:S(2)}, u32[]{:S(2)}) collective-permute-start(bf16[64,10,1]{2,0,1:T(8,128)(2,1)S(1)} %get-tuple-element.20), channel_id=1, source_target_pairs={{0,1},{1,2},{2,3},{3,4},{4,5},{5,6},{6,7},{8,9},{9,10},{10,11},{11... | collective-permute-start | bytes 3848 | tf_op jit(solution)/shard_map/ppermute | solution.py:17
  124.1 5.6 %collective-permute-start.11 = (bf16[64,10,1]{2,0,1:T(8,128)(2,1)S(1)}, bf16[64,10,1]{2,0,1:T(8,128)(2,1)S(1)}, u32[]{:S(2)}, u32[]{:S(2)}) collective-permute-start(bf16[64,10,1]{2,0,1:T(8,128)(2,1)S(1)} %get-tuple-element.21), channel_id=1, source_target_pairs={{1,0},{2,1},{3,2},{4,3},{5,4},{6,5},{7,6},{9,8},{10,9},{11,10},{12... | collective-permute-start | bytes 3848 | tf_op jit(solution)/shard_map/ppermute | solution.py:19
  130.5 5.8 %collective-permute-start.12 = (bf16[64,1,128]{2,0,1:T(8,128)(2,1)S(1)}, bf16[64,1,128]{2,0,1:T(8,128)(2,1)S(1)}, u32[]{:S(2)}, u32[]{:S(2)}) collective-permute-start(bf16[64,1,128]{2,0,1:T(8,128)(2,1)S(1)} %get-tuple-element.38), channel_id=1, source_target_pairs={{0,8},{8,16},{16,24},{1,9},{9,17},{17,25},{2,10},{10,18},{18,26},{... | collective-permute-start | bytes 49160 | tf_op jit(solution)/shard_map/ppermute | solution.py:17
  134.8 5.6 %collective-permute-start.13 = (bf16[64,1,128]{2,0,1:T(8,128)(2,1)S(1)}, bf16[64,1,128]{2,0,1:T(8,128)(2,1)S(1)}, u32[]{:S(2)}, u32[]{:S(2)}) collective-permute-start(bf16[64,1,128]{2,0,1:T(8,128)(2,1)S(1)} %get-tuple-element.39), channel_id=1, source_target_pairs={{8,0},{16,8},{24,16},{9,1},{17,9},{25,17},{10,2},{18,10},{26,18},{... | collective-permute-start | bytes 49160 | tf_op jit(solution)/shard_map/ppermute | solution.py:19
  140.6 6.8 %collective-permute-start.14 = (bf16[64,10,1]{2,0,1:T(8,128)(2,1)S(1)}, bf16[64,10,1]{2,0,1:T(8,128)(2,1)S(1)}, u32[]{:S(2)}, u32[]{:S(2)}) collective-permute-start(bf16[64,10,1]{2,0,1:T(8,128)(2,1)S(1)} %get-tuple-element.18), channel_id=1, source_target_pairs={{0,1},{1,2},{2,3},{3,4},{4,5},{5,6},{6,7},{8,9},{9,10},{10,11},{11... | collective-permute-start | bytes 3848 | tf_op jit(solution)/shard_map/ppermute | solution.py:17
  145.9 4.1 %collective-permute-start.15 = (bf16[64,10,1]{2,0,1:T(8,128)(2,1)S(1)}, bf16[64,10,1]{2,0,1:T(8,128)(2,1)S(1)}, u32[]{:S(2)}, u32[]{:S(2)}) collective-permute-start(bf16[64,10,1]{2,0,1:T(8,128)(2,1)S(1)} %get-tuple-element.19), channel_id=1, source_target_pairs={{1,0},{2,1},{3,2},{4,3},{5,4},{6,5},{7,6},{9,8},{10,9},{11,10},{12... | collective-permute-start | bytes 3848 | tf_op jit(solution)/shard_map/ppermute | solution.py:19
  150.6 3.4 %collective-permute-start.16 = (bf16[64,1,128]{2,0,1:T(8,128)(2,1)S(1)}, bf16[64,1,128]{2,0,1:T(8,128)(2,1)S(1)}, u32[]{:S(2)}, u32[]{:S(2)}) collective-permute-start(bf16[64,1,128]{2,0,1:T(8,128)(2,1)S(1)} %get-tuple-element.36), channel_id=1, source_target_pairs={{0,8},{8,16},{16,24},{1,9},{9,17},{17,25},{2,10},{10,18},{18,26},{... | collective-permute-start | bytes 49160 | tf_op jit(solution)/shard_map/ppermute | solution.py:17
  152.5 5.6 %collective-permute-start.17 = (bf16[64,1,128]{2,0,1:T(8,128)(2,1)S(1)}, bf16[64,1,128]{2,0,1:T(8,128)(2,1)S(1)}, u32[]{:S(2)}, u32[]{:S(2)}) collective-permute-start(bf16[64,1,128]{2,0,1:T(8,128)(2,1)S(1)} %get-tuple-element.37), channel_id=1, source_target_pairs={{8,0},{16,8},{24,16},{9,1},{17,9},{25,17},{10,2},{18,10},{26,18},{... | collective-permute-start | bytes 49160 | tf_op jit(solution)/shard_map/ppermute | solution.py:19
  158.3 6.6 %collective-permute-start.18 = (bf16[64,10,1]{2,0,1:T(8,128)(2,1)S(1)}, bf16[64,10,1]{2,0,1:T(8,128)(2,1)S(1)}, u32[]{:S(2)}, u32[]{:S(2)}) collective-permute-start(bf16[64,10,1]{2,0,1:T(8,128)(2,1)S(1)} %get-tuple-element.16), channel_id=1, source_target_pairs={{0,1},{1,2},{2,3},{3,4},{4,5},{5,6},{6,7},{8,9},{9,10},{10,11},{11... | collective-permute-start | bytes 3848 | tf_op jit(solution)/shard_map/ppermute | solution.py:17
  163.6 4.1 %collective-permute-start.19 = (bf16[64,10,1]{2,0,1:T(8,128)(2,1)S(1)}, bf16[64,10,1]{2,0,1:T(8,128)(2,1)S(1)}, u32[]{:S(2)}, u32[]{:S(2)}) collective-permute-start(bf16[64,10,1]{2,0,1:T(8,128)(2,1)S(1)} %get-tuple-element.17), channel_id=1, source_target_pairs={{1,0},{2,1},{3,2},{4,3},{5,4},{6,5},{7,6},{9,8},{10,9},{11,10},{12... | collective-permute-start | bytes 3848 | tf_op jit(solution)/shard_map/ppermute | solution.py:19
  168.2 4.3 %collective-permute-start.20 = (bf16[64,1,128]{2,0,1:T(8,128)(2,1)S(1)}, bf16[64,1,128]{2,0,1:T(8,128)(2,1)S(1)}, u32[]{:S(2)}, u32[]{:S(2)}) collective-permute-start(bf16[64,1,128]{2,0,1:T(8,128)(2,1)S(1)} %get-tuple-element.34), channel_id=1, source_target_pairs={{0,8},{8,16},{16,24},{1,9},{9,17},{17,25},{2,10},{10,18},{18,26},{... | collective-permute-start | bytes 49160 | tf_op jit(solution)/shard_map/ppermute | solution.py:17
  170.1 5.6 %collective-permute-start.21 = (bf16[64,1,128]{2,0,1:T(8,128)(2,1)S(1)}, bf16[64,1,128]{2,0,1:T(8,128)(2,1)S(1)}, u32[]{:S(2)}, u32[]{:S(2)}) collective-permute-start(bf16[64,1,128]{2,0,1:T(8,128)(2,1)S(1)} %get-tuple-element.35), channel_id=1, source_target_pairs={{8,0},{16,8},{24,16},{9,1},{17,9},{25,17},{10,2},{18,10},{26,18},{... | collective-permute-start | bytes 49160 | tf_op jit(solution)/shard_map/ppermute | solution.py:19
  171.8 0.7 copy-start.2
  175.9 126.5 %collective-permute-start.22 = (bf16[64,10,1]{2,0,1:T(8,128)(2,1)S(1)}, bf16[64,10,1]{2,0,1:T(8,128)(2,1)S(1)}, u32[]{:S(2)}, u32[]{:S(2)}) collective-permute-start(bf16[64,10,1]{2,0,1:T(8,128)(2,1)S(1)} %get-tuple-element.14), channel_id=1, source_target_pairs={{0,1},{1,2},{2,3},{3,4},{4,5},{5,6},{6,7},{8,9},{9,10},{10,11},{11... | collective-permute-start | bytes 3848 | tf_op jit(solution)/shard_map/ppermute | solution.py:17
  181.2 121.2 %collective-permute-start.23 = (bf16[64,10,1]{2,0,1:T(8,128)(2,1)S(1)}, bf16[64,10,1]{2,0,1:T(8,128)(2,1)S(1)}, u32[]{:S(2)}, u32[]{:S(2)}) collective-permute-start(bf16[64,10,1]{2,0,1:T(8,128)(2,1)S(1)} %get-tuple-element.15), channel_id=1, source_target_pairs={{1,0},{2,1},{3,2},{4,3},{5,4},{6,5},{7,6},{9,8},{10,9},{11,10},{12... | collective-permute-start | bytes 3848 | tf_op jit(solution)/shard_map/ppermute | solution.py:19
Sparse Core Ops, SparseCore 0:
  172.7 128.0 all-reduce.1
where the time goes:
time: 312 us; the launch traced here: 311 us
  waiting for transfers between devices  164 us (53%)
  starting transfers between devices  117 us (38%)
  between operations  15.1 us (5%)
  other arithmetic  5.95 us (2%)
  local copies, waits for them, and re-layouts  5.42 us (2%)
    psum x1, waiting for transfers between devices, body(): summed = lax.psum(partial_grads, ('row', 'col'))  118 us
    ppermute x22, starting transfers between devices, with_halo(): lax.ppermute(tail, axis, [(i, (i + 1) % count) for i in range(ends)])  88.3 us
    ppermute x22, waiting for transfers between devices, with_halo(): lax.ppermute(head, axis, [((i + 1) % count, i) for i in range(ends)])  46 us
    ppermute x22, starting transfers between devices, with_halo(): lax.ppermute(head, axis, [((i + 1) % count, i) for i in range(ends)])  28.4 us
  transfers between devices with their start and end apart: 45, of which 15 were waited for; matrix products, arithmetic and copies ran while one was open for 2% of the time, Pallas kernels for 0%

commit v1 on v0

v1 whole, which is shorter than its diff:
```python
import functools
import math

import jax
import jax.numpy as jnp
from jax import lax
from jax.experimental import pallas as pl
from jax.experimental.pallas import tpu as pltpu
from jax.sharding import PartitionSpec as P

RIM = 8
F32 = jnp.float32
BF16 = jnp.bfloat16
NT = (((1,), (1,)), ((), ()))


def iota(shape, dim):
    return lax.broadcasted_iota(jnp.int32, shape, dim)


def swap_halves(x):
    return pltpu.roll(x, x.shape[-1] // 2, x.ndim - 1)


def even_place(axis):
    return lax.axis_index(axis) % 2 == 0


def even_parity():
    place = lax.axis_index("row") * lax.axis_size("col") + lax.axis_index("col")
    for shift in (16, 8, 4, 2, 1):
        place = place ^ (place >> shift)
    return place % 2 == 0


def in_order(axis, first, second):
    even, place = even_place(axis), lax.axis_index(axis)
    before, after = jnp.where(even, second, first), jnp.where(even, first, second)
    return jnp.where(place == 0, 0.0, before), jnp.where(place == lax.axis_size(axis) - 1, 0.0, after)


def mask_kernel(mask_ref, out_ref):
    mask = mask_ref[...].astype(F32)
    out_ref[...] = jnp.concatenate([mask, jnp.zeros_like(mask)], axis=0).astype(BF16)


def pack_kernel(halo, cot_ref, mask_ref, body_ref, first_ref, second_ref, wide_ref):
    channels, rows, cols = cot_ref.shape
    half, lanes = cols // 2, 2 * channels
    wide_ref[...] = cot_ref[...].astype(F32).reshape(channels * rows, cols)
    fold = (iota((half, cols), 1) % half == iota((half, cols), 0)).astype(BF16)
    left = iota((channels, cols), 1) < half
    stacked = []
    for r in range(rows):
        row = wide_ref[pl.ds(r, channels, stride=rows), :]
        stacked += [jnp.where(left, row, 0.0), jnp.where(left, 0.0, row)]
    stacked = jnp.concatenate(stacked, axis=0).astype(BF16)
    body = lax.dot_general(fold, stacked, NT, preferred_element_type=F32)
    for r in range(rows):
        body_ref[r * half : (r + 1) * half, :] = body[:, r * lanes : (r + 1) * lanes].astype(BF16)
    south, count = even_place("row"), halo * half
    for out_ref, lower in ((first_ref, south), (second_ref, jnp.logical_not(south))):
        start = pl.multiple_of(jnp.where(lower, rows * half - count, 0), half)
        out_ref[:count, :] = body_ref[pl.ds(start, count), :]
        out_ref[count:, :] = mask_ref[...]


def early_kernel(feature_ref, weight_ref, feature_out_ref, rim_out_ref, weight_out_ref, wide_ref):
    channels, rows, cols = feature_ref.shape
    lanes = 2 * channels
    wide_ref[...] = feature_ref[...].astype(F32).reshape(channels * rows, cols)
    left = iota((channels, cols), 1) < cols // 2
    for q in range(rows // 2):
        even = wide_ref[pl.ds(2 * q, channels, stride=rows), :]
        odd = wide_ref[pl.ds(2 * q + 1, channels, stride=rows), :]
        at = slice(q * cols, (q + 1) * cols)
        feature_out_ref[:channels, at] = jnp.where(left, even, swap_halves(odd)).astype(BF16)
        feature_out_ref[channels:, at] = jnp.where(left, swap_halves(even), odd).astype(BF16)
    half, shape = cols // 2, (rows * cols // 2, rows * RIM)
    pixel, target = iota(shape, 0), iota(shape, 1)
    here = target // RIM * half + target % RIM
    sides = [
        jnp.dot(feature_out_ref[...], (pixel == here + skip).astype(BF16), preferred_element_type=F32)
        for skip in (0, half - RIM)
    ]
    rim_out_ref[:channels, :] = sides[0][:channels].astype(BF16)
    rim_out_ref[channels:, :] = sides[1][channels:].astype(BF16)
    for k in range(weight_ref.shape[0]):
        weight = weight_ref[k].astype(F32) * (-1.0) ** k
        blank = jnp.zeros_like(weight)
        at = slice(k * lanes, (k + 1) * lanes)
        weight_out_ref[:channels, at] = jnp.concatenate([weight, blank], axis=1).astype(BF16)
        weight_out_ref[channels:, at] = jnp.concatenate([blank, weight], axis=1).astype(BF16)


def row_pieces(halo, half, body_ref, first_ref, second_ref, begin, size):
    rows = body_ref.shape[0] // half

    def piece(ref, r):
        return ref[r * half + begin : r * half + begin + size, :].astype(F32)

    received = [in_order("row", piece(first_ref, r), piece(second_ref, r)) for r in range(halo)]
    return [north for north, _ in received] + [piece(body_ref, r) for r in range(rows)] + [south for _, south in received]


def all_masks(halo, half, mask_ref, first_ref, second_ref):
    rows, begin = mask_ref.shape[0] // 2, halo * half
    north, south = in_order("row", first_ref[begin:, :].astype(F32), second_ref[begin:, :].astype(F32))
    return jnp.concatenate([north[:rows], mask_ref[...].astype(F32)[:rows], south[:rows]], axis=0)


def strips_kernel(halo, body_ref, mask_ref, second_ref, first_ref, to_first_ref, to_second_ref):
    rows = mask_ref.shape[0] // 2
    half = body_ref.shape[0] // rows
    total = rows + 2 * halo
    marks = 3 * rows
    masks = all_masks(halo, half, mask_ref, first_ref, second_ref)
    leading = row_pieces(halo, half, body_ref, first_ref, second_ref, 0, 2 * RIM)
    trailing = row_pieces(halo, half, body_ref, first_ref, second_ref, half - 2 * RIM, 2 * RIM)
    low = iota((RIM, body_ref.shape[1]), 1) < body_ref.shape[1] // 2
    west, east = [], []
    for n in range(total // 2):
        west.append(jnp.where(low, leading[n][:RIM], swap_halves(leading[n + total // 2][:RIM])))
        east.append(jnp.where(low, swap_halves(trailing[n][RIM:]), trailing[n + total // 2][RIM:]))
    spare = to_first_ref.shape[0] - total // 2 * RIM - marks
    blank = [jnp.zeros((spare, body_ref.shape[1]), F32)] if spare else []
    west, east = (jnp.concatenate([masks, *x] + blank, axis=0) for x in (west, east))
    even = even_place("col")
    to_first_ref[...] = jnp.where(even, east, west).astype(BF16)
    to_second_ref[...] = jnp.where(even, west, east).astype(BF16)


def compact_scales(mask):
    rows, cols = mask.shape
    column = mask + pltpu.roll(mask, 1, 0) + pltpu.roll(mask, rows - 1, 0)
    degree = mask * (column + pltpu.roll(column, 1, 1) + pltpu.roll(column, cols - 1, 1) - mask)
    return jnp.transpose(mask * jnp.sqrt(2.0 / jnp.maximum(degree, 1.0)), (1, 0))


def spread_scales(left, right, scale_ref):
    (tall, marks), lanes = left.shape, scale_ref.shape[1]
    total = scale_ref.shape[0] // tall
    spare = jnp.zeros((tall, lanes // 2 - marks), F32)
    both = jnp.concatenate([left, spare, right, spare], axis=1)
    lane = iota((tall, lanes), 1)
    start = jnp.where(lane < lanes // 2, 0, lanes // 2) + (marks - total) // 2
    for q in range(total):
        picked = jnp.take_along_axis(both, start + q, axis=1, mode="promise_in_bounds")
        scale_ref[q * tall : (q + 1) * tall, :] = picked


def next_term(k, tall, scale_ref, newer_ref, older_ref, visit):
    total = scale_ref.shape[0] // tall

    def at(q):
        return slice(q * tall, (q + 1) * tall)

    def weighted(q):
        return scale_ref[at(q), :] * newer_ref[at(q), :]

    above, here = weighted(k - 1), weighted(k)
    for q in range(k, total - k):
        below = weighted(q + 1)
        column = above + here + below
        nearby = column + pltpu.roll(column, 1, 0) + pltpu.roll(column, tall - 1, 0) - here
        fresh = scale_ref[at(q), :] * nearby
        fresh = 0.5 * fresh if k == 1 else fresh - older_ref[at(q), :]
        older_ref[at(q), :] = fresh
        visit(q, fresh)
        above, here = here, below


def order_products(b, lanes, feature, terms):
    channels = lanes // 2
    product = jnp.dot(feature, terms[:, 2 * b * lanes : 2 * (b + 1) * lanes], preferred_element_type=F32)
    near, far = product[:channels], product[channels:]
    even = near[:, :lanes] + swap_halves(far[:, :lanes])
    odd = swap_halves(near[:, lanes:]) + far[:, lanes:]
    return jnp.where(iota((channels, lanes), 1) < channels, even, -odd)


def interior_kernel(
    orders, body_ref, mask_ref, second_ref, first_ref, feature_ref, terms_ref, sums_ref, own_ref, even_ref, odd_ref, scale_ref
):
    rows, cols = mask_ref.shape[0] // 2, mask_ref.shape[1]
    half, halo, lanes = cols // 2, orders - 1, body_ref.shape[1]
    tall = half + 2 * RIM
    across = compact_scales(all_masks(halo, half, mask_ref, first_ref, second_ref))
    rim = jnp.zeros((RIM, across.shape[1]), F32)
    left = jnp.concatenate([rim, across[: half + RIM]], axis=0)
    right = jnp.concatenate([across[half - RIM :], rim], axis=0)
    spread_scales(left, right, scale_ref)
    low = iota((RIM, lanes), 1) < lanes // 2
    for q, middle in enumerate(row_pieces(halo, half, body_ref, first_ref, second_ref, 0, half)):
        at = q * tall
        odd_ref[at : at + RIM, :] = jnp.where(low, 0.0, swap_halves(middle[half - RIM :]))
        odd_ref[at + RIM : at + RIM + half, :] = middle
        odd_ref[at + RIM + half : at + tall, :] = jnp.where(low, swap_halves(middle[:RIM]), 0.0)
        at = q * 3 * RIM
        tail = half - 2 * RIM
        own_ref[at : at + RIM, :] = jnp.where(low, 0.0, middle[tail : tail + RIM])
        own_ref[at + RIM : at + 2 * RIM, :] = jnp.where(low, middle[:RIM], middle[tail + RIM :])
        own_ref[at + 2 * RIM : at + 3 * RIM, :] = jnp.where(low, middle[RIM : 2 * RIM], 0.0)
    terms_ref[:, :lanes] = body_ref[...]
    newer, older = odd_ref, even_ref
    for k in range(1, orders):
        def keep(q, fresh):
            r = q - halo
            if 0 <= r < rows:
                columns = slice(k * lanes, (k + 1) * lanes)
                first = jnp.where(low, 0.0, fresh[RIM : 2 * RIM])
                last = jnp.where(low, fresh[half : half + RIM], 0.0)
                kept = jnp.concatenate([first, fresh[2 * RIM : half], last], axis=0)
                terms_ref[r * half : (r + 1) * half, columns] = kept.astype(BF16)

        next_term(k, tall, scale_ref, newer, older, keep)
        newer, older = older, newer
        if k % 2:
            sums_ref[k // 2] = order_products(k // 2, lanes, feature_ref[...], terms_ref)


def edge_kernel(
    orders, own_ref, mask_ref, north_second_ref, north_first_ref, second_ref, first_ref, rim_ref, sums_ref,
    terms_ref, keep_ref, give_ref, even_ref, odd_ref, scale_ref, wide_ref,
):
    rows, cols = mask_ref.shape[0] // 2, mask_ref.shape[1]
    half, halo, lanes = cols // 2, orders - 1, own_ref.shape[1]
    channels, total, tall = lanes // 2, rows + 2 * halo, 3 * RIM
    west, east = in_order("col", first_ref[...].astype(F32), second_ref[...].astype(F32))
    lower = iota((3 * rows, cols), 1) < half
    centre = all_masks(halo, half, mask_ref, north_first_ref, north_second_ref)
    beside = jnp.where(lower, east[: 3 * rows], west[: 3 * rows])
    across = compact_scales(jnp.concatenate([centre, beside], axis=1))
    left = jnp.concatenate([across[2 * cols - RIM :], across[: 2 * RIM]], axis=0)
    spread_scales(left, across[cols - 2 * RIM : cols + RIM], scale_ref)

    low = iota((RIM, lanes), 1) < channels
    for q in range(total):
        n, upper_row = q % (total // 2), q >= total // 2
        strip = slice(3 * rows + n * RIM, 3 * rows + (n + 1) * RIM)
        before = swap_halves(west[strip]) if upper_row else west[strip]
        after = east[strip] if upper_row else swap_halves(east[strip])
        at = q * tall
        odd_ref[at : at + RIM, :] = jnp.where(low, before, own_ref[at : at + RIM, :])
        odd_ref[at + RIM : at + 2 * RIM, :] = own_ref[at + RIM : at + 2 * RIM, :]
        odd_ref[at + 2 * RIM : at + tall, :] = jnp.where(low, own_ref[at + 2 * RIM : at + tall, :], after)

    wide_ref[:, :lanes] = jnp.zeros((rows * RIM, lanes), F32)
    newer, older = odd_ref, even_ref
    for k in range(1, orders):
        def keep(q, fresh):
            r = q - halo
            if 0 <= r < rows:
                wide_ref[r * RIM : (r + 1) * RIM, k * lanes : (k + 1) * lanes] = fresh[RIM : 2 * RIM]

        next_term(k, tall, scale_ref, newer, older, keep)
        newer, older = older, newer
    terms_ref[...] = wide_ref[...].astype(BF16)
    upper = even_parity()
    for b in range(orders // 2):
        block = sums_ref[b] + order_products(b, lanes, rim_ref[...], terms_ref)
        a, b_half = block[: channels // 2], block[channels // 2 :]
        keep_ref[b] = jnp.where(upper, a, b_half)
        give_ref[b] = jnp.where(upper, b_half, a)


def mix_kernel(weight_ref, inner_ref, rim_ref, grad_ref, wide_ref, terms_ref):
    channels, rows, cols = grad_ref.shape
    half, lanes = cols // 2, 2 * channels
    terms_ref[...] = inner_ref[...]
    lane, sublane = iota((2 * RIM, lanes), 1), iota((2 * RIM, lanes), 0)
    first_columns = jnp.logical_and(lane < channels, sublane < RIM)
    last_columns = jnp.logical_and(lane >= channels, sublane >= RIM)
    for k in range(1, rim_ref.shape[1] // lanes):
        columns = slice(k * lanes, (k + 1) * lanes)
        rims = rim_ref[:, columns].astype(F32)
        for r in range(rows):
            twice = jnp.concatenate([rims[r * RIM : (r + 1) * RIM]] * 2, axis=0)
            for begin, chosen in ((r * half, first_columns), ((r + 1) * half - 2 * RIM, last_columns)):
                at = (slice(begin, begin + 2 * RIM), columns)
                terms_ref[at] = jnp.where(chosen, twice, inner_ref[at].astype(F32)).astype(BF16)
    low = iota((channels, cols), 1) < half
    mixed = lax.dot_general(weight_ref[...], terms_ref[...], NT, preferred_element_type=F32)
    for q in range(rows // 2):
        upper, lower = mixed[:channels, q * cols : (q + 1) * cols], mixed[channels:, q * cols : (q + 1) * cols]
        wide_ref[pl.ds(2 * q, channels, stride=rows), :] = jnp.where(low, upper, swap_halves(lower))
        wide_ref[pl.ds(2 * q + 1, channels, stride=rows), :] = jnp.where(low, swap_halves(upper), lower)
    grad_ref[...] = wide_ref[...].reshape(channels, rows, cols).astype(BF16)


def finish_kernel(divisor, mine_ref, other_ref, out_ref):
    orders, channels, _ = out_ref.shape
    upper = even_parity()
    for b in range(orders // 2):
        mine, other = mine_ref[b] / divisor, other_ref[b] / divisor
        block = jnp.concatenate([jnp.where(upper, mine, other), jnp.where(upper, other, mine)], axis=0)
        out_ref[2 * b] = block[:, :channels]
        out_ref[2 * b + 1] = block[:, channels:]


def call(kernel, outs, scratch, cost, *args):
    return pl.pallas_call(
        kernel,
        out_shape=outs,
        in_specs=[pl.BlockSpec(memory_space=pltpu.VMEM)] * len(args),
        out_specs=jax.tree.map(lambda _: pl.BlockSpec(memory_space=pltpu.VMEM), outs),
        scratch_shapes=scratch,
        compiler_params=pltpu.CompilerParams(vmem_limit_bytes=32 * 1024 * 1024),
        cost_estimate=pl.CostEstimate(flops=cost, bytes_accessed=1 << 20, transcendentals=0),
    )(*args)


def swap(x, partner):
    places = range(lax.axis_size("row") * lax.axis_size("col"))
    return lax.ppermute(x, ("row", "col"), [(i, partner(i)) for i in places])


def exchange_cols(first, second):
    across = lax.axis_size("col")

    def after_odd(i):
        row, col = i // across, i % across
        return row * across + (((col - 1) % across ^ 1) + 1) % across

    second = swap(second, after_odd)
    return swap(first, lambda i: i ^ 1), second


def exchange_rows(first, second):
    across, down = lax.axis_size("col"), lax.axis_size("row")

    def after_odd(i):
        row, col = i // across, i % across
        return i ^ 1 if row in (0, down - 1) else (((row - 1) ^ 1) + 1) * across + col

    return swap(first, lambda i: (i // across ^ 1) * across + i % across), swap(second, after_odd)


def sum_everywhere(keep, give, work, *args):
    across, down = lax.axis_size("col"), lax.axis_size("row")
    beside = list(range(1, across.bit_length() - 1))
    below = list(range(across.bit_length() - 1, (across * down).bit_length() - 1))
    turns = [(beside[n : n + 1], below[n : n + 1]) for n in range(max(len(beside), len(below)))]
    even = [bit for a, b in turns for bit in a + b]
    odd = [bit for a, b in turns for bit in b + a]
    mine = keep + swap(give, lambda i: i ^ 1)
    for n, bits in enumerate(zip(even, odd)):
        received = swap(mine, lambda i: i ^ (1 << bits[i.bit_count() % 2]) ^ 1)
        if n == 0:
            _, *args = lax.optimization_barrier((mine, *args))
            received, done = lax.optimization_barrier((received, work(*args)))
        mine = mine + received
    return mine, swap(mine, lambda i: i ^ 1), done


def body(feature, cotangent, order_weight, pixel_mask):
    orders, channels, _ = order_weight.shape
    _, rows, cols = feature.shape
    half, lanes, halo = cols // 2, 2 * channels, orders - 1
    tall, total = half + 2 * RIM, rows + 2 * halo
    shape = jax.ShapeDtypeStruct
    wide = pltpu.VMEM((channels * rows, cols), F32)
    marks = shape((2 * rows, cols), BF16)

    mask16 = call(mask_kernel, marks, [], 1 << 31, pixel_mask)
    sent = shape((halo * half + 2 * rows, lanes), BF16)
    cot_body, first, second = call(
        functools.partial(pack_kernel, halo), [shape((rows * half, lanes), BF16), sent, sent], [wide], 1 << 20,
        cotangent, mask16,
    )
    first, second = exchange_rows(first, second)
    features, rims, weights = call(
        early_kernel,
        [shape((lanes, rows * half), BF16), shape((lanes, rows * RIM), BF16), shape((lanes, orders * lanes), BF16)],
        [wide], 1 << 20, feature, order_weight,
    )
    sent = shape((-(-(3 * rows + total // 2 * RIM) // 16) * 16, lanes), BF16)
    west_first, west_second = call(
        functools.partial(strips_kernel, halo), [sent, sent], [], 1 << 16, cot_body, mask16, second, first
    )
    west_first, west_second = exchange_cols(west_first, west_second)
    buffer = pltpu.VMEM((total * tall, lanes), F32)
    small = pltpu.VMEM((total * 3 * RIM, lanes), F32)
    terms = shape((rows * half, orders * lanes), BF16)
    rim_terms = shape((rows * RIM, orders * lanes), BF16)
    part = shape((orders // 2, channels // 2, lanes), F32)
    inner, sums, own = call(
        functools.partial(interior_kernel, orders),
        [terms, shape((orders // 2, channels, lanes), F32), shape((total * 3 * RIM, lanes), F32)],
        [buffer, buffer, buffer], 1 << 28, cot_body, mask16, second, first, features,
    )
    outer, keep, give = call(
        functools.partial(edge_kernel, orders), [rim_terms, part, part],
        [small, small, small, pltpu.VMEM(rim_terms.shape, F32)], 1 << 26,
        own, mask16, second, first, west_second, west_first, rims, sums,
    )
    mix = functools.partial(
        call, mix_kernel, shape((channels, rows, cols), BF16), [wide, pltpu.VMEM(terms.shape, BF16)], 1 << 20
    )
    mine, other, grad_feature = sum_everywhere(keep, give, mix, weights, inner, outer)
    pixel_count = rows * cols * lax.axis_size("row") * lax.axis_size("col")
    grad_order = call(
        functools.partial(finish_kernel, math.sqrt(pixel_count)),
        shape((orders, channels, channels), F32), [], 1 << 16, mine, other,
    )
    return (grad_feature, grad_order)


def solution(mesh):
    placed = (P(None, "row", "col"), P(None, "row", "col"), P(), P("row", "col"))
    return jax.shard_map(
        body, mesh=mesh, in_specs=placed, out_specs=(P(None, "row", "col"), P()), check_vma=False
    )
```

time: 312 us -> 33.2 us (0.11)
  waiting for transfers between devices: 164 us -> 13.3 us
  starting transfers between devices: 117 us -> 12.4 us
  between operations: 15.1 us -> 0.72 us
  other arithmetic: 5.95 us -> 0.04 us
  Pallas kernels: 0 us -> 5.62 us
  local copies, waits for them, and re-layouts: 5.42 us -> 0.91 us
    psum x1 -> x0, waiting for transfers between devices: 118 us -> none  [body(): summed = lax.psum(partial_grads, ('row', 'col'))]
    ppermute x44 -> x10, starting transfers between devices: 117 us -> 12.4 us  [swap(): return lax.ppermute(x, ('row', 'col'), [(i, partner(i)) for i in places])]
    ppermute x44 -> x10, waiting for transfers between devices: 46.2 us -> 13.3 us  [swap(): return lax.ppermute(x, ('row', 'col'), [(i, partner(i)) for i in places])]
    pallas_call x0 -> x8, Pallas kernels: none -> 5.62 us  [call(): pl.pallas_call(kernel, out_shape=outs, in_specs=[pl.BlockSpec(memory_spac...]
    slice x23 -> x0, local copies, waits for them, and re-layouts: 3.15 us -> none  [the longest x21 2.04 us: with_halo(): lax.slice_in_dim(cells, cells.shape[dim] - width, cells.shape[dim], axis=...]
  transfers between devices with their start and end apart: 45 -> 10, of which waited for: 15 -> 8; matrix products, arithmetic and copies ran while one was open for 2% -> 0% of each run, Pallas kernels for 0% -> 11%
where the time goes in v1:
time: 33.2 us; the launch traced here: 33 us
  waiting for transfers between devices  13.3 us (40%)
  starting transfers between devices  12.4 us (37%)
  Pallas kernels  5.62 us (17%)
  local copies, waits for them, and re-layouts  0.91 us (3%)
  between operations  0.72 us (2%)
    ppermute x10, waiting for transfers between devices, swap(): return lax.ppermute(x, ('row', 'col'), [(i, partner(i)) for i in places])  13.3 us
    ppermute x10, starting transfers between devices, swap(): return lax.ppermute(x, ('row', 'col'), [(i, partner(i)) for i in places])  12.4 us
    pallas_call x8, Pallas kernels, call(): pl.pallas_call(kernel, out_shape=outs, in_specs=[pl.BlockSpec(memory_spac...  5.62 us
    unnamed x8, local copies, waits for them, and re-layouts  0.91 us
  transfers between devices with their start and end apart: 10, of which 8 were waited for; matrix products, arithmetic and copies ran while one was open for 0% of the time, Pallas kernels for 11%

profile of v1, /device:TPU:0, one launch (start us, length us, event | category | flops | bytes accessed | tf_op | source)
XLA Modules:
  0.0 33.0 jit_solution(651783881368260408)
XLA Ops:
  0.6 0.0 copy-start.1
  0.6 0.0 copy-start.3
  0.7 0.7 %copy-done.3 = s32[8,128]{1,0:T(8,128)S(1)} copy-done((s32[8,128]{1,0:T(8,128)S(1)}, s32[8,128]{1,0:T(8,128)}, u32[]{:S(2)}) %copy-start.3) | copy-done | bytes 4120
  1.4 0.0 copy-start.2
  1.4 0.2 copy-done.1
  1.6 0.0 copy-start
  1.6 0.3 shard_map.60
  1.8 0.5 %collective-permute-start = (bf16[336,128]{1,0:T(8,128)(2,1)S(1)}, bf16[336,128]{1,0:T(8,128)(2,1)S(1)}, u32[]{:S(2)}, u32[]{:S(2)}) collective-permute-start(bf16[336,128]{1,0:T(8,128)(2,1)S(1)} %get-tuple-element.22), channel_id=1, source_target_pairs={{0,1},{1,0},{2,3},{3,2},{4,5},{5,4},{6,7},{7,6},{8,16},{9,17},{10,... | collective-permute-start | bytes 258056 | tf_op jit(solution)/shard_map/ppermute | solution.py:315
  2.3 4.1 %collective-permute-start.1 = (bf16[336,128]{1,0:T(8,128)(2,1)S(1)}, bf16[336,128]{1,0:T(8,128)(2,1)S(1)}, u32[]{:S(2)}, u32[]{:S(2)}) collective-permute-start(bf16[336,128]{1,0:T(8,128)(2,1)S(1)} %get-tuple-element.23), channel_id=1, source_target_pairs={{0,8},{1,9},{2,10},{3,11},{4,12},{5,13},{6,14},{7,15},{8,0},{9,1},... | collective-permute-start | bytes 258056 | tf_op jit(solution)/shard_map/ppermute | solution.py:315
  6.5 0.0 copy-done.2
  6.5 0.0 copy-done
  6.5 0.3 %shard_map.61 = (bf16[128,512]{1,0:T(8,128)(2,1)S(1)}, bf16[128,64]{1,0:T(8,128)(2,1)S(1)}, bf16[128,768]{1,0:T(8,128)(2,1)S(1)}) custom-call(bf16[64,8,128]{2,1,0:T(8,128)(2,1)S(1)} %copy-done, bf16[6,64,64]{2,1,0:T(8,128)(2,1)S(1)} %copy-done.2), custom_call_target="tpu_custom_call" | custom-call | flops 1048576 | bytes 1048576 | tf_op jit(solution)/shard_map/pallas_call | solution.py:302
  6.8 0.0 collective-permute-done.second_ref.north_second_ref
  6.8 2.1 %collective-permute-done.1.first_ref.north_first_ref = bf16[336,128]{1,0:T(8,128)(2,1)S(1)} collective-permute-done((bf16[336,128]{1,0:T(8,128)(2,1)S(1)}, bf16[336,128]{1,0:T(8,128)(2,1)S(1)}, u32[]{:S(2)}, u32[]{:S(2)}) %collective-permute-start.1) | collective-permute-done | bytes 86048 | tf_op jit(solution)/shard_map/ppermute | solution.py:315
  8.9 0.1 shard_map.63
  9.0 0.8 %collective-permute-start.2 = (bf16[96,128]{1,0:T(8,128)(2,1)S(1)}, bf16[96,128]{1,0:T(8,128)(2,1)S(1)}, u32[]{:S(2)}, u32[]{:S(2)}) collective-permute-start(bf16[96,128]{1,0:T(8,128)(2,1)S(1)} %get-tuple-element.26), channel_id=1, source_target_pairs={{0,7},{1,2},{2,1},{3,4},{4,3},{5,6},{6,5},{7,0},{8,15},{9,10},{10,... | collective-permute-start | bytes 73736 | tf_op jit(solution)/shard_map/ppermute | solution.py:315
  9.8 0.9 %collective-permute-start.3 = (bf16[96,128]{1,0:T(8,128)(2,1)S(1)}, bf16[96,128]{1,0:T(8,128)(2,1)S(1)}, u32[]{:S(2)}, u32[]{:S(2)}) collective-permute-start(bf16[96,128]{1,0:T(8,128)(2,1)S(1)} %get-tuple-element.27), channel_id=1, source_target_pairs={{0,1},{1,0},{2,3},{3,2},{4,5},{5,4},{6,7},{7,6},{8,9},{9,8},{10,11... | collective-permute-start | bytes 73736 | tf_op jit(solution)/shard_map/ppermute | solution.py:315
  10.7 2.0 %shard_map.62 = (bf16[512,768]{1,0:T(8,128)(2,1)S(1)}, f32[3,64,128]{2,1,0:T(8,128)S(1)}, f32[432,128]{1,0:T(8,128)S(1)}) custom-call(bf16[512,128]{1,0:T(8,128)(2,1)S(1)} %get-tuple-element.21.body_ref, bf16[16,128]{1,0:T(8,128)(2,1)S(1)} %shard_map.59.mask_ref, bf16[336,128]{1,0:T(8,128)(2,1)S(1)} %collective-permute-done.second_ref.north_second_ref, ...), custom_call_target="tpu_custom_call" | custom-call | flops 268435456 | bytes 1048576 | tf_op jit(solution)/shard_map/pallas_call | solution.py:302
  12.7 0.7 %collective-permute-done.2.second_ref = bf16[96,128]{1,0:T(8,128)(2,1)S(1)} collective-permute-done((bf16[96,128]{1,0:T(8,128)(2,1)S(1)}, bf16[96,128]{1,0:T(8,128)(2,1)S(1)}, u32[]{:S(2)}, u32[]{:S(2)}) %collective-permute-start.2) | collective-permute-done | bytes 24608 | tf_op jit(solution)/shard_map/ppermute | solution.py:315
  13.4 0.0 collective-permute-done.3.first_ref
  13.4 0.9 %shard_map.64 = (bf16[64,768]{1,0:T(8,128)(2,1)S(1)}, f32[3,32,128]{2,1,0:T(8,128)S(1)}, f32[3,32,128]{2,1,0:T(8,128)S(1)}) custom-call(f32[432,128]{1,0:T(8,128)S(1)} %get-tuple-element.25.own_ref, bf16[16,128]{1,0:T(8,128)(2,1)S(1)} %shard_map.59.mask_ref, bf16[336,128]{1,0:T(8,128)(2,1)S(1)} %collective-permute-done.second_ref.north_second_ref, ...), custom_call_target="tpu_custom_call" | custom-call | flops 67108864 | bytes 1048576 | tf_op jit(solution)/shard_map/pallas_call | solution.py:302
  14.3 0.1 collective-permute-start.4
  14.4 1.2 %collective-permute-done.4 = f32[3,32,128]{2,1,0:T(8,128)S(1)} collective-permute-done((f32[3,32,128]{2,1,0:T(8,128)S(1)}, f32[3,32,128]{2,1,0:T(8,128)S(1)}, u32[]{:S(2)}, u32[]{:S(2)}) %collective-permute-start.4) | collective-permute-done | bytes 49184 | tf_op jit(solution)/shard_map/ppermute | solution.py:315
  15.7 0.7 %collective-permute-start.5 = (f32[3,32,128]{2,1,0:T(8,128)S(1)}, f32[3,32,128]{2,1,0:T(8,128)S(1)}, u32[]{:S(2)}, u32[]{:S(2)}) collective-permute-start(f32[3,32,128]{2,1,0:T(8,128)S(1)} %add.15), channel_id=1, source_target_pairs={{0,3},{1,8},{2,11},{3,0},{4,13},{5,6},{6,5},{7,14},{8,1},{9,10},{1... | collective-permute-start | bytes 147464 | tf_op jit(solution)/shard_map/ppermute | solution.py:315
  16.3 1.2 %shard_map.65 = bf16[64,8,128]{2,1,0:T(8,128)(2,1)} custom-call(bf16[128,768]{1,0:T(8,128)(2,1)S(1)} %get-tuple-element.35.weight_ref, bf16[512,768]{1,0:T(8,128)(2,1)S(1)} %get-tuple-element.36.inner_ref, bf16[64,768]{1,0:T(8,128)(2,1)S(1)} %get-tuple-element.37.rim_ref), custom_call_target="tpu_custom_call" | custom-call | flops 1048576 | bytes 1048576 | tf_op jit(solution)/shard_map/pallas_call | solution.py:302
  17.5 1.7 %collective-permute-done.5 = f32[3,32,128]{2,1,0:T(8,128)S(1)} collective-permute-done((f32[3,32,128]{2,1,0:T(8,128)S(1)}, f32[3,32,128]{2,1,0:T(8,128)S(1)}, u32[]{:S(2)}, u32[]{:S(2)}) %collective-permute-start.5) | collective-permute-done | bytes 49184 | tf_op jit(solution)/shard_map/ppermute | solution.py:315
  19.2 1.8 %collective-permute-start.6 = (f32[3,32,128]{2,1,0:T(8,128)S(1)}, f32[3,32,128]{2,1,0:T(8,128)S(1)}, u32[]{:S(2)}, u32[]{:S(2)}) collective-permute-start(f32[3,32,128]{2,1,0:T(8,128)S(1)} %add.16), channel_id=1, source_target_pairs={{0,9},{1,2},{2,1},{3,10},{4,7},{5,12},{6,15},{7,4},{8,11},{9,0},{1... | collective-permute-start | bytes 147464 | tf_op jit(solution)/shard_map/ppermute | solution.py:315
  21.1 1.8 %collective-permute-done.6 = f32[3,32,128]{2,1,0:T(8,128)S(1)} collective-permute-done((f32[3,32,128]{2,1,0:T(8,128)S(1)}, f32[3,32,128]{2,1,0:T(8,128)S(1)}, u32[]{:S(2)}, u32[]{:S(2)}) %collective-permute-start.6) | collective-permute-done | bytes 49184 | tf_op jit(solution)/shard_map/ppermute | solution.py:315
  22.9 1.4 %collective-permute-start.7 = (f32[3,32,128]{2,1,0:T(8,128)S(1)}, f32[3,32,128]{2,1,0:T(8,128)S(1)}, u32[]{:S(2)}, u32[]{:S(2)}) collective-permute-start(f32[3,32,128]{2,1,0:T(8,128)S(1)} %add.17), channel_id=1, source_target_pairs={{0,5},{1,16},{2,19},{3,6},{4,21},{5,0},{6,3},{7,22},{8,25},{9,12},... | collective-permute-start | bytes 147464 | tf_op jit(solution)/shard_map/ppermute | solution.py:315
  24.3 2.2 %collective-permute-done.7 = f32[3,32,128]{2,1,0:T(8,128)S(1)} collective-permute-done((f32[3,32,128]{2,1,0:T(8,128)S(1)}, f32[3,32,128]{2,1,0:T(8,128)S(1)}, u32[]{:S(2)}, u32[]{:S(2)}) %collective-permute-start.7) | collective-permute-done | bytes 49184 | tf_op jit(solution)/shard_map/ppermute | solution.py:315
  26.5 1.7 %collective-permute-start.8 = (f32[3,32,128]{2,1,0:T(8,128)S(1)}, f32[3,32,128]{2,1,0:T(8,128)S(1)}, u32[]{:S(2)}, u32[]{:S(2)}) collective-permute-start(f32[3,32,128]{2,1,0:T(8,128)S(1)} %add.18), channel_id=1, source_target_pairs={{0,17},{1,4},{2,7},{3,18},{4,1},{5,20},{6,23},{7,2},{8,13},{9,24},... | collective-permute-start | bytes 147464 | tf_op jit(solution)/shard_map/ppermute | solution.py:315
  28.2 2.8 %collective-permute-done.8 = f32[3,32,128]{2,1,0:T(8,128)S(1)} collective-permute-done((f32[3,32,128]{2,1,0:T(8,128)S(1)}, f32[3,32,128]{2,1,0:T(8,128)S(1)}, u32[]{:S(2)}, u32[]{:S(2)}) %collective-permute-start.8) | collective-permute-done | bytes 49184 | tf_op jit(solution)/shard_map/ppermute | solution.py:315
  31.0 0.4 %collective-permute-start.9 = (f32[3,32,128]{2,1,0:T(8,128)S(1)}, f32[3,32,128]{2,1,0:T(8,128)S(1)}, u32[]{:S(2)}, u32[]{:S(2)}) collective-permute-start(f32[3,32,128]{2,1,0:T(8,128)S(1)} %add.19.mine_ref), channel_id=1, source_target_pairs={{0,1},{1,0},{2,3},{3,2},{4,5},{5,4},{6,7},{7,6},{8,9},{9,8},{10,11... | collective-permute-start | bytes 147464 | tf_op jit(solution)/shard_map/ppermute | solution.py:315
  31.4 0.9 %collective-permute-done.9.other_ref = f32[3,32,128]{2,1,0:T(8,128)S(1)} collective-permute-done((f32[3,32,128]{2,1,0:T(8,128)S(1)}, f32[3,32,128]{2,1,0:T(8,128)S(1)}, u32[]{:S(2)}, u32[]{:S(2)}) %collective-permute-start.9) | collective-permute-done | bytes 49184 | tf_op jit(solution)/shard_map/ppermute | solution.py:315
  32.3 0.8 %shard_map.66 = f32[6,64,64]{2,1,0:T(8,128)} custom-call(f32[3,32,128]{2,1,0:T(8,128)S(1)} %add.19.mine_ref, f32[3,32,128]{2,1,0:T(8,128)S(1)} %collective-permute-done.9.other_ref), custom_call_target="tpu_custom_call" | custom-call | flops 65536 | bytes 1048576 | tf_op jit(solution)/shard_map/pallas_call | solution.py:302
  (6 shorter events, 0.0 us)
Async XLA Ops:
  0.6 0.9 %copy-start.1 = (bf16[64,8,128]{2,1,0:T(8,128)(2,1)S(1)}, bf16[64,8,128]{2,1,0:T(8,128)(2,1)}, u32[]{:S(2)}) copy-start(bf16[64,8,128]{2,1,0:T(8,128)(2,1)} %cot_ref.1) | copy-start | bytes 393220
  0.6 0.7 %copy-start.3 = (s32[8,128]{1,0:T(8,128)S(1)}, s32[8,128]{1,0:T(8,128)}, u32[]{:S(2)}) copy-start(s32[8,128]{1,0:T(8,128)} %mask_ref.1) | copy-start | bytes 12292
  1.4 5.1 %copy-start.2 = (bf16[6,64,64]{2,1,0:T(8,128)(2,1)S(1)}, bf16[6,64,64]{2,1,0:T(8,128)(2,1)}, u32[]{:S(2)}) copy-start(bf16[6,64,64]{2,1,0:T(8,128)(2,1)} %weight_ref.1) | copy-start | bytes 147460
  1.6 4.9 %copy-start = (bf16[64,8,128]{2,1,0:T(8,128)(2,1)S(1)}, bf16[64,8,128]{2,1,0:T(8,128)(2,1)}, u32[]{:S(2)}) copy-start(bf16[64,8,128]{2,1,0:T(8,128)(2,1)} %feature_ref.1) | copy-start | bytes 393220
  1.8 5.0 %collective-permute-start = (bf16[336,128]{1,0:T(8,128)(2,1)S(1)}, bf16[336,128]{1,0:T(8,128)(2,1)S(1)}, u32[]{:S(2)}, u32[]{:S(2)}) collective-permute-start(bf16[336,128]{1,0:T(8,128)(2,1)S(1)} %get-tuple-element.22), channel_id=1, source_target_pairs={{0,1},{1,0},{2,3},{3,2},{4,5},{5,4},{6,7},{7,6},{8,16},{9,17},{10,... | collective-permute-start | bytes 258056 | tf_op jit(solution)/shard_map/ppermute | solution.py:315
  2.3 6.6 %collective-permute-start.1 = (bf16[336,128]{1,0:T(8,128)(2,1)S(1)}, bf16[336,128]{1,0:T(8,128)(2,1)S(1)}, u32[]{:S(2)}, u32[]{:S(2)}) collective-permute-start(bf16[336,128]{1,0:T(8,128)(2,1)S(1)} %get-tuple-element.23), channel_id=1, source_target_pairs={{0,8},{1,9},{2,10},{3,11},{4,12},{5,13},{6,14},{7,15},{8,0},{9,1},... | collective-permute-start | bytes 258056 | tf_op jit(solution)/shard_map/ppermute | solution.py:315
  9.0 4.4 %collective-permute-start.2 = (bf16[96,128]{1,0:T(8,128)(2,1)S(1)}, bf16[96,128]{1,0:T(8,128)(2,1)S(1)}, u32[]{:S(2)}, u32[]{:S(2)}) collective-permute-start(bf16[96,128]{1,0:T(8,128)(2,1)S(1)} %get-tuple-element.26), channel_id=1, source_target_pairs={{0,7},{1,2},{2,1},{3,4},{4,3},{5,6},{6,5},{7,0},{8,15},{9,10},{10,... | collective-permute-start | bytes 73736 | tf_op jit(solution)/shard_map/ppermute | solution.py:315
  9.8 3.6 %collective-permute-start.3 = (bf16[96,128]{1,0:T(8,128)(2,1)S(1)}, bf16[96,128]{1,0:T(8,128)(2,1)S(1)}, u32[]{:S(2)}, u32[]{:S(2)}) collective-permute-start(bf16[96,128]{1,0:T(8,128)(2,1)S(1)} %get-tuple-element.27), channel_id=1, source_target_pairs={{0,1},{1,0},{2,3},{3,2},{4,5},{5,4},{6,7},{7,6},{8,9},{9,8},{10,11... | collective-permute-start | bytes 73736 | tf_op jit(solution)/shard_map/ppermute | solution.py:315
  14.3 1.3 %collective-permute-start.4 = (f32[3,32,128]{2,1,0:T(8,128)S(1)}, f32[3,32,128]{2,1,0:T(8,128)S(1)}, u32[]{:S(2)}, u32[]{:S(2)}) collective-permute-start(f32[3,32,128]{2,1,0:T(8,128)S(1)} %get-tuple-element.31), channel_id=1, source_target_pairs={{0,1},{1,0},{2,3},{3,2},{4,5},{5,4},{6,7},{7,6},{8,9},{9,8},{10,11... | collective-permute-start | bytes 147464 | tf_op jit(solution)/shard_map/ppermute | solution.py:315
  15.7 3.6 %collective-permute-start.5 = (f32[3,32,128]{2,1,0:T(8,128)S(1)}, f32[3,32,128]{2,1,0:T(8,128)S(1)}, u32[]{:S(2)}, u32[]{:S(2)}) collective-permute-start(f32[3,32,128]{2,1,0:T(8,128)S(1)} %add.15), channel_id=1, source_target_pairs={{0,3},{1,8},{2,11},{3,0},{4,13},{5,6},{6,5},{7,14},{8,1},{9,10},{1... | collective-permute-start | bytes 147464 | tf_op jit(solution)/shard_map/ppermute | solution.py:315
  19.2 3.6 %collective-permute-start.6 = (f32[3,32,128]{2,1,0:T(8,128)S(1)}, f32[3,32,128]{2,1,0:T(8,128)S(1)}, u32[]{:S(2)}, u32[]{:S(2)}) collective-permute-start(f32[3,32,128]{2,1,0:T(8,128)S(1)} %add.16), channel_id=1, source_target_pairs={{0,9},{1,2},{2,1},{3,10},{4,7},{5,12},{6,15},{7,4},{8,11},{9,0},{1... | collective-permute-start | bytes 147464 | tf_op jit(solution)/shard_map/ppermute | solution.py:315
  22.9 3.6 %collective-permute-start.7 = (f32[3,32,128]{2,1,0:T(8,128)S(1)}, f32[3,32,128]{2,1,0:T(8,128)S(1)}, u32[]{:S(2)}, u32[]{:S(2)}) collective-permute-start(f32[3,32,128]{2,1,0:T(8,128)S(1)} %add.17), channel_id=1, source_target_pairs={{0,5},{1,16},{2,19},{3,6},{4,21},{5,0},{6,3},{7,22},{8,25},{9,12},... | collective-permute-start | bytes 147464 | tf_op jit(solution)/shard_map/ppermute | solution.py:315
  26.5 4.5 %collective-permute-start.8 = (f32[3,32,128]{2,1,0:T(8,128)S(1)}, f32[3,32,128]{2,1,0:T(8,128)S(1)}, u32[]{:S(2)}, u32[]{:S(2)}) collective-permute-start(f32[3,32,128]{2,1,0:T(8,128)S(1)} %add.18), channel_id=1, source_target_pairs={{0,17},{1,4},{2,7},{3,18},{4,1},{5,20},{6,23},{7,2},{8,13},{9,24},... | collective-permute-start | bytes 147464 | tf_op jit(solution)/shard_map/ppermute | solution.py:315
  31.0 1.3 %collective-permute-start.9 = (f32[3,32,128]{2,1,0:T(8,128)S(1)}, f32[3,32,128]{2,1,0:T(8,128)S(1)}, u32[]{:S(2)}, u32[]{:S(2)}) collective-permute-start(f32[3,32,128]{2,1,0:T(8,128)S(1)} %add.19.mine_ref), channel_id=1, source_target_pairs={{0,1},{1,0},{2,3},{3,2},{4,5},{5,4},{6,7},{7,6},{8,9},{9,8},{10,11... | collective-permute-start | bytes 147464 | tf_op jit(solution)/shard_map/ppermute | solution.py:315

commit v2 on v1

--- a/solution.py
+++ b/solution.py
@@ -9,6 +9,7 @@
 from jax.sharding import PartitionSpec as P
 
 RIM = 8
+NOTES = 16
 F32 = jnp.float32
 BF16 = jnp.bfloat16
 NT = (((1,), (1,)), ((), ()))
@@ -24,13 +25,6 @@
 
 def even_place(axis):
     return lax.axis_index(axis) % 2 == 0
-
-
-def even_parity():
-    place = lax.axis_index("row") * lax.axis_size("col") + lax.axis_index("col")
-    for shift in (16, 8, 4, 2, 1):
-        place = place ^ (place >> shift)
-    return place % 2 == 0
 
 
 def in_order(axis, first, second):
@@ -109,12 +103,18 @@
     return jnp.concatenate([north[:rows], mask_ref[...].astype(F32)[:rows], south[:rows]], axis=0)
 
 
+def edge_lanes(masks):
+    cols = masks.shape[1]
+    return pltpu.roll(masks, cols // 4, 1), pltpu.roll(masks, cols - cols // 4, 1)
+
+
 def strips_kernel(halo, body_ref, mask_ref, second_ref, first_ref, to_first_ref, to_second_ref):
     rows = mask_ref.shape[0] // 2
     half = body_ref.shape[0] // rows
     total = rows + 2 * halo
     marks = 3 * rows
     masks = all_masks(halo, half, mask_ref, first_ref, second_ref)
+    ahead, behind = edge_lanes(masks)
     leading = row_pieces(halo, half, body_ref, first_ref, second_ref, 0, 2 * RIM)
     trailing = row_pieces(halo, half, body_ref, first_ref, second_ref, half - 2 * RIM, 2 * RIM)
     low = iota((RIM, body_ref.shape[1]), 1) < body_ref.shape[1] // 2
@@ -124,7 +124,7 @@
         east.append(jnp.where(low, swap_halves(trailing[n][RIM:]), trailing[n + total // 2][RIM:]))
     spare = to_first_ref.shape[0] - total // 2 * RIM - marks
     blank = [jnp.zeros((spare, body_ref.shape[1]), F32)] if spare else []
-    west, east = (jnp.concatenate([masks, *x] + blank, axis=0) for x in (west, east))
+    west, east = (jnp.concatenate([marks_sent, *x] + blank, axis=0) for marks_sent, x in ((behind, west), (ahead, east)))
     even = even_place("col")
     to_first_ref[...] = jnp.where(even, east, west).astype(BF16)
     to_second_ref[...] = jnp.where(even, west, east).astype(BF16)
@@ -180,12 +180,15 @@
 
 
 def interior_kernel(
-    orders, body_ref, mask_ref, second_ref, first_ref, feature_ref, terms_ref, sums_ref, own_ref, even_ref, odd_ref, scale_ref
+    orders, body_ref, mask_ref, second_ref, first_ref, feature_ref, terms_ref, sums_ref, own_ref, centre_ref, even_ref, odd_ref, scale_ref
 ):
     rows, cols = mask_ref.shape[0] // 2, mask_ref.shape[1]
     half, halo, lanes = cols // 2, orders - 1, body_ref.shape[1]
     tall = half + 2 * RIM
-    across = compact_scales(all_masks(halo, half, mask_ref, first_ref, second_ref))
+    masks = all_masks(halo, half, mask_ref, first_ref, second_ref)
+    ahead, behind = edge_lanes(masks)
+    centre_ref[...] = jnp.where(iota(masks.shape, 1) < half, ahead, behind)
+    across = compact_scales(masks)
     rim = jnp.zeros((RIM, across.shape[1]), F32)
     left = jnp.concatenate([rim, across[: half + RIM]], axis=0)
     right = jnp.concatenate([across[half - RIM :], rim], axis=0)
@@ -219,20 +222,42 @@
             sums_ref[k // 2] = order_products(k // 2, lanes, feature_ref[...], terms_ref)
 
 
+def store_sums(message_ref, blocks, exponent):
+    scale, at = jnp.exp2(9.0 - exponent), 0
+    for block in blocks:
+        for row in range(0, block.shape[0], 8):
+            message_ref[at : at + 8, :] = block[row : row + 8] * scale
+            at += 8
+    message_ref[at:, :] = jnp.concatenate([exponent] * (NOTES // 8), axis=0)
+
+
+def add_kernel(mine_ref, received_ref, out_ref):
+    notes = mine_ref.shape[0] - NOTES
+    mine, received = mine_ref[notes : notes + 8, :], received_ref[notes : notes + 8, :]
+    scales = jnp.exp2(mine - 9.0), jnp.exp2(received - 9.0)
+    sums = []
+    for row in range(0, notes, 8):
+        at = slice(row, row + 8)
+        sums.append(mine_ref[at, :] * scales[0] + received_ref[at, :] * scales[1])
+    if out_ref.shape[0] == notes:
+        out_ref[...] = jnp.concatenate(sums, axis=0)
+    else:
+        store_sums(out_ref, sums, jnp.maximum(mine, received) + 1.0)
+
+
 def edge_kernel(
-    orders, own_ref, mask_ref, north_second_ref, north_first_ref, second_ref, first_ref, rim_ref, sums_ref,
-    terms_ref, keep_ref, give_ref, even_ref, odd_ref, scale_ref, wide_ref,
+    orders, own_ref, centre_ref, second_ref, first_ref, rim_ref, sums_ref,
+    terms_ref, message_ref, even_ref, odd_ref, scale_ref, wide_ref,
 ):
-    rows, cols = mask_ref.shape[0] // 2, mask_ref.shape[1]
-    half, halo, lanes = cols // 2, orders - 1, own_ref.shape[1]
+    rows, cols = centre_ref.shape[0] // 3, centre_ref.shape[1]
+    halo, lanes, quarter = orders - 1, own_ref.shape[1], cols // 4
     channels, total, tall = lanes // 2, rows + 2 * halo, 3 * RIM
     west, east = in_order("col", first_ref[...].astype(F32), second_ref[...].astype(F32))
-    lower = iota((3 * rows, cols), 1) < half
-    centre = all_masks(halo, half, mask_ref, north_first_ref, north_second_ref)
-    beside = jnp.where(lower, east[: 3 * rows], west[: 3 * rows])
-    across = compact_scales(jnp.concatenate([centre, beside], axis=1))
-    left = jnp.concatenate([across[2 * cols - RIM :], across[: 2 * RIM]], axis=0)
-    spread_scales(left, across[cols - 2 * RIM : cols + RIM], scale_ref)
+    lane = iota((3 * rows, cols), 1)
+    masks = jnp.where(lane < quarter, west[: 3 * rows], jnp.where(lane < 3 * quarter, centre_ref[...], east[: 3 * rows]))
+    across = compact_scales(masks)
+    begin = quarter - RIM
+    spread_scales(across[begin : begin + tall], across[3 * quarter - 2 * RIM : 3 * quarter + RIM], scale_ref)
 
     low = iota((RIM, lanes), 1) < channels
     for q in range(total):
@@ -256,12 +281,11 @@
         next_term(k, tall, scale_ref, newer, older, keep)
         newer, older = older, newer
     terms_ref[...] = wide_ref[...].astype(BF16)
-    upper = even_parity()
-    for b in range(orders // 2):
-        block = sums_ref[b] + order_products(b, lanes, rim_ref[...], terms_ref)
-        a, b_half = block[: channels // 2], block[channels // 2 :]
-        keep_ref[b] = jnp.where(upper, a, b_half)
-        give_ref[b] = jnp.where(upper, b_half, a)
+    blocks = [sums_ref[b] + order_products(b, lanes, rim_ref[...], terms_ref) for b in range(orders // 2)]
+    tiles = [jnp.abs(block[row : row + 8]) for block in blocks for row in range(0, channels, 8)]
+    largest = functools.reduce(jnp.maximum, tiles)
+    exponent = jnp.floor(jnp.log2(jnp.maximum(largest, 1e-30))) + 1.0
+    store_sums(message_ref, blocks, exponent)
 
 
 def mix_kernel(weight_ref, inner_ref, rim_ref, grad_ref, wide_ref, terms_ref):
@@ -289,11 +313,10 @@
 
 
 def finish_kernel(divisor, mine_ref, other_ref, out_ref):
-    orders, channels, _ = out_ref.shape
-    upper = even_parity()
-    for b in range(orders // 2):
-        mine, other = mine_ref[b] / divisor, other_ref[b] / divisor
-        block = jnp.concatenate([jnp.where(upper, mine, other), jnp.where(upper, other, mine)], axis=0)
+    channels = out_ref.shape[1]
+    for b in range(out_ref.shape[0] // 2):
+        at = slice(b * channels, (b + 1) * channels)
+        block = (mine_ref[at, :] + other_ref[at, :]) / divisor
         out_ref[2 * b] = block[:, :channels]
         out_ref[2 * b + 1] = block[:, channels:]
 
@@ -336,21 +359,25 @@
     return swap(first, lambda i: (i // across ^ 1) * across + i % across), swap(second, after_odd)
 
 
-def sum_everywhere(keep, give, work, *args):
+def sum_everywhere(part, work, *args):
     across, down = lax.axis_size("col"), lax.axis_size("row")
     beside = list(range(1, across.bit_length() - 1))
     below = list(range(across.bit_length() - 1, (across * down).bit_length() - 1))
     turns = [(beside[n : n + 1], below[n : n + 1]) for n in range(max(len(beside), len(below)))]
     even = [bit for a, b in turns for bit in a + b]
     odd = [bit for a, b in turns for bit in b + a]
-    mine = keep + swap(give, lambda i: i ^ 1)
     for n, bits in enumerate(zip(even, odd)):
-        received = swap(mine, lambda i: i ^ (1 << bits[i.bit_count() % 2]) ^ 1)
+        message = lax.optimization_barrier(lax.reduce_precision(part, 5, 10).astype(jnp.float16))
+        received = swap(message, lambda i: i ^ (1 << bits[i.bit_count() % 2]) ^ 1)
         if n == 0:
-            _, *args = lax.optimization_barrier((mine, *args))
+            _, *args = lax.optimization_barrier((message, *args))
             received, done = lax.optimization_barrier((received, work(*args)))
-        mine = mine + received
-    return mine, swap(mine, lambda i: i ^ 1), done
+        rows = part.shape[0] - (NOTES if n == len(even) - 1 else 0)
+        part = call(
+            add_kernel, jax.ShapeDtypeStruct((rows, part.shape[1]), F32), [], 1 << 16,
+            message.astype(F32), received.astype(F32),
+        )
+    return part, swap(part, lambda i: i ^ 1), done
 
 
 def body(feature, cotangent, order_weight, pixel_mask):
@@ -383,21 +410,23 @@
     small = pltpu.VMEM((total * 3 * RIM, lanes), F32)
     terms = shape((rows * half, orders * lanes), BF16)
     rim_terms = shape((rows * RIM, orders * lanes), BF16)
-    part = shape((orders // 2, channels // 2, lanes), F32)
-    inner, sums, own = call(
+    inner, sums, own, centre = call(
         functools.partial(interior_kernel, orders),
-        [terms, shape((orders // 2, channels, lanes), F32), shape((total * 3 * RIM, lanes), F32)],
+        [
+            terms, shape((orders // 2, channels, lanes), F32), shape((total * 3 * RIM, lanes), F32),
+            shape((3 * rows, cols), F32),
+        ],
         [buffer, buffer, buffer], 1 << 28, cot_body, mask16, second, first, features,
     )
-    outer, keep, give = call(
-        functools.partial(edge_kernel, orders), [rim_terms, part, part],
+    outer, message = call(
+        functools.partial(edge_kernel, orders), [rim_terms, shape((orders // 2 * channels + NOTES, lanes), F32)],
         [small, small, small, pltpu.VMEM(rim_terms.shape, F32)], 1 << 26,
-        own, mask16, second, first, west_second, west_first, rims, sums,
+        own, centre, west_second, west_first, rims, sums,
     )
     mix = functools.partial(
         call, mix_kernel, shape((channels, rows, cols), BF16), [wide, pltpu.VMEM(terms.shape, BF16)], 1 << 20
     )
-    mine, other, grad_feature = sum_everywhere(keep, give, mix, weights, inner, outer)
+    mine, other, grad_feature = sum_everywhere(message, mix, weights, inner, outer)
     pixel_count = rows * cols * lax.axis_size("row") * lax.axis_size("col")
     grad_order = call(
         functools.partial(finish_kernel, math.sqrt(pixel_count)),

time: 33.2 us -> 32.6 us (0.982)
  starting transfers between devices: 12.4 us -> 11.7 us
  waiting for transfers between devices: 13.3 us -> 12.9 us
    ppermute x10 -> x9, starting transfers between devices: 12.4 us -> 11.7 us  [swap(): return lax.ppermute(x, ('row', 'col'), [(i, partner(i)) for i in places])]
    ppermute x10 -> x9, waiting for transfers between devices: 13.3 us -> 12.9 us  [swap(): return lax.ppermute(x, ('row', 'col'), [(i, partner(i)) for i in places])]
    pallas_call x8 -> x12, Pallas kernels: 5.62 us -> 5.74 us  [call(): pl.pallas_call(kernel, out_shape=outs, in_specs=[pl.BlockSpec(memory_spac...]
  transfers between devices with their start and end apart: 10 -> 9, of which waited for: 8 -> 7; matrix products, arithmetic and copies ran while one was open for 0% -> 0% of each run, Pallas kernels for 11% -> 11%
where the time goes in v2:
time: 32.6 us; the launch traced here: 32.4 us
  waiting for transfers between devices  12.9 us (40%)
  starting transfers between devices  11.7 us (36%)
  Pallas kernels  5.74 us (18%)
  local copies, waits for them, and re-layouts  0.91 us (3%)
  between operations  0.77 us (2%)
  other arithmetic  0.33 us (1%)
    ppermute x9, waiting for transfers between devices, swap(): return lax.ppermute(x, ('row', 'col'), [(i, partner(i)) for i in places])  12.9 us
    ppermute x9, starting transfers between devices, swap(): return lax.ppermute(x, ('row', 'col'), [(i, partner(i)) for i in places])  11.7 us
    pallas_call x12, Pallas kernels, call(): pl.pallas_call(kernel, out_shape=outs, in_specs=[pl.BlockSpec(memory_spac...  5.74 us
    unnamed x8, local copies, waits for them, and re-layouts  0.91 us
  transfers between devices with their start and end apart: 9, of which 7 were waited for; matrix products, arithmetic and copies ran while one was open for 0% of the time, Pallas kernels for 11%

profile of v2, /device:TPU:0, one launch (start us, length us, event | category | flops | bytes accessed | tf_op | source)
XLA Modules:
  0.0 32.4 jit_solution(5960849477803442027)
XLA Ops:
  0.6 0.0 copy-start.1
  0.6 0.0 copy-start.3
  0.7 0.7 %copy-done.3 = s32[8,128]{1,0:T(8,128)S(1)} copy-done((s32[8,128]{1,0:T(8,128)S(1)}, s32[8,128]{1,0:T(8,128)}, u32[]{:S(2)}) %copy-start.3) | copy-done | bytes 4120
  1.4 0.0 copy-start.2
  1.4 0.2 copy-done.1
  1.6 0.0 copy-start
  1.6 0.3 shard_map.60
  1.8 0.5 %collective-permute-start = (bf16[336,128]{1,0:T(8,128)(2,1)S(1)}, bf16[336,128]{1,0:T(8,128)(2,1)S(1)}, u32[]{:S(2)}, u32[]{:S(2)}) collective-permute-start(bf16[336,128]{1,0:T(8,128)(2,1)S(1)} %get-tuple-element.22), channel_id=1, source_target_pairs={{0,1},{1,0},{2,3},{3,2},{4,5},{5,4},{6,7},{7,6},{8,16},{9,17},{10,... | collective-permute-start | bytes 258056 | tf_op jit(solution)/shard_map/ppermute | solution.py:338
  2.3 4.1 %collective-permute-start.1 = (bf16[336,128]{1,0:T(8,128)(2,1)S(1)}, bf16[336,128]{1,0:T(8,128)(2,1)S(1)}, u32[]{:S(2)}, u32[]{:S(2)}) collective-permute-start(bf16[336,128]{1,0:T(8,128)(2,1)S(1)} %get-tuple-element.23), channel_id=1, source_target_pairs={{0,8},{1,9},{2,10},{3,11},{4,12},{5,13},{6,14},{7,15},{8,0},{9,1},... | collective-permute-start | bytes 258056 | tf_op jit(solution)/shard_map/ppermute | solution.py:338
  6.5 0.0 copy-done.2
  6.5 0.0 copy-done
  6.5 0.3 %shard_map.61 = (bf16[128,512]{1,0:T(8,128)(2,1)S(1)}, bf16[128,64]{1,0:T(8,128)(2,1)S(1)}, bf16[128,768]{1,0:T(8,128)(2,1)S(1)}) custom-call(bf16[64,8,128]{2,1,0:T(8,128)(2,1)S(1)} %copy-done, bf16[6,64,64]{2,1,0:T(8,128)(2,1)S(1)} %copy-done.2), custom_call_target="tpu_custom_call" | custom-call | flops 1048576 | bytes 1048576 | tf_op jit(solution)/shard_map/pallas_call | solution.py:325
  6.8 0.0 collective-permute-done.second_ref
  6.8 2.1 %collective-permute-done.1.first_ref = bf16[336,128]{1,0:T(8,128)(2,1)S(1)} collective-permute-done((bf16[336,128]{1,0:T(8,128)(2,1)S(1)}, bf16[336,128]{1,0:T(8,128)(2,1)S(1)}, u32[]{:S(2)}, u32[]{:S(2)}) %collective-permute-start.1) | collective-permute-done | bytes 86048 | tf_op jit(solution)/shard_map/ppermute | solution.py:338
  8.9 0.1 shard_map.63
  9.0 0.8 %collective-permute-start.2 = (bf16[96,128]{1,0:T(8,128)(2,1)S(1)}, bf16[96,128]{1,0:T(8,128)(2,1)S(1)}, u32[]{:S(2)}, u32[]{:S(2)}) collective-permute-start(bf16[96,128]{1,0:T(8,128)(2,1)S(1)} %get-tuple-element.27), channel_id=1, source_target_pairs={{0,7},{1,2},{2,1},{3,4},{4,3},{5,6},{6,5},{7,0},{8,15},{9,10},{10,... | collective-permute-start | bytes 73736 | tf_op jit(solution)/shard_map/ppermute | solution.py:338
  9.8 0.9 %collective-permute-start.3 = (bf16[96,128]{1,0:T(8,128)(2,1)S(1)}, bf16[96,128]{1,0:T(8,128)(2,1)S(1)}, u32[]{:S(2)}, u32[]{:S(2)}) collective-permute-start(bf16[96,128]{1,0:T(8,128)(2,1)S(1)} %get-tuple-element.28), channel_id=1, source_target_pairs={{0,1},{1,0},{2,3},{3,2},{4,5},{5,4},{6,7},{7,6},{8,9},{9,8},{10,11... | collective-permute-start | bytes 73736 | tf_op jit(solution)/shard_map/ppermute | solution.py:338
  10.7 2.0 %shard_map.62 = (bf16[512,768]{1,0:T(8,128)(2,1)S(1)}, f32[3,64,128]{2,1,0:T(8,128)S(1)}, f32[432,128]{1,0:T(8,128)S(1)}, f32[24,128]{1,0:T(8,128)S(1)}) custom-call(bf16[512,128]{1,0:T(8,128)(2,1)S(1)} %get-tuple-element.21.body_ref, bf16[16,128]{1,0:T(8,128)(2,1)S(1)} %shard_map.59.mask_ref, bf16[336,128]{1,0:T(8,128)(2,1)S(1)} %collective-permute-done.second_ref, ...), custom_call_target="tpu_custom_call" | custom-call | flops 268435456 | bytes 1048576 | tf_op jit(solution)/shard_map/pallas_call | solution.py:325
  12.7 0.7 %collective-permute-done.2.second_ref = bf16[96,128]{1,0:T(8,128)(2,1)S(1)} collective-permute-done((bf16[96,128]{1,0:T(8,128)(2,1)S(1)}, bf16[96,128]{1,0:T(8,128)(2,1)S(1)}, u32[]{:S(2)}, u32[]{:S(2)}) %collective-permute-start.2) | collective-permute-done | bytes 24608 | tf_op jit(solution)/shard_map/ppermute | solution.py:338
  13.4 0.0 collective-permute-done.3.first_ref
  13.4 1.0 %shard_map.64 = (bf16[64,768]{1,0:T(8,128)(2,1)S(1)}, f32[208,128]{1,0:T(8,128)S(1)}) custom-call(f32[432,128]{1,0:T(8,128)S(1)} %get-tuple-element.25.own_ref, f32[24,128]{1,0:T(8,128)S(1)} %get-tuple-element.26.centre_ref, bf16[96,128]{1,0:T(8,128)(2,1)S(1)} %collective-permute-done.2.second_ref, bf16[96,128]{1,0:T(8,128)(2,1)S(1)} %collective-permute-done.3.first_ref, ...), custom_call_target="tpu_custom_call" | custom-call | flops 67108864 | bytes 1048576 | tf_op jit(solution)/shard_map/pallas_call | solution.py:325
  14.4 0.1 reduce-precision_convert_fusion.3
  14.5 0.5 %collective-permute-start.4 = (f16[208,128]{1,0:T(8,128)(2,1)S(1)}, f16[208,128]{1,0:T(8,128)(2,1)S(1)}, u32[]{:S(2)}, u32[]{:S(2)}) collective-permute-start(f16[208,128]{1,0:T(8,128)(2,1)S(1)} %reduce-precision_convert_fusion.3), channel_id=1, source_target_pairs={{0,3},{1,8},{2,11},{3,0},{4,13},{5,6},{6,5},{7,14},{8,1},{9,10},{1... | collective-permute-start | bytes 159752 | tf_op jit(solution)/shard_map/ppermute | solution.py:338
  15.0 1.2 %shard_map.65 = bf16[64,8,128]{2,1,0:T(8,128)(2,1)} custom-call(bf16[128,768]{1,0:T(8,128)(2,1)S(1)} %get-tuple-element.35.weight_ref, bf16[512,768]{1,0:T(8,128)(2,1)S(1)} %get-tuple-element.36.inner_ref, bf16[64,768]{1,0:T(8,128)(2,1)S(1)} %get-tuple-element.37.rim_ref), custom_call_target="tpu_custom_call" | custom-call | flops 1048576 | bytes 1048576 | tf_op jit(solution)/shard_map/pallas_call | solution.py:325
  16.2 1.9 %collective-permute-done.4 = f16[208,128]{1,0:T(8,128)(2,1)S(1)} collective-permute-done((f16[208,128]{1,0:T(8,128)(2,1)S(1)}, f16[208,128]{1,0:T(8,128)(2,1)S(1)}, u32[]{:S(2)}, u32[]{:S(2)}) %collective-permute-start.4) | collective-permute-done | bytes 53280 | tf_op jit(solution)/shard_map/ppermute | solution.py:338
  18.1 0.1 reduce-precision_convert_fusion.2
  18.2 1.3 %collective-permute-start.5 = (f16[208,128]{1,0:T(8,128)(2,1)S(1)}, f16[208,128]{1,0:T(8,128)(2,1)S(1)}, u32[]{:S(2)}, u32[]{:S(2)}) collective-permute-start(f16[208,128]{1,0:T(8,128)(2,1)S(1)} %reduce-precision_convert_fusion.2), channel_id=1, source_target_pairs={{0,9},{1,2},{2,1},{3,10},{4,7},{5,12},{6,15},{7,4},{8,11},{9,0},{1... | collective-permute-start | bytes 159752 | tf_op jit(solution)/shard_map/ppermute | solution.py:338
  19.5 2.3 %collective-permute-done.5 = f16[208,128]{1,0:T(8,128)(2,1)S(1)} collective-permute-done((f16[208,128]{1,0:T(8,128)(2,1)S(1)}, f16[208,128]{1,0:T(8,128)(2,1)S(1)}, u32[]{:S(2)}, u32[]{:S(2)}) %collective-permute-start.5) | collective-permute-done | bytes 53280 | tf_op jit(solution)/shard_map/ppermute | solution.py:338
  21.9 0.1 reduce-precision_convert_fusion.1
  22.0 1.4 %collective-permute-start.6 = (f16[208,128]{1,0:T(8,128)(2,1)S(1)}, f16[208,128]{1,0:T(8,128)(2,1)S(1)}, u32[]{:S(2)}, u32[]{:S(2)}) collective-permute-start(f16[208,128]{1,0:T(8,128)(2,1)S(1)} %reduce-precision_convert_fusion.1), channel_id=1, source_target_pairs={{0,5},{1,16},{2,19},{3,6},{4,21},{5,0},{6,3},{7,22},{8,25},{9,12},... | collective-permute-start | bytes 159752 | tf_op jit(solution)/shard_map/ppermute | solution.py:338
  23.4 2.2 %collective-permute-done.6 = f16[208,128]{1,0:T(8,128)(2,1)S(1)} collective-permute-done((f16[208,128]{1,0:T(8,128)(2,1)S(1)}, f16[208,128]{1,0:T(8,128)(2,1)S(1)}, u32[]{:S(2)}, u32[]{:S(2)}) %collective-permute-start.6) | collective-permute-done | bytes 53280 | tf_op jit(solution)/shard_map/ppermute | solution.py:338
  25.6 0.1 reduce-precision_convert_fusion
  25.7 1.7 %collective-permute-start.7 = (f16[208,128]{1,0:T(8,128)(2,1)S(1)}, f16[208,128]{1,0:T(8,128)(2,1)S(1)}, u32[]{:S(2)}, u32[]{:S(2)}) collective-permute-start(f16[208,128]{1,0:T(8,128)(2,1)S(1)} %reduce-precision_convert_fusion), channel_id=1, source_target_pairs={{0,17},{1,4},{2,7},{3,18},{4,1},{5,20},{6,23},{7,2},{8,13},{9,24},... | collective-permute-start | bytes 159752 | tf_op jit(solution)/shard_map/ppermute | solution.py:338
  27.4 2.8 %collective-permute-done.7 = f16[208,128]{1,0:T(8,128)(2,1)S(1)} collective-permute-done((f16[208,128]{1,0:T(8,128)(2,1)S(1)}, f16[208,128]{1,0:T(8,128)(2,1)S(1)}, u32[]{:S(2)}, u32[]{:S(2)}) %collective-permute-start.7) | collective-permute-done | bytes 53280 | tf_op jit(solution)/shard_map/ppermute | solution.py:338
  30.3 0.5 %collective-permute-start.8 = (f32[192,128]{1,0:T(8,128)S(1)}, f32[192,128]{1,0:T(8,128)S(1)}, u32[]{:S(2)}, u32[]{:S(2)}) collective-permute-start(f32[192,128]{1,0:T(8,128)S(1)} %shard_map.69.mine_ref), channel_id=1, source_target_pairs={{0,1},{1,0},{2,3},{3,2},{4,5},{5,4},{6,7},{7,6},{8,9},{9,8},{10,11... | collective-permute-start | bytes 294920 | tf_op jit(solution)/shard_map/ppermute | solution.py:338
  30.7 0.9 %collective-permute-done.8.other_ref = f32[192,128]{1,0:T(8,128)S(1)} collective-permute-done((f32[192,128]{1,0:T(8,128)S(1)}, f32[192,128]{1,0:T(8,128)S(1)}, u32[]{:S(2)}, u32[]{:S(2)}) %collective-permute-start.8) | collective-permute-done | bytes 98336 | tf_op jit(solution)/shard_map/ppermute | solution.py:338
  31.7 0.8 %shard_map.70 = f32[6,64,64]{2,1,0:T(8,128)} custom-call(f32[192,128]{1,0:T(8,128)S(1)} %shard_map.69.mine_ref, f32[192,128]{1,0:T(8,128)S(1)} %collective-permute-done.8.other_ref), custom_call_target="tpu_custom_call" | custom-call | flops 65536 | bytes 1048576 | tf_op jit(solution)/shard_map/pallas_call | solution.py:325
  (13 shorter events, 0.2 us)
Async XLA Ops:
  0.6 0.9 %copy-start.1 = (bf16[64,8,128]{2,1,0:T(8,128)(2,1)S(1)}, bf16[64,8,128]{2,1,0:T(8,128)(2,1)}, u32[]{:S(2)}) copy-start(bf16[64,8,128]{2,1,0:T(8,128)(2,1)} %cot_ref.1) | copy-start | bytes 393220
  0.6 0.7 %copy-start.3 = (s32[8,128]{1,0:T(8,128)S(1)}, s32[8,128]{1,0:T(8,128)}, u32[]{:S(2)}) copy-start(s32[8,128]{1,0:T(8,128)} %mask_ref.1) | copy-start | bytes 12292
  1.4 5.1 %copy-start.2 = (bf16[6,64,64]{2,1,0:T(8,128)(2,1)S(1)}, bf16[6,64,64]{2,1,0:T(8,128)(2,1)}, u32[]{:S(2)}) copy-start(bf16[6,64,64]{2,1,0:T(8,128)(2,1)} %weight_ref.1) | copy-start | bytes 147460
  1.6 4.9 %copy-start = (bf16[64,8,128]{2,1,0:T(8,128)(2,1)S(1)}, bf16[64,8,128]{2,1,0:T(8,128)(2,1)}, u32[]{:S(2)}) copy-start(bf16[64,8,128]{2,1,0:T(8,128)(2,1)} %feature_ref.1) | copy-start | bytes 393220
  1.8 5.0 %collective-permute-start = (bf16[336,128]{1,0:T(8,128)(2,1)S(1)}, bf16[336,128]{1,0:T(8,128)(2,1)S(1)}, u32[]{:S(2)}, u32[]{:S(2)}) collective-permute-start(bf16[336,128]{1,0:T(8,128)(2,1)S(1)} %get-tuple-element.22), channel_id=1, source_target_pairs={{0,1},{1,0},{2,3},{3,2},{4,5},{5,4},{6,7},{7,6},{8,16},{9,17},{10,... | collective-permute-start | bytes 258056 | tf_op jit(solution)/shard_map/ppermute | solution.py:338
  2.3 6.6 %collective-permute-start.1 = (bf16[336,128]{1,0:T(8,128)(2,1)S(1)}, bf16[336,128]{1,0:T(8,128)(2,1)S(1)}, u32[]{:S(2)}, u32[]{:S(2)}) collective-permute-start(bf16[336,128]{1,0:T(8,128)(2,1)S(1)} %get-tuple-element.23), channel_id=1, source_target_pairs={{0,8},{1,9},{2,10},{3,11},{4,12},{5,13},{6,14},{7,15},{8,0},{9,1},... | collective-permute-start | bytes 258056 | tf_op jit(solution)/shard_map/ppermute | solution.py:338
  9.0 4.4 %collective-permute-start.2 = (bf16[96,128]{1,0:T(8,128)(2,1)S(1)}, bf16[96,128]{1,0:T(8,128)(2,1)S(1)}, u32[]{:S(2)}, u32[]{:S(2)}) collective-permute-start(bf16[96,128]{1,0:T(8,128)(2,1)S(1)} %get-tuple-element.27), channel_id=1, source_target_pairs={{0,7},{1,2},{2,1},{3,4},{4,3},{5,6},{6,5},{7,0},{8,15},{9,10},{10,... | collective-permute-start | bytes 73736 | tf_op jit(solution)/shard_map/ppermute | solution.py:338
  9.8 3.6 %collective-permute-start.3 = (bf16[96,128]{1,0:T(8,128)(2,1)S(1)}, bf16[96,128]{1,0:T(8,128)(2,1)S(1)}, u32[]{:S(2)}, u32[]{:S(2)}) collective-permute-start(bf16[96,128]{1,0:T(8,128)(2,1)S(1)} %get-tuple-element.28), channel_id=1, source_target_pairs={{0,1},{1,0},{2,3},{3,2},{4,5},{5,4},{6,7},{7,6},{8,9},{9,8},{10,11... | collective-permute-start | bytes 73736 | tf_op jit(solution)/shard_map/ppermute | solution.py:338
  14.5 3.6 %collective-permute-start.4 = (f16[208,128]{1,0:T(8,128)(2,1)S(1)}, f16[208,128]{1,0:T(8,128)(2,1)S(1)}, u32[]{:S(2)}, u32[]{:S(2)}) collective-permute-start(f16[208,128]{1,0:T(8,128)(2,1)S(1)} %reduce-precision_convert_fusion.3), channel_id=1, source_target_pairs={{0,3},{1,8},{2,11},{3,0},{4,13},{5,6},{6,5},{7,14},{8,1},{9,10},{1... | collective-permute-start | bytes 159752 | tf_op jit(solution)/shard_map/ppermute | solution.py:338
  18.2 3.6 %collective-permute-start.5 = (f16[208,128]{1,0:T(8,128)(2,1)S(1)}, f16[208,128]{1,0:T(8,128)(2,1)S(1)}, u32[]{:S(2)}, u32[]{:S(2)}) collective-permute-start(f16[208,128]{1,0:T(8,128)(2,1)S(1)} %reduce-precision_convert_fusion.2), channel_id=1, source_target_pairs={{0,9},{1,2},{2,1},{3,10},{4,7},{5,12},{6,15},{7,4},{8,11},{9,0},{1... | collective-permute-start | bytes 159752 | tf_op jit(solution)/shard_map/ppermute | solution.py:338
  22.0 3.6 %collective-permute-start.6 = (f16[208,128]{1,0:T(8,128)(2,1)S(1)}, f16[208,128]{1,0:T(8,128)(2,1)S(1)}, u32[]{:S(2)}, u32[]{:S(2)}) collective-permute-start(f16[208,128]{1,0:T(8,128)(2,1)S(1)} %reduce-precision_convert_fusion.1), channel_id=1, source_target_pairs={{0,5},{1,16},{2,19},{3,6},{4,21},{5,0},{6,3},{7,22},{8,25},{9,12},... | collective-permute-start | bytes 159752 | tf_op jit(solution)/shard_map/ppermute | solution.py:338
  25.7 4.5 %collective-permute-start.7 = (f16[208,128]{1,0:T(8,128)(2,1)S(1)}, f16[208,128]{1,0:T(8,128)(2,1)S(1)}, u32[]{:S(2)}, u32[]{:S(2)}) collective-permute-start(f16[208,128]{1,0:T(8,128)(2,1)S(1)} %reduce-precision_convert_fusion), channel_id=1, source_target_pairs={{0,17},{1,4},{2,7},{3,18},{4,1},{5,20},{6,23},{7,2},{8,13},{9,24},... | collective-permute-start | bytes 159752 | tf_op jit(solution)/shard_map/ppermute | solution.py:338
  30.3 1.4 %collective-permute-start.8 = (f32[192,128]{1,0:T(8,128)S(1)}, f32[192,128]{1,0:T(8,128)S(1)}, u32[]{:S(2)}, u32[]{:S(2)}) collective-permute-start(f32[192,128]{1,0:T(8,128)S(1)} %shard_map.69.mine_ref), channel_id=1, source_target_pairs={{0,1},{1,0},{2,3},{3,2},{4,5},{5,4},{6,7},{7,6},{8,9},{9,8},{10,11... | collective-permute-start | bytes 294920 | tf_op jit(solution)/shard_map/ppermute | solution.py:338

commit v3 on v2

--- a/solution.py
+++ b/solution.py
@@ -134,7 +134,7 @@
     rows, cols = mask.shape
     column = mask + pltpu.roll(mask, 1, 0) + pltpu.roll(mask, rows - 1, 0)
     degree = mask * (column + pltpu.roll(column, 1, 1) + pltpu.roll(column, cols - 1, 1) - mask)
-    return jnp.transpose(mask * jnp.sqrt(2.0 / jnp.maximum(degree, 1.0)), (1, 0))
+    return jnp.transpose(mask * lax.rsqrt(jnp.maximum(0.5 * degree, 0.5)), (1, 0))
 
 
 def spread_scales(left, right, scale_ref):
@@ -170,9 +170,9 @@
         above, here = here, below
 
 
-def order_products(b, lanes, feature, terms):
+def order_products(lanes, feature, terms):
     channels = lanes // 2
-    product = jnp.dot(feature, terms[:, 2 * b * lanes : 2 * (b + 1) * lanes], preferred_element_type=F32)
+    product = jnp.dot(feature, terms, preferred_element_type=F32)
     near, far = product[:channels], product[channels:]
     even = near[:, :lanes] + swap_halves(far[:, :lanes])
     odd = swap_halves(near[:, lanes:]) + far[:, lanes:]
@@ -219,7 +219,8 @@
         next_term(k, tall, scale_ref, newer, older, keep)
         newer, older = older, newer
         if k % 2:
-            sums_ref[k // 2] = order_products(k // 2, lanes, feature_ref[...], terms_ref)
+            pair = slice((k - 1) * lanes, (k + 1) * lanes)
+            sums_ref[k // 2] = order_products(lanes, feature_ref[...], terms_ref[:, pair])
 
 
 def store_sums(message_ref, blocks, exponent):
@@ -271,6 +272,7 @@
         odd_ref[at + 2 * RIM : at + tall, :] = jnp.where(low, own_ref[at + 2 * RIM : at + tall, :], after)
 
     wide_ref[:, :lanes] = jnp.zeros((rows * RIM, lanes), F32)
+    blocks = []
     newer, older = odd_ref, even_ref
     for k in range(1, orders):
         def keep(q, fresh):
@@ -280,8 +282,11 @@
 
         next_term(k, tall, scale_ref, newer, older, keep)
         newer, older = older, newer
-    terms_ref[...] = wide_ref[...].astype(BF16)
-    blocks = [sums_ref[b] + order_products(b, lanes, rim_ref[...], terms_ref) for b in range(orders // 2)]
+        if k % 2:
+            pair = slice((k - 1) * lanes, (k + 1) * lanes)
+            terms = wide_ref[:, pair].astype(BF16)
+            terms_ref[:, pair] = terms
+            blocks.append(sums_ref[k // 2] + order_products(lanes, rim_ref[...], terms))
     tiles = [jnp.abs(block[row : row + 8]) for block in blocks for row in range(0, channels, 8)]
     largest = functools.reduce(jnp.maximum, tiles)
     exponent = jnp.floor(jnp.log2(jnp.maximum(largest, 1e-30))) + 1.0
@@ -367,7 +372,7 @@
     even = [bit for a, b in turns for bit in a + b]
     odd = [bit for a, b in turns for bit in b + a]
     for n, bits in enumerate(zip(even, odd)):
-        message = lax.optimization_barrier(lax.reduce_precision(part, 5, 10).astype(jnp.float16))
+        message = lax.optimization_barrier(part.astype(jnp.float16))
         received = swap(message, lambda i: i ^ (1 << bits[i.bit_count() % 2]) ^ 1)
         if n == 0:
             _, *args = lax.optimization_barrier((message, *args))

time: 32.6 us -> 32.4 us (level)
  no operation moved by 1% of the time
where the time goes in v3:
time: 32.4 us; the launch traced here: 32.2 us
  waiting for transfers between devices  12.9 us (40%)
  starting transfers between devices  11.8 us (36%)
  Pallas kernels  5.72 us (18%)
  local copies, waits for them, and re-layouts  0.91 us (3%)
  between operations  0.78 us (2%)
    ppermute x9, waiting for transfers between devices, swap(): return lax.ppermute(x, ('row', 'col'), [(i, partner(i)) for i in places])  12.9 us
    ppermute x9, starting transfers between devices, swap(): return lax.ppermute(x, ('row', 'col'), [(i, partner(i)) for i in places])  11.8 us
    pallas_call x12, Pallas kernels, call(): pl.pallas_call(kernel, out_shape=outs, in_specs=[pl.BlockSpec(memory_spac...  5.72 us
    unnamed x8, local copies, waits for them, and re-layouts  0.91 us
  transfers between devices with their start and end apart: 9, of which 7 were waited for; matrix products, arithmetic and copies ran while one was open for 0% of the time, Pallas kernels for 11%

profile of v3, /device:TPU:0, one launch (start us, length us, event | category | flops | bytes accessed | tf_op | source)
XLA Modules:
  0.0 32.2 jit_solution(7151605541502037969)
XLA Ops:
  0.6 0.0 copy-start.1
  0.6 0.0 copy-start.3
  0.7 0.7 %copy-done.3 = s32[8,128]{1,0:T(8,128)S(1)} copy-done((s32[8,128]{1,0:T(8,128)S(1)}, s32[8,128]{1,0:T(8,128)}, u32[]{:S(2)}) %copy-start.3) | copy-done | bytes 4120
  1.4 0.0 copy-start.2
  1.4 0.2 copy-done.1
  1.6 0.0 copy-start
  1.6 0.3 shard_map.60
  1.8 0.5 %collective-permute-start = (bf16[336,128]{1,0:T(8,128)(2,1)S(1)}, bf16[336,128]{1,0:T(8,128)(2,1)S(1)}, u32[]{:S(2)}, u32[]{:S(2)}) collective-permute-start(bf16[336,128]{1,0:T(8,128)(2,1)S(1)} %get-tuple-element.22), channel_id=1, source_target_pairs={{0,1},{1,0},{2,3},{3,2},{4,5},{5,4},{6,7},{7,6},{8,16},{9,17},{10,... | collective-permute-start | bytes 258056 | tf_op jit(solution)/shard_map/ppermute | solution.py:343
  2.3 4.1 %collective-permute-start.1 = (bf16[336,128]{1,0:T(8,128)(2,1)S(1)}, bf16[336,128]{1,0:T(8,128)(2,1)S(1)}, u32[]{:S(2)}, u32[]{:S(2)}) collective-permute-start(bf16[336,128]{1,0:T(8,128)(2,1)S(1)} %get-tuple-element.23), channel_id=1, source_target_pairs={{0,8},{1,9},{2,10},{3,11},{4,12},{5,13},{6,14},{7,15},{8,0},{9,1},... | collective-permute-start | bytes 258056 | tf_op jit(solution)/shard_map/ppermute | solution.py:343
  6.5 0.0 copy-done.2
  6.5 0.0 copy-done
  6.5 0.3 %shard_map.61 = (bf16[128,512]{1,0:T(8,128)(2,1)S(1)}, bf16[128,64]{1,0:T(8,128)(2,1)S(1)}, bf16[128,768]{1,0:T(8,128)(2,1)S(1)}) custom-call(bf16[64,8,128]{2,1,0:T(8,128)(2,1)S(1)} %copy-done, bf16[6,64,64]{2,1,0:T(8,128)(2,1)S(1)} %copy-done.2), custom_call_target="tpu_custom_call" | custom-call | flops 1048576 | bytes 1048576 | tf_op jit(solution)/shard_map/pallas_call | solution.py:330
  6.8 0.0 collective-permute-done.second_ref
  6.8 2.1 %collective-permute-done.1.first_ref = bf16[336,128]{1,0:T(8,128)(2,1)S(1)} collective-permute-done((bf16[336,128]{1,0:T(8,128)(2,1)S(1)}, bf16[336,128]{1,0:T(8,128)(2,1)S(1)}, u32[]{:S(2)}, u32[]{:S(2)}) %collective-permute-start.1) | collective-permute-done | bytes 86048 | tf_op jit(solution)/shard_map/ppermute | solution.py:343
  8.9 0.1 shard_map.63
  9.0 0.8 %collective-permute-start.2 = (bf16[96,128]{1,0:T(8,128)(2,1)S(1)}, bf16[96,128]{1,0:T(8,128)(2,1)S(1)}, u32[]{:S(2)}, u32[]{:S(2)}) collective-permute-start(bf16[96,128]{1,0:T(8,128)(2,1)S(1)} %get-tuple-element.27), channel_id=1, source_target_pairs={{0,7},{1,2},{2,1},{3,4},{4,3},{5,6},{6,5},{7,0},{8,15},{9,10},{10,... | collective-permute-start | bytes 73736 | tf_op jit(solution)/shard_map/ppermute | solution.py:343
  9.8 0.9 %collective-permute-start.3 = (bf16[96,128]{1,0:T(8,128)(2,1)S(1)}, bf16[96,128]{1,0:T(8,128)(2,1)S(1)}, u32[]{:S(2)}, u32[]{:S(2)}) collective-permute-start(bf16[96,128]{1,0:T(8,128)(2,1)S(1)} %get-tuple-element.28), channel_id=1, source_target_pairs={{0,1},{1,0},{2,3},{3,2},{4,5},{5,4},{6,7},{7,6},{8,9},{9,8},{10,11... | collective-permute-start | bytes 73736 | tf_op jit(solution)/shard_map/ppermute | solution.py:343
  10.7 2.0 %shard_map.62 = (bf16[512,768]{1,0:T(8,128)(2,1)S(1)}, f32[3,64,128]{2,1,0:T(8,128)S(1)}, f32[432,128]{1,0:T(8,128)S(1)}, f32[24,128]{1,0:T(8,128)S(1)}) custom-call(bf16[512,128]{1,0:T(8,128)(2,1)S(1)} %get-tuple-element.21.body_ref, bf16[16,128]{1,0:T(8,128)(2,1)S(1)} %shard_map.59.mask_ref, bf16[336,128]{1,0:T(8,128)(2,1)S(1)} %collective-permute-done.second_ref, ...), custom_call_target="tpu_custom_call" | custom-call | flops 268435456 | bytes 1048576 | tf_op jit(solution)/shard_map/pallas_call | solution.py:330
  12.7 0.7 %collective-permute-done.2.second_ref = bf16[96,128]{1,0:T(8,128)(2,1)S(1)} collective-permute-done((bf16[96,128]{1,0:T(8,128)(2,1)S(1)}, bf16[96,128]{1,0:T(8,128)(2,1)S(1)}, u32[]{:S(2)}, u32[]{:S(2)}) %collective-permute-start.2) | collective-permute-done | bytes 24608 | tf_op jit(solution)/shard_map/ppermute | solution.py:343
  13.4 0.0 collective-permute-done.3.first_ref
  13.4 1.0 %shard_map.64 = (bf16[64,768]{1,0:T(8,128)(2,1)S(1)}, f32[208,128]{1,0:T(8,128)S(1)}) custom-call(f32[432,128]{1,0:T(8,128)S(1)} %get-tuple-element.25.own_ref, f32[24,128]{1,0:T(8,128)S(1)} %get-tuple-element.26.centre_ref, bf16[96,128]{1,0:T(8,128)(2,1)S(1)} %collective-permute-done.2.second_ref, bf16[96,128]{1,0:T(8,128)(2,1)S(1)} %collective-permute-done.3.first_ref, ...), custom_call_target="tpu_custom_call" | custom-call | flops 67108864 | bytes 1048576 | tf_op jit(solution)/shard_map/pallas_call | solution.py:330
  14.4 0.5 %collective-permute-start.4 = (f16[208,128]{1,0:T(8,128)(2,1)S(1)}, f16[208,128]{1,0:T(8,128)(2,1)S(1)}, u32[]{:S(2)}, u32[]{:S(2)}) collective-permute-start(f16[208,128]{1,0:T(8,128)(2,1)S(1)} %convert_element_type.36), channel_id=1, source_target_pairs={{0,3},{1,8},{2,11},{3,0},{4,13},{5,6},{6,5},{7,14},{8,1},{9,10},{1... | collective-permute-start | bytes 159752 | tf_op jit(solution)/shard_map/ppermute | solution.py:343
  14.9 1.2 %shard_map.65 = bf16[64,8,128]{2,1,0:T(8,128)(2,1)} custom-call(bf16[128,768]{1,0:T(8,128)(2,1)S(1)} %get-tuple-element.35.weight_ref, bf16[512,768]{1,0:T(8,128)(2,1)S(1)} %get-tuple-element.36.inner_ref, bf16[64,768]{1,0:T(8,128)(2,1)S(1)} %get-tuple-element.37.rim_ref), custom_call_target="tpu_custom_call" | custom-call | flops 1048576 | bytes 1048576 | tf_op jit(solution)/shard_map/pallas_call | solution.py:330
  16.1 1.9 %collective-permute-done.4 = f16[208,128]{1,0:T(8,128)(2,1)S(1)} collective-permute-done((f16[208,128]{1,0:T(8,128)(2,1)S(1)}, f16[208,128]{1,0:T(8,128)(2,1)S(1)}, u32[]{:S(2)}, u32[]{:S(2)}) %collective-permute-start.4) | collective-permute-done | bytes 53280 | tf_op jit(solution)/shard_map/ppermute | solution.py:343
  18.1 1.3 %collective-permute-start.5 = (f16[208,128]{1,0:T(8,128)(2,1)S(1)}, f16[208,128]{1,0:T(8,128)(2,1)S(1)}, u32[]{:S(2)}, u32[]{:S(2)}) collective-permute-start(f16[208,128]{1,0:T(8,128)(2,1)S(1)} %convert_element_type.39), channel_id=1, source_target_pairs={{0,9},{1,2},{2,1},{3,10},{4,7},{5,12},{6,15},{7,4},{8,11},{9,0},{1... | collective-permute-start | bytes 159752 | tf_op jit(solution)/shard_map/ppermute | solution.py:343
  19.4 2.3 %collective-permute-done.5 = f16[208,128]{1,0:T(8,128)(2,1)S(1)} collective-permute-done((f16[208,128]{1,0:T(8,128)(2,1)S(1)}, f16[208,128]{1,0:T(8,128)(2,1)S(1)}, u32[]{:S(2)}, u32[]{:S(2)}) %collective-permute-start.5) | collective-permute-done | bytes 53280 | tf_op jit(solution)/shard_map/ppermute | solution.py:343
  21.8 1.4 %collective-permute-start.6 = (f16[208,128]{1,0:T(8,128)(2,1)S(1)}, f16[208,128]{1,0:T(8,128)(2,1)S(1)}, u32[]{:S(2)}, u32[]{:S(2)}) collective-permute-start(f16[208,128]{1,0:T(8,128)(2,1)S(1)} %convert_element_type.42), channel_id=1, source_target_pairs={{0,5},{1,16},{2,19},{3,6},{4,21},{5,0},{6,3},{7,22},{8,25},{9,12},... | collective-permute-start | bytes 159752 | tf_op jit(solution)/shard_map/ppermute | solution.py:343
  23.2 2.2 %collective-permute-done.6 = f16[208,128]{1,0:T(8,128)(2,1)S(1)} collective-permute-done((f16[208,128]{1,0:T(8,128)(2,1)S(1)}, f16[208,128]{1,0:T(8,128)(2,1)S(1)}, u32[]{:S(2)}, u32[]{:S(2)}) %collective-permute-start.6) | collective-permute-done | bytes 53280 | tf_op jit(solution)/shard_map/ppermute | solution.py:343
  25.5 1.7 %collective-permute-start.7 = (f16[208,128]{1,0:T(8,128)(2,1)S(1)}, f16[208,128]{1,0:T(8,128)(2,1)S(1)}, u32[]{:S(2)}, u32[]{:S(2)}) collective-permute-start(f16[208,128]{1,0:T(8,128)(2,1)S(1)} %convert_element_type.45), channel_id=1, source_target_pairs={{0,17},{1,4},{2,7},{3,18},{4,1},{5,20},{6,23},{7,2},{8,13},{9,24},... | collective-permute-start | bytes 159752 | tf_op jit(solution)/shard_map/ppermute | solution.py:343
  27.2 2.8 %collective-permute-done.7 = f16[208,128]{1,0:T(8,128)(2,1)S(1)} collective-permute-done((f16[208,128]{1,0:T(8,128)(2,1)S(1)}, f16[208,128]{1,0:T(8,128)(2,1)S(1)}, u32[]{:S(2)}, u32[]{:S(2)}) %collective-permute-start.7) | collective-permute-done | bytes 53280 | tf_op jit(solution)/shard_map/ppermute | solution.py:343
  30.0 0.5 %collective-permute-start.8 = (f32[192,128]{1,0:T(8,128)S(1)}, f32[192,128]{1,0:T(8,128)S(1)}, u32[]{:S(2)}, u32[]{:S(2)}) collective-permute-start(f32[192,128]{1,0:T(8,128)S(1)} %shard_map.69.mine_ref), channel_id=1, source_target_pairs={{0,1},{1,0},{2,3},{3,2},{4,5},{5,4},{6,7},{7,6},{8,9},{9,8},{10,11... | collective-permute-start | bytes 294920 | tf_op jit(solution)/shard_map/ppermute | solution.py:343
  30.5 0.9 %collective-permute-done.8.other_ref = f32[192,128]{1,0:T(8,128)S(1)} collective-permute-done((f32[192,128]{1,0:T(8,128)S(1)}, f32[192,128]{1,0:T(8,128)S(1)}, u32[]{:S(2)}, u32[]{:S(2)}) %collective-permute-start.8) | collective-permute-done | bytes 98336 | tf_op jit(solution)/shard_map/ppermute | solution.py:343
  31.4 0.8 %shard_map.70 = f32[6,64,64]{2,1,0:T(8,128)} custom-call(f32[192,128]{1,0:T(8,128)S(1)} %shard_map.69.mine_ref, f32[192,128]{1,0:T(8,128)S(1)} %collective-permute-done.8.other_ref), custom_call_target="tpu_custom_call" | custom-call | flops 65536 | bytes 1048576 | tf_op jit(solution)/shard_map/pallas_call | solution.py:330
  (17 shorter events, 0.2 us)
Async XLA Ops:
  0.6 0.9 %copy-start.1 = (bf16[64,8,128]{2,1,0:T(8,128)(2,1)S(1)}, bf16[64,8,128]{2,1,0:T(8,128)(2,1)}, u32[]{:S(2)}) copy-start(bf16[64,8,128]{2,1,0:T(8,128)(2,1)} %cot_ref.1) | copy-start | bytes 393220
  0.6 0.7 %copy-start.3 = (s32[8,128]{1,0:T(8,128)S(1)}, s32[8,128]{1,0:T(8,128)}, u32[]{:S(2)}) copy-start(s32[8,128]{1,0:T(8,128)} %mask_ref.1) | copy-start | bytes 12292
  1.4 5.1 %copy-start.2 = (bf16[6,64,64]{2,1,0:T(8,128)(2,1)S(1)}, bf16[6,64,64]{2,1,0:T(8,128)(2,1)}, u32[]{:S(2)}) copy-start(bf16[6,64,64]{2,1,0:T(8,128)(2,1)} %weight_ref.1) | copy-start | bytes 147460
  1.6 4.9 %copy-start = (bf16[64,8,128]{2,1,0:T(8,128)(2,1)S(1)}, bf16[64,8,128]{2,1,0:T(8,128)(2,1)}, u32[]{:S(2)}) copy-start(bf16[64,8,128]{2,1,0:T(8,128)(2,1)} %feature_ref.1) | copy-start | bytes 393220
  1.8 5.0 %collective-permute-start = (bf16[336,128]{1,0:T(8,128)(2,1)S(1)}, bf16[336,128]{1,0:T(8,128)(2,1)S(1)}, u32[]{:S(2)}, u32[]{:S(2)}) collective-permute-start(bf16[336,128]{1,0:T(8,128)(2,1)S(1)} %get-tuple-element.22), channel_id=1, source_target_pairs={{0,1},{1,0},{2,3},{3,2},{4,5},{5,4},{6,7},{7,6},{8,16},{9,17},{10,... | collective-permute-start | bytes 258056 | tf_op jit(solution)/shard_map/ppermute | solution.py:343
  2.3 6.6 %collective-permute-start.1 = (bf16[336,128]{1,0:T(8,128)(2,1)S(1)}, bf16[336,128]{1,0:T(8,128)(2,1)S(1)}, u32[]{:S(2)}, u32[]{:S(2)}) collective-permute-start(bf16[336,128]{1,0:T(8,128)(2,1)S(1)} %get-tuple-element.23), channel_id=1, source_target_pairs={{0,8},{1,9},{2,10},{3,11},{4,12},{5,13},{6,14},{7,15},{8,0},{9,1},... | collective-permute-start | bytes 258056 | tf_op jit(solution)/shard_map/ppermute | solution.py:343
  9.0 4.4 %collective-permute-start.2 = (bf16[96,128]{1,0:T(8,128)(2,1)S(1)}, bf16[96,128]{1,0:T(8,128)(2,1)S(1)}, u32[]{:S(2)}, u32[]{:S(2)}) collective-permute-start(bf16[96,128]{1,0:T(8,128)(2,1)S(1)} %get-tuple-element.27), channel_id=1, source_target_pairs={{0,7},{1,2},{2,1},{3,4},{4,3},{5,6},{6,5},{7,0},{8,15},{9,10},{10,... | collective-permute-start | bytes 73736 | tf_op jit(solution)/shard_map/ppermute | solution.py:343
  9.8 3.6 %collective-permute-start.3 = (bf16[96,128]{1,0:T(8,128)(2,1)S(1)}, bf16[96,128]{1,0:T(8,128)(2,1)S(1)}, u32[]{:S(2)}, u32[]{:S(2)}) collective-permute-start(bf16[96,128]{1,0:T(8,128)(2,1)S(1)} %get-tuple-element.28), channel_id=1, source_target_pairs={{0,1},{1,0},{2,3},{3,2},{4,5},{5,4},{6,7},{7,6},{8,9},{9,8},{10,11... | collective-permute-start | bytes 73736 | tf_op jit(solution)/shard_map/ppermute | solution.py:343
  14.4 3.6 %collective-permute-start.4 = (f16[208,128]{1,0:T(8,128)(2,1)S(1)}, f16[208,128]{1,0:T(8,128)(2,1)S(1)}, u32[]{:S(2)}, u32[]{:S(2)}) collective-permute-start(f16[208,128]{1,0:T(8,128)(2,1)S(1)} %convert_element_type.36), channel_id=1, source_target_pairs={{0,3},{1,8},{2,11},{3,0},{4,13},{5,6},{6,5},{7,14},{8,1},{9,10},{1... | collective-permute-start | bytes 159752 | tf_op jit(solution)/shard_map/ppermute | solution.py:343
  18.1 3.6 %collective-permute-start.5 = (f16[208,128]{1,0:T(8,128)(2,1)S(1)}, f16[208,128]{1,0:T(8,128)(2,1)S(1)}, u32[]{:S(2)}, u32[]{:S(2)}) collective-permute-start(f16[208,128]{1,0:T(8,128)(2,1)S(1)} %convert_element_type.39), channel_id=1, source_target_pairs={{0,9},{1,2},{2,1},{3,10},{4,7},{5,12},{6,15},{7,4},{8,11},{9,0},{1... | collective-permute-start | bytes 159752 | tf_op jit(solution)/shard_map/ppermute | solution.py:343
  21.8 3.6 %collective-permute-start.6 = (f16[208,128]{1,0:T(8,128)(2,1)S(1)}, f16[208,128]{1,0:T(8,128)(2,1)S(1)}, u32[]{:S(2)}, u32[]{:S(2)}) collective-permute-start(f16[208,128]{1,0:T(8,128)(2,1)S(1)} %convert_element_type.42), channel_id=1, source_target_pairs={{0,5},{1,16},{2,19},{3,6},{4,21},{5,0},{6,3},{7,22},{8,25},{9,12},... | collective-permute-start | bytes 159752 | tf_op jit(solution)/shard_map/ppermute | solution.py:343
  25.5 4.5 %collective-permute-start.7 = (f16[208,128]{1,0:T(8,128)(2,1)S(1)}, f16[208,128]{1,0:T(8,128)(2,1)S(1)}, u32[]{:S(2)}, u32[]{:S(2)}) collective-permute-start(f16[208,128]{1,0:T(8,128)(2,1)S(1)} %convert_element_type.45), channel_id=1, source_target_pairs={{0,17},{1,4},{2,7},{3,18},{4,1},{5,20},{6,23},{7,2},{8,13},{9,24},... | collective-permute-start | bytes 159752 | tf_op jit(solution)/shard_map/ppermute | solution.py:343
  30.0 1.4 %collective-permute-start.8 = (f32[192,128]{1,0:T(8,128)S(1)}, f32[192,128]{1,0:T(8,128)S(1)}, u32[]{:S(2)}, u32[]{:S(2)}) collective-permute-start(f32[192,128]{1,0:T(8,128)S(1)} %shard_map.69.mine_ref), channel_id=1, source_target_pairs={{0,1},{1,0},{2,3},{3,2},{4,5},{5,4},{6,7},{7,6},{8,9},{9,8},{10,11... | collective-permute-start | bytes 294920 | tf_op jit(solution)/shard_map/ppermute | solution.py:343

commit v4 on v3

--- a/solution.py
+++ b/solution.py
@@ -149,7 +149,7 @@
         scale_ref[q * tall : (q + 1) * tall, :] = picked
 
 
-def next_term(k, tall, scale_ref, newer_ref, older_ref, visit):
+def next_term(k, tall, scale_ref, newer_ref, older_ref, shift_ref, visit):
     total = scale_ref.shape[0] // tall
 
     def at(q):
@@ -161,8 +161,11 @@
     above, here = weighted(k - 1), weighted(k)
     for q in range(k, total - k):
         below = weighted(q + 1)
-        column = above + here + below
-        nearby = column + pltpu.roll(column, 1, 0) + pltpu.roll(column, tall - 1, 0) - here
+        beside = above + below
+        column = beside + here
+        begin = q * (tall + 2 * RIM) + RIM
+        shift_ref[begin : begin + tall, :] = column
+        nearby = beside + shift_ref[begin - 1 : begin - 1 + tall, :] + shift_ref[begin + 1 : begin + 1 + tall, :]
         fresh = scale_ref[at(q), :] * nearby
         fresh = 0.5 * fresh if k == 1 else fresh - older_ref[at(q), :]
         older_ref[at(q), :] = fresh
@@ -180,7 +183,7 @@
 
 
 def interior_kernel(
-    orders, body_ref, mask_ref, second_ref, first_ref, feature_ref, terms_ref, sums_ref, own_ref, centre_ref, even_ref, odd_ref, scale_ref
+    orders, body_ref, mask_ref, second_ref, first_ref, feature_ref, terms_ref, sums_ref, own_ref, centre_ref, even_ref, odd_ref, scale_ref, shift_ref
 ):
     rows, cols = mask_ref.shape[0] // 2, mask_ref.shape[1]
     half, halo, lanes = cols // 2, orders - 1, body_ref.shape[1]
@@ -205,6 +208,7 @@
         own_ref[at + RIM : at + 2 * RIM, :] = jnp.where(low, middle[:RIM], middle[tail + RIM :])
         own_ref[at + 2 * RIM : at + 3 * RIM, :] = jnp.where(low, middle[RIM : 2 * RIM], 0.0)
     terms_ref[:, :lanes] = body_ref[...]
+    shift_ref[...] = jnp.zeros_like(shift_ref)
     newer, older = odd_ref, even_ref
     for k in range(1, orders):
         def keep(q, fresh):
@@ -216,7 +220,7 @@
                 kept = jnp.concatenate([first, fresh[2 * RIM : half], last], axis=0)
                 terms_ref[r * half : (r + 1) * half, columns] = kept.astype(BF16)
 
-        next_term(k, tall, scale_ref, newer, older, keep)
+        next_term(k, tall, scale_ref, newer, older, shift_ref, keep)
         newer, older = older, newer
         if k % 2:
             pair = slice((k - 1) * lanes, (k + 1) * lanes)
@@ -248,7 +252,7 @@
 
 def edge_kernel(
     orders, own_ref, centre_ref, second_ref, first_ref, rim_ref, sums_ref,
-    terms_ref, message_ref, even_ref, odd_ref, scale_ref, wide_ref,
+    terms_ref, message_ref, even_ref, odd_ref, scale_ref, wide_ref, shift_ref,
 ):
     rows, cols = centre_ref.shape[0] // 3, centre_ref.shape[1]
     halo, lanes, quarter = orders - 1, own_ref.shape[1], cols // 4
@@ -273,6 +277,7 @@
 
     wide_ref[:, :lanes] = jnp.zeros((rows * RIM, lanes), F32)
     blocks = []
+    shift_ref[...] = jnp.zeros_like(shift_ref)
     newer, older = odd_ref, even_ref
     for k in range(1, orders):
         def keep(q, fresh):
@@ -280,7 +285,7 @@
             if 0 <= r < rows:
                 wide_ref[r * RIM : (r + 1) * RIM, k * lanes : (k + 1) * lanes] = fresh[RIM : 2 * RIM]
 
-        next_term(k, tall, scale_ref, newer, older, keep)
+        next_term(k, tall, scale_ref, newer, older, shift_ref, keep)
         newer, older = older, newer
         if k % 2:
             pair = slice((k - 1) * lanes, (k + 1) * lanes)
@@ -421,11 +426,11 @@
             terms, shape((orders // 2, channels, lanes), F32), shape((total * 3 * RIM, lanes), F32),
             shape((3 * rows, cols), F32),
         ],
-        [buffer, buffer, buffer], 1 << 28, cot_body, mask16, second, first, features,
+        [buffer, buffer, buffer, pltpu.VMEM((total * (tall + 2 * RIM), lanes), F32)], 1 << 28, cot_body, mask16, second, first, features,
     )
     outer, message = call(
         functools.partial(edge_kernel, orders), [rim_terms, shape((orders // 2 * channels + NOTES, lanes), F32)],
-        [small, small, small, pltpu.VMEM(rim_terms.shape, F32)], 1 << 26,
+        [small, small, small, pltpu.VMEM(rim_terms.shape, F32), pltpu.VMEM((total * 5 * RIM, lanes), F32)], 1 << 26,
         own, centre, west_second, west_first, rims, sums,
     )
     mix = functools.partial(

time: 32.4 us -> 32.4 us (level)
  waiting for transfers between devices: 12.9 us -> 13.9 us
  starting transfers between devices: 11.8 us -> 11 us
    ppermute x9, waiting for transfers between devices: 12.9 us -> 13.9 us  [swap(): return lax.ppermute(x, ('row', 'col'), [(i, partner(i)) for i in places])]
    ppermute x9, starting transfers between devices: 11.8 us -> 11 us  [swap(): return lax.ppermute(x, ('row', 'col'), [(i, partner(i)) for i in places])]
  transfers between devices with their start and end apart: 9 -> 9, of which waited for: 7 -> 7; matrix products, arithmetic and copies ran while one was open for 0% -> 0% of each run, Pallas kernels for 11% -> 10%
where the time goes in v4:
time: 32.4 us; the launch traced here: 32.2 us
  waiting for transfers between devices  13.9 us (43%)
  starting transfers between devices  11 us (34%)
  Pallas kernels  5.48 us (17%)
  local copies, waits for them, and re-layouts  0.91 us (3%)
  between operations  0.78 us (2%)
    ppermute x9, waiting for transfers between devices, swap(): return lax.ppermute(x, ('row', 'col'), [(i, partner(i)) for i in places])  13.9 us
    ppermute x9, starting transfers between devices, swap(): return lax.ppermute(x, ('row', 'col'), [(i, partner(i)) for i in places])  11 us
    pallas_call x12, Pallas kernels, call(): pl.pallas_call(kernel, out_shape=outs, in_specs=[pl.BlockSpec(memory_spac...  5.48 us
    unnamed x8, local copies, waits for them, and re-layouts  0.91 us
  transfers between devices with their start and end apart: 9, of which 7 were waited for; matrix products, arithmetic and copies ran while one was open for 0% of the time, Pallas kernels for 10%

profile of v4, /device:TPU:0, one launch (start us, length us, event | category | flops | bytes accessed | tf_op | source)
XLA Modules:
  0.0 32.2 jit_solution(11277875857221791161)
XLA Ops:
  0.6 0.0 copy-start.1
  0.6 0.0 copy-start.3
  0.7 0.7 %copy-done.3 = s32[8,128]{1,0:T(8,128)S(1)} copy-done((s32[8,128]{1,0:T(8,128)S(1)}, s32[8,128]{1,0:T(8,128)}, u32[]{:S(2)}) %copy-start.3) | copy-done | bytes 4120
  1.4 0.0 copy-start.2
  1.4 0.2 copy-done.1
  1.6 0.0 copy-start
  1.6 0.3 shard_map.60
  1.8 0.5 %collective-permute-start = (bf16[336,128]{1,0:T(8,128)(2,1)S(1)}, bf16[336,128]{1,0:T(8,128)(2,1)S(1)}, u32[]{:S(2)}, u32[]{:S(2)}) collective-permute-start(bf16[336,128]{1,0:T(8,128)(2,1)S(1)} %get-tuple-element.22), channel_id=1, source_target_pairs={{0,1},{1,0},{2,3},{3,2},{4,5},{5,4},{6,7},{7,6},{8,16},{9,17},{10,... | collective-permute-start | bytes 258056 | tf_op jit(solution)/shard_map/ppermute | solution.py:348
  2.3 4.1 %collective-permute-start.1 = (bf16[336,128]{1,0:T(8,128)(2,1)S(1)}, bf16[336,128]{1,0:T(8,128)(2,1)S(1)}, u32[]{:S(2)}, u32[]{:S(2)}) collective-permute-start(bf16[336,128]{1,0:T(8,128)(2,1)S(1)} %get-tuple-element.23), channel_id=1, source_target_pairs={{0,8},{1,9},{2,10},{3,11},{4,12},{5,13},{6,14},{7,15},{8,0},{9,1},... | collective-permute-start | bytes 258056 | tf_op jit(solution)/shard_map/ppermute | solution.py:348
  6.5 0.0 copy-done.2
  6.5 0.0 copy-done
  6.5 0.3 %shard_map.61 = (bf16[128,512]{1,0:T(8,128)(2,1)S(1)}, bf16[128,64]{1,0:T(8,128)(2,1)S(1)}, bf16[128,768]{1,0:T(8,128)(2,1)S(1)}) custom-call(bf16[64,8,128]{2,1,0:T(8,128)(2,1)S(1)} %copy-done, bf16[6,64,64]{2,1,0:T(8,128)(2,1)S(1)} %copy-done.2), custom_call_target="tpu_custom_call" | custom-call | flops 1048576 | bytes 1048576 | tf_op jit(solution)/shard_map/pallas_call | solution.py:335
  6.8 0.0 collective-permute-done.second_ref
  6.8 2.1 %collective-permute-done.1.first_ref = bf16[336,128]{1,0:T(8,128)(2,1)S(1)} collective-permute-done((bf16[336,128]{1,0:T(8,128)(2,1)S(1)}, bf16[336,128]{1,0:T(8,128)(2,1)S(1)}, u32[]{:S(2)}, u32[]{:S(2)}) %collective-permute-start.1) | collective-permute-done | bytes 86048 | tf_op jit(solution)/shard_map/ppermute | solution.py:348
  8.9 0.1 shard_map.63
  9.0 0.8 %collective-permute-start.2 = (bf16[96,128]{1,0:T(8,128)(2,1)S(1)}, bf16[96,128]{1,0:T(8,128)(2,1)S(1)}, u32[]{:S(2)}, u32[]{:S(2)}) collective-permute-start(bf16[96,128]{1,0:T(8,128)(2,1)S(1)} %get-tuple-element.27), channel_id=1, source_target_pairs={{0,7},{1,2},{2,1},{3,4},{4,3},{5,6},{6,5},{7,0},{8,15},{9,10},{10,... | collective-permute-start | bytes 73736 | tf_op jit(solution)/shard_map/ppermute | solution.py:348
  9.8 0.9 %collective-permute-start.3 = (bf16[96,128]{1,0:T(8,128)(2,1)S(1)}, bf16[96,128]{1,0:T(8,128)(2,1)S(1)}, u32[]{:S(2)}, u32[]{:S(2)}) collective-permute-start(bf16[96,128]{1,0:T(8,128)(2,1)S(1)} %get-tuple-element.28), channel_id=1, source_target_pairs={{0,1},{1,0},{2,3},{3,2},{4,5},{5,4},{6,7},{7,6},{8,9},{9,8},{10,11... | collective-permute-start | bytes 73736 | tf_op jit(solution)/shard_map/ppermute | solution.py:348
  10.7 1.8 %shard_map.62 = (bf16[512,768]{1,0:T(8,128)(2,1)S(1)}, f32[3,64,128]{2,1,0:T(8,128)S(1)}, f32[432,128]{1,0:T(8,128)S(1)}, f32[24,128]{1,0:T(8,128)S(1)}) custom-call(bf16[512,128]{1,0:T(8,128)(2,1)S(1)} %get-tuple-element.21.body_ref, bf16[16,128]{1,0:T(8,128)(2,1)S(1)} %shard_map.59.mask_ref, bf16[336,128]{1,0:T(8,128)(2,1)S(1)} %collective-permute-done.second_ref, ...), custom_call_target="tpu_custom_call" | custom-call | flops 268435456 | bytes 1048576 | tf_op jit(solution)/shard_map/pallas_call | solution.py:335
  12.5 0.9 %collective-permute-done.2.second_ref = bf16[96,128]{1,0:T(8,128)(2,1)S(1)} collective-permute-done((bf16[96,128]{1,0:T(8,128)(2,1)S(1)}, bf16[96,128]{1,0:T(8,128)(2,1)S(1)}, u32[]{:S(2)}, u32[]{:S(2)}) %collective-permute-start.2) | collective-permute-done | bytes 24608 | tf_op jit(solution)/shard_map/ppermute | solution.py:348
  13.4 0.0 collective-permute-done.3.first_ref
  13.4 0.9 %shard_map.64 = (bf16[64,768]{1,0:T(8,128)(2,1)S(1)}, f32[208,128]{1,0:T(8,128)S(1)}) custom-call(f32[432,128]{1,0:T(8,128)S(1)} %get-tuple-element.25.own_ref, f32[24,128]{1,0:T(8,128)S(1)} %get-tuple-element.26.centre_ref, bf16[96,128]{1,0:T(8,128)(2,1)S(1)} %collective-permute-done.2.second_ref, bf16[96,128]{1,0:T(8,128)(2,1)S(1)} %collective-permute-done.3.first_ref, ...), custom_call_target="tpu_custom_call" | custom-call | flops 67108864 | bytes 1048576 | tf_op jit(solution)/shard_map/pallas_call | solution.py:335
  14.4 0.3 collective-permute-start.4
  14.7 1.2 %shard_map.65 = bf16[64,8,128]{2,1,0:T(8,128)(2,1)} custom-call(bf16[128,768]{1,0:T(8,128)(2,1)S(1)} %get-tuple-element.35.weight_ref, bf16[512,768]{1,0:T(8,128)(2,1)S(1)} %get-tuple-element.36.inner_ref, bf16[64,768]{1,0:T(8,128)(2,1)S(1)} %get-tuple-element.37.rim_ref), custom_call_target="tpu_custom_call" | custom-call | flops 1048576 | bytes 1048576 | tf_op jit(solution)/shard_map/pallas_call | solution.py:335
  15.9 2.1 %collective-permute-done.4 = f16[208,128]{1,0:T(8,128)(2,1)S(1)} collective-permute-done((f16[208,128]{1,0:T(8,128)(2,1)S(1)}, f16[208,128]{1,0:T(8,128)(2,1)S(1)}, u32[]{:S(2)}, u32[]{:S(2)}) %collective-permute-start.4) | collective-permute-done | bytes 53280 | tf_op jit(solution)/shard_map/ppermute | solution.py:348
  18.1 0.8 %collective-permute-start.5 = (f16[208,128]{1,0:T(8,128)(2,1)S(1)}, f16[208,128]{1,0:T(8,128)(2,1)S(1)}, u32[]{:S(2)}, u32[]{:S(2)}) collective-permute-start(f16[208,128]{1,0:T(8,128)(2,1)S(1)} %convert_element_type.39), channel_id=1, source_target_pairs={{0,9},{1,2},{2,1},{3,10},{4,7},{5,12},{6,15},{7,4},{8,11},{9,0},{1... | collective-permute-start | bytes 159752 | tf_op jit(solution)/shard_map/ppermute | solution.py:348
  18.9 2.8 %collective-permute-done.5 = f16[208,128]{1,0:T(8,128)(2,1)S(1)} collective-permute-done((f16[208,128]{1,0:T(8,128)(2,1)S(1)}, f16[208,128]{1,0:T(8,128)(2,1)S(1)}, u32[]{:S(2)}, u32[]{:S(2)}) %collective-permute-start.5) | collective-permute-done | bytes 53280 | tf_op jit(solution)/shard_map/ppermute | solution.py:348
  21.8 1.4 %collective-permute-start.6 = (f16[208,128]{1,0:T(8,128)(2,1)S(1)}, f16[208,128]{1,0:T(8,128)(2,1)S(1)}, u32[]{:S(2)}, u32[]{:S(2)}) collective-permute-start(f16[208,128]{1,0:T(8,128)(2,1)S(1)} %convert_element_type.42), channel_id=1, source_target_pairs={{0,5},{1,16},{2,19},{3,6},{4,21},{5,0},{6,3},{7,22},{8,25},{9,12},... | collective-permute-start | bytes 159752 | tf_op jit(solution)/shard_map/ppermute | solution.py:348
  23.2 2.2 %collective-permute-done.6 = f16[208,128]{1,0:T(8,128)(2,1)S(1)} collective-permute-done((f16[208,128]{1,0:T(8,128)(2,1)S(1)}, f16[208,128]{1,0:T(8,128)(2,1)S(1)}, u32[]{:S(2)}, u32[]{:S(2)}) %collective-permute-start.6) | collective-permute-done | bytes 53280 | tf_op jit(solution)/shard_map/ppermute | solution.py:348
  25.4 1.7 %collective-permute-start.7 = (f16[208,128]{1,0:T(8,128)(2,1)S(1)}, f16[208,128]{1,0:T(8,128)(2,1)S(1)}, u32[]{:S(2)}, u32[]{:S(2)}) collective-permute-start(f16[208,128]{1,0:T(8,128)(2,1)S(1)} %convert_element_type.45), channel_id=1, source_target_pairs={{0,17},{1,4},{2,7},{3,18},{4,1},{5,20},{6,23},{7,2},{8,13},{9,24},... | collective-permute-start | bytes 159752 | tf_op jit(solution)/shard_map/ppermute | solution.py:348
  27.2 2.8 %collective-permute-done.7 = f16[208,128]{1,0:T(8,128)(2,1)S(1)} collective-permute-done((f16[208,128]{1,0:T(8,128)(2,1)S(1)}, f16[208,128]{1,0:T(8,128)(2,1)S(1)}, u32[]{:S(2)}, u32[]{:S(2)}) %collective-permute-start.7) | collective-permute-done | bytes 53280 | tf_op jit(solution)/shard_map/ppermute | solution.py:348
  30.0 0.5 %collective-permute-start.8 = (f32[192,128]{1,0:T(8,128)S(1)}, f32[192,128]{1,0:T(8,128)S(1)}, u32[]{:S(2)}, u32[]{:S(2)}) collective-permute-start(f32[192,128]{1,0:T(8,128)S(1)} %shard_map.69.mine_ref), channel_id=1, source_target_pairs={{0,1},{1,0},{2,3},{3,2},{4,5},{5,4},{6,7},{7,6},{8,9},{9,8},{10,11... | collective-permute-start | bytes 294920 | tf_op jit(solution)/shard_map/ppermute | solution.py:348
  30.5 0.9 %collective-permute-done.8.other_ref = f32[192,128]{1,0:T(8,128)S(1)} collective-permute-done((f32[192,128]{1,0:T(8,128)S(1)}, f32[192,128]{1,0:T(8,128)S(1)}, u32[]{:S(2)}, u32[]{:S(2)}) %collective-permute-start.8) | collective-permute-done | bytes 98336 | tf_op jit(solution)/shard_map/ppermute | solution.py:348
  31.4 0.8 %shard_map.70 = f32[6,64,64]{2,1,0:T(8,128)} custom-call(f32[192,128]{1,0:T(8,128)S(1)} %shard_map.69.mine_ref, f32[192,128]{1,0:T(8,128)S(1)} %collective-permute-done.8.other_ref), custom_call_target="tpu_custom_call" | custom-call | flops 65536 | bytes 1048576 | tf_op jit(solution)/shard_map/pallas_call | solution.py:335
  (17 shorter events, 0.2 us)
Async XLA Ops:
  0.6 0.9 %copy-start.1 = (bf16[64,8,128]{2,1,0:T(8,128)(2,1)S(1)}, bf16[64,8,128]{2,1,0:T(8,128)(2,1)}, u32[]{:S(2)}) copy-start(bf16[64,8,128]{2,1,0:T(8,128)(2,1)} %cot_ref.1) | copy-start | bytes 393220
  0.6 0.7 %copy-start.3 = (s32[8,128]{1,0:T(8,128)S(1)}, s32[8,128]{1,0:T(8,128)}, u32[]{:S(2)}) copy-start(s32[8,128]{1,0:T(8,128)} %mask_ref.1) | copy-start | bytes 12292
  1.4 5.1 %copy-start.2 = (bf16[6,64,64]{2,1,0:T(8,128)(2,1)S(1)}, bf16[6,64,64]{2,1,0:T(8,128)(2,1)}, u32[]{:S(2)}) copy-start(bf16[6,64,64]{2,1,0:T(8,128)(2,1)} %weight_ref.1) | copy-start | bytes 147460
  1.6 4.9 %copy-start = (bf16[64,8,128]{2,1,0:T(8,128)(2,1)S(1)}, bf16[64,8,128]{2,1,0:T(8,128)(2,1)}, u32[]{:S(2)}) copy-start(bf16[64,8,128]{2,1,0:T(8,128)(2,1)} %feature_ref.1) | copy-start | bytes 393220
  1.8 5.0 %collective-permute-start = (bf16[336,128]{1,0:T(8,128)(2,1)S(1)}, bf16[336,128]{1,0:T(8,128)(2,1)S(1)}, u32[]{:S(2)}, u32[]{:S(2)}) collective-permute-start(bf16[336,128]{1,0:T(8,128)(2,1)S(1)} %get-tuple-element.22), channel_id=1, source_target_pairs={{0,1},{1,0},{2,3},{3,2},{4,5},{5,4},{6,7},{7,6},{8,16},{9,17},{10,... | collective-permute-start | bytes 258056 | tf_op jit(solution)/shard_map/ppermute | solution.py:348
  2.3 6.6 %collective-permute-start.1 = (bf16[336,128]{1,0:T(8,128)(2,1)S(1)}, bf16[336,128]{1,0:T(8,128)(2,1)S(1)}, u32[]{:S(2)}, u32[]{:S(2)}) collective-permute-start(bf16[336,128]{1,0:T(8,128)(2,1)S(1)} %get-tuple-element.23), channel_id=1, source_target_pairs={{0,8},{1,9},{2,10},{3,11},{4,12},{5,13},{6,14},{7,15},{8,0},{9,1},... | collective-permute-start | bytes 258056 | tf_op jit(solution)/shard_map/ppermute | solution.py:348
  9.0 4.4 %collective-permute-start.2 = (bf16[96,128]{1,0:T(8,128)(2,1)S(1)}, bf16[96,128]{1,0:T(8,128)(2,1)S(1)}, u32[]{:S(2)}, u32[]{:S(2)}) collective-permute-start(bf16[96,128]{1,0:T(8,128)(2,1)S(1)} %get-tuple-element.27), channel_id=1, source_target_pairs={{0,7},{1,2},{2,1},{3,4},{4,3},{5,6},{6,5},{7,0},{8,15},{9,10},{10,... | collective-permute-start | bytes 73736 | tf_op jit(solution)/shard_map/ppermute | solution.py:348
  9.8 3.6 %collective-permute-start.3 = (bf16[96,128]{1,0:T(8,128)(2,1)S(1)}, bf16[96,128]{1,0:T(8,128)(2,1)S(1)}, u32[]{:S(2)}, u32[]{:S(2)}) collective-permute-start(bf16[96,128]{1,0:T(8,128)(2,1)S(1)} %get-tuple-element.28), channel_id=1, source_target_pairs={{0,1},{1,0},{2,3},{3,2},{4,5},{5,4},{6,7},{7,6},{8,9},{9,8},{10,11... | collective-permute-start | bytes 73736 | tf_op jit(solution)/shard_map/ppermute | solution.py:348
  14.4 3.6 %collective-permute-start.4 = (f16[208,128]{1,0:T(8,128)(2,1)S(1)}, f16[208,128]{1,0:T(8,128)(2,1)S(1)}, u32[]{:S(2)}, u32[]{:S(2)}) collective-permute-start(f16[208,128]{1,0:T(8,128)(2,1)S(1)} %convert_element_type.36), channel_id=1, source_target_pairs={{0,3},{1,8},{2,11},{3,0},{4,13},{5,6},{6,5},{7,14},{8,1},{9,10},{1... | collective-permute-start | bytes 159752 | tf_op jit(solution)/shard_map/ppermute | solution.py:348
  18.1 3.6 %collective-permute-start.5 = (f16[208,128]{1,0:T(8,128)(2,1)S(1)}, f16[208,128]{1,0:T(8,128)(2,1)S(1)}, u32[]{:S(2)}, u32[]{:S(2)}) collective-permute-start(f16[208,128]{1,0:T(8,128)(2,1)S(1)} %convert_element_type.39), channel_id=1, source_target_pairs={{0,9},{1,2},{2,1},{3,10},{4,7},{5,12},{6,15},{7,4},{8,11},{9,0},{1... | collective-permute-start | bytes 159752 | tf_op jit(solution)/shard_map/ppermute | solution.py:348
  21.8 3.6 %collective-permute-start.6 = (f16[208,128]{1,0:T(8,128)(2,1)S(1)}, f16[208,128]{1,0:T(8,128)(2,1)S(1)}, u32[]{:S(2)}, u32[]{:S(2)}) collective-permute-start(f16[208,128]{1,0:T(8,128)(2,1)S(1)} %convert_element_type.42), channel_id=1, source_target_pairs={{0,5},{1,16},{2,19},{3,6},{4,21},{5,0},{6,3},{7,22},{8,25},{9,12},... | collective-permute-start | bytes 159752 | tf_op jit(solution)/shard_map/ppermute | solution.py:348
  25.4 4.5 %collective-permute-start.7 = (f16[208,128]{1,0:T(8,128)(2,1)S(1)}, f16[208,128]{1,0:T(8,128)(2,1)S(1)}, u32[]{:S(2)}, u32[]{:S(2)}) collective-permute-start(f16[208,128]{1,0:T(8,128)(2,1)S(1)} %convert_element_type.45), channel_id=1, source_target_pairs={{0,17},{1,4},{2,7},{3,18},{4,1},{5,20},{6,23},{7,2},{8,13},{9,24},... | collective-permute-start | bytes 159752 | tf_op jit(solution)/shard_map/ppermute | solution.py:348
  30.0 1.4 %collective-permute-start.8 = (f32[192,128]{1,0:T(8,128)S(1)}, f32[192,128]{1,0:T(8,128)S(1)}, u32[]{:S(2)}, u32[]{:S(2)}) collective-permute-start(f32[192,128]{1,0:T(8,128)S(1)} %shard_map.69.mine_ref), channel_id=1, source_target_pairs={{0,1},{1,0},{2,3},{3,2},{4,5},{5,4},{6,7},{7,6},{8,9},{9,8},{10,11... | collective-permute-start | bytes 294920 | tf_op jit(solution)/shard_map/ppermute | solution.py:348

commit v5 on v4

--- a/solution.py
+++ b/solution.py
@@ -373,9 +373,7 @@
     across, down = lax.axis_size("col"), lax.axis_size("row")
     beside = list(range(1, across.bit_length() - 1))
     below = list(range(across.bit_length() - 1, (across * down).bit_length() - 1))
-    turns = [(beside[n : n + 1], below[n : n + 1]) for n in range(max(len(beside), len(below)))]
-    even = [bit for a, b in turns for bit in a + b]
-    odd = [bit for a, b in turns for bit in b + a]
+    even, odd = beside + below, beside[::-1] + below[::-1]
     for n, bits in enumerate(zip(even, odd)):
         message = lax.optimization_barrier(part.astype(jnp.float16))
         received = swap(message, lambda i: i ^ (1 << bits[i.bit_count() % 2]) ^ 1)

time: 32.4 us -> 32.5 us (level)
  no operation moved by 1% of the time
where the time goes in v5:
time: 32.5 us; the launch traced here: 32.2 us
  waiting for transfers between devices  13.9 us (43%)
  starting transfers between devices  11 us (34%)
  Pallas kernels  5.48 us (17%)
  local copies, waits for them, and re-layouts  0.91 us (3%)
  between operations  0.78 us (2%)
    ppermute x9, waiting for transfers between devices, swap(): return lax.ppermute(x, ('row', 'col'), [(i, partner(i)) for i in places])  13.9 us
    ppermute x9, starting transfers between devices, swap(): return lax.ppermute(x, ('row', 'col'), [(i, partner(i)) for i in places])  11 us
    pallas_call x12, Pallas kernels, call(): pl.pallas_call(kernel, out_shape=outs, in_specs=[pl.BlockSpec(memory_spac...  5.48 us
    unnamed x8, local copies, waits for them, and re-layouts  0.91 us
  transfers between devices with their start and end apart: 9, of which 7 were waited for; matrix products, arithmetic and copies ran while one was open for 0% of the time, Pallas kernels for 10%

profile of v5, /device:TPU:0, one launch (start us, length us, event | category | flops | bytes accessed | tf_op | source)
XLA Modules:
  0.0 32.2 jit_solution(14224483345648800723)
XLA Ops:
  0.6 0.0 copy-start.1
  0.6 0.0 copy-start.3
  0.7 0.7 %copy-done.3 = s32[8,128]{1,0:T(8,128)S(1)} copy-done((s32[8,128]{1,0:T(8,128)S(1)}, s32[8,128]{1,0:T(8,128)}, u32[]{:S(2)}) %copy-start.3) | copy-done | bytes 4120
  1.4 0.0 copy-start.2
  1.4 0.2 copy-done.1
  1.6 0.0 copy-start
  1.6 0.3 shard_map.60
  1.8 0.5 %collective-permute-start = (bf16[336,128]{1,0:T(8,128)(2,1)S(1)}, bf16[336,128]{1,0:T(8,128)(2,1)S(1)}, u32[]{:S(2)}, u32[]{:S(2)}) collective-permute-start(bf16[336,128]{1,0:T(8,128)(2,1)S(1)} %get-tuple-element.22), channel_id=1, source_target_pairs={{0,1},{1,0},{2,3},{3,2},{4,5},{5,4},{6,7},{7,6},{8,16},{9,17},{10,... | collective-permute-start | bytes 258056 | tf_op jit(solution)/shard_map/ppermute | solution.py:348
  2.3 4.1 %collective-permute-start.1 = (bf16[336,128]{1,0:T(8,128)(2,1)S(1)}, bf16[336,128]{1,0:T(8,128)(2,1)S(1)}, u32[]{:S(2)}, u32[]{:S(2)}) collective-permute-start(bf16[336,128]{1,0:T(8,128)(2,1)S(1)} %get-tuple-element.23), channel_id=1, source_target_pairs={{0,8},{1,9},{2,10},{3,11},{4,12},{5,13},{6,14},{7,15},{8,0},{9,1},... | collective-permute-start | bytes 258056 | tf_op jit(solution)/shard_map/ppermute | solution.py:348
  6.5 0.0 copy-done.2
  6.5 0.0 copy-done
  6.5 0.3 %shard_map.61 = (bf16[128,512]{1,0:T(8,128)(2,1)S(1)}, bf16[128,64]{1,0:T(8,128)(2,1)S(1)}, bf16[128,768]{1,0:T(8,128)(2,1)S(1)}) custom-call(bf16[64,8,128]{2,1,0:T(8,128)(2,1)S(1)} %copy-done, bf16[6,64,64]{2,1,0:T(8,128)(2,1)S(1)} %copy-done.2), custom_call_target="tpu_custom_call" | custom-call | flops 1048576 | bytes 1048576 | tf_op jit(solution)/shard_map/pallas_call | solution.py:335
  6.8 0.0 collective-permute-done.second_ref
  6.8 2.1 %collective-permute-done.1.first_ref = bf16[336,128]{1,0:T(8,128)(2,1)S(1)} collective-permute-done((bf16[336,128]{1,0:T(8,128)(2,1)S(1)}, bf16[336,128]{1,0:T(8,128)(2,1)S(1)}, u32[]{:S(2)}, u32[]{:S(2)}) %collective-permute-start.1) | collective-permute-done | bytes 86048 | tf_op jit(solution)/shard_map/ppermute | solution.py:348
  8.9 0.1 shard_map.63
  9.0 0.8 %collective-permute-start.2 = (bf16[96,128]{1,0:T(8,128)(2,1)S(1)}, bf16[96,128]{1,0:T(8,128)(2,1)S(1)}, u32[]{:S(2)}, u32[]{:S(2)}) collective-permute-start(bf16[96,128]{1,0:T(8,128)(2,1)S(1)} %get-tuple-element.27), channel_id=1, source_target_pairs={{0,7},{1,2},{2,1},{3,4},{4,3},{5,6},{6,5},{7,0},{8,15},{9,10},{10,... | collective-permute-start | bytes 73736 | tf_op jit(solution)/shard_map/ppermute | solution.py:348
  9.8 0.9 %collective-permute-start.3 = (bf16[96,128]{1,0:T(8,128)(2,1)S(1)}, bf16[96,128]{1,0:T(8,128)(2,1)S(1)}, u32[]{:S(2)}, u32[]{:S(2)}) collective-permute-start(bf16[96,128]{1,0:T(8,128)(2,1)S(1)} %get-tuple-element.28), channel_id=1, source_target_pairs={{0,1},{1,0},{2,3},{3,2},{4,5},{5,4},{6,7},{7,6},{8,9},{9,8},{10,11... | collective-permute-start | bytes 73736 | tf_op jit(solution)/shard_map/ppermute | solution.py:348
  10.7 1.8 %shard_map.62 = (bf16[512,768]{1,0:T(8,128)(2,1)S(1)}, f32[3,64,128]{2,1,0:T(8,128)S(1)}, f32[432,128]{1,0:T(8,128)S(1)}, f32[24,128]{1,0:T(8,128)S(1)}) custom-call(bf16[512,128]{1,0:T(8,128)(2,1)S(1)} %get-tuple-element.21.body_ref, bf16[16,128]{1,0:T(8,128)(2,1)S(1)} %shard_map.59.mask_ref, bf16[336,128]{1,0:T(8,128)(2,1)S(1)} %collective-permute-done.second_ref, ...), custom_call_target="tpu_custom_call" | custom-call | flops 268435456 | bytes 1048576 | tf_op jit(solution)/shard_map/pallas_call | solution.py:335
  12.5 0.9 %collective-permute-done.2.second_ref = bf16[96,128]{1,0:T(8,128)(2,1)S(1)} collective-permute-done((bf16[96,128]{1,0:T(8,128)(2,1)S(1)}, bf16[96,128]{1,0:T(8,128)(2,1)S(1)}, u32[]{:S(2)}, u32[]{:S(2)}) %collective-permute-start.2) | collective-permute-done | bytes 24608 | tf_op jit(solution)/shard_map/ppermute | solution.py:348
  13.4 0.0 collective-permute-done.3.first_ref
  13.4 0.9 %shard_map.64 = (bf16[64,768]{1,0:T(8,128)(2,1)S(1)}, f32[208,128]{1,0:T(8,128)S(1)}) custom-call(f32[432,128]{1,0:T(8,128)S(1)} %get-tuple-element.25.own_ref, f32[24,128]{1,0:T(8,128)S(1)} %get-tuple-element.26.centre_ref, bf16[96,128]{1,0:T(8,128)(2,1)S(1)} %collective-permute-done.2.second_ref, bf16[96,128]{1,0:T(8,128)(2,1)S(1)} %collective-permute-done.3.first_ref, ...), custom_call_target="tpu_custom_call" | custom-call | flops 67108864 | bytes 1048576 | tf_op jit(solution)/shard_map/pallas_call | solution.py:335
  14.4 0.3 collective-permute-start.4
  14.7 1.2 %shard_map.65 = bf16[64,8,128]{2,1,0:T(8,128)(2,1)} custom-call(bf16[128,768]{1,0:T(8,128)(2,1)S(1)} %get-tuple-element.35.weight_ref, bf16[512,768]{1,0:T(8,128)(2,1)S(1)} %get-tuple-element.36.inner_ref, bf16[64,768]{1,0:T(8,128)(2,1)S(1)} %get-tuple-element.37.rim_ref), custom_call_target="tpu_custom_call" | custom-call | flops 1048576 | bytes 1048576 | tf_op jit(solution)/shard_map/pallas_call | solution.py:335
  15.9 2.1 %collective-permute-done.4 = f16[208,128]{1,0:T(8,128)(2,1)S(1)} collective-permute-done((f16[208,128]{1,0:T(8,128)(2,1)S(1)}, f16[208,128]{1,0:T(8,128)(2,1)S(1)}, u32[]{:S(2)}, u32[]{:S(2)}) %collective-permute-start.4) | collective-permute-done | bytes 53280 | tf_op jit(solution)/shard_map/ppermute | solution.py:348
  18.1 0.6 %collective-permute-start.5 = (f16[208,128]{1,0:T(8,128)(2,1)S(1)}, f16[208,128]{1,0:T(8,128)(2,1)S(1)}, u32[]{:S(2)}, u32[]{:S(2)}) collective-permute-start(f16[208,128]{1,0:T(8,128)(2,1)S(1)} %convert_element_type.39), channel_id=1, source_target_pairs={{0,5},{1,2},{2,1},{3,6},{4,7},{5,0},{6,3},{7,4},{8,11},{9,12},{10,... | collective-permute-start | bytes 159752 | tf_op jit(solution)/shard_map/ppermute | solution.py:348
  18.7 3.0 %collective-permute-done.5 = f16[208,128]{1,0:T(8,128)(2,1)S(1)} collective-permute-done((f16[208,128]{1,0:T(8,128)(2,1)S(1)}, f16[208,128]{1,0:T(8,128)(2,1)S(1)}, u32[]{:S(2)}, u32[]{:S(2)}) %collective-permute-start.5) | collective-permute-done | bytes 53280 | tf_op jit(solution)/shard_map/ppermute | solution.py:348
  21.8 1.7 %collective-permute-start.6 = (f16[208,128]{1,0:T(8,128)(2,1)S(1)}, f16[208,128]{1,0:T(8,128)(2,1)S(1)}, u32[]{:S(2)}, u32[]{:S(2)}) collective-permute-start(f16[208,128]{1,0:T(8,128)(2,1)S(1)} %convert_element_type.42), channel_id=1, source_target_pairs={{0,9},{1,16},{2,19},{3,10},{4,21},{5,12},{6,15},{7,22},{8,25},{9,0... | collective-permute-start | bytes 159752 | tf_op jit(solution)/shard_map/ppermute | solution.py:348
  23.5 1.9 %collective-permute-done.6 = f16[208,128]{1,0:T(8,128)(2,1)S(1)} collective-permute-done((f16[208,128]{1,0:T(8,128)(2,1)S(1)}, f16[208,128]{1,0:T(8,128)(2,1)S(1)}, u32[]{:S(2)}, u32[]{:S(2)}) %collective-permute-start.6) | collective-permute-done | bytes 53280 | tf_op jit(solution)/shard_map/ppermute | solution.py:348
  25.4 1.6 %collective-permute-start.7 = (f16[208,128]{1,0:T(8,128)(2,1)S(1)}, f16[208,128]{1,0:T(8,128)(2,1)S(1)}, u32[]{:S(2)}, u32[]{:S(2)}) collective-permute-start(f16[208,128]{1,0:T(8,128)(2,1)S(1)} %convert_element_type.45), channel_id=1, source_target_pairs={{0,17},{1,8},{2,11},{3,18},{4,13},{5,20},{6,23},{7,14},{8,1},{9,24... | collective-permute-start | bytes 159752 | tf_op jit(solution)/shard_map/ppermute | solution.py:348
  27.1 2.9 %collective-permute-done.7 = f16[208,128]{1,0:T(8,128)(2,1)S(1)} collective-permute-done((f16[208,128]{1,0:T(8,128)(2,1)S(1)}, f16[208,128]{1,0:T(8,128)(2,1)S(1)}, u32[]{:S(2)}, u32[]{:S(2)}) %collective-permute-start.7) | collective-permute-done | bytes 53280 | tf_op jit(solution)/shard_map/ppermute | solution.py:348
  30.0 0.5 %collective-permute-start.8 = (f32[192,128]{1,0:T(8,128)S(1)}, f32[192,128]{1,0:T(8,128)S(1)}, u32[]{:S(2)}, u32[]{:S(2)}) collective-permute-start(f32[192,128]{1,0:T(8,128)S(1)} %shard_map.69.mine_ref), channel_id=1, source_target_pairs={{0,1},{1,0},{2,3},{3,2},{4,5},{5,4},{6,7},{7,6},{8,9},{9,8},{10,11... | collective-permute-start | bytes 294920 | tf_op jit(solution)/shard_map/ppermute | solution.py:348
  30.5 0.9 %collective-permute-done.8.other_ref = f32[192,128]{1,0:T(8,128)S(1)} collective-permute-done((f32[192,128]{1,0:T(8,128)S(1)}, f32[192,128]{1,0:T(8,128)S(1)}, u32[]{:S(2)}, u32[]{:S(2)}) %collective-permute-start.8) | collective-permute-done | bytes 98336 | tf_op jit(solution)/shard_map/ppermute | solution.py:348
  31.4 0.8 %shard_map.70 = f32[6,64,64]{2,1,0:T(8,128)} custom-call(f32[192,128]{1,0:T(8,128)S(1)} %shard_map.69.mine_ref, f32[192,128]{1,0:T(8,128)S(1)} %collective-permute-done.8.other_ref), custom_call_target="tpu_custom_call" | custom-call | flops 65536 | bytes 1048576 | tf_op jit(solution)/shard_map/pallas_call | solution.py:335
  (17 shorter events, 0.2 us)
Async XLA Ops:
  0.6 0.9 %copy-start.1 = (bf16[64,8,128]{2,1,0:T(8,128)(2,1)S(1)}, bf16[64,8,128]{2,1,0:T(8,128)(2,1)}, u32[]{:S(2)}) copy-start(bf16[64,8,128]{2,1,0:T(8,128)(2,1)} %cot_ref.1) | copy-start | bytes 393220
  0.6 0.7 %copy-start.3 = (s32[8,128]{1,0:T(8,128)S(1)}, s32[8,128]{1,0:T(8,128)}, u32[]{:S(2)}) copy-start(s32[8,128]{1,0:T(8,128)} %mask_ref.1) | copy-start | bytes 12292
  1.4 5.1 %copy-start.2 = (bf16[6,64,64]{2,1,0:T(8,128)(2,1)S(1)}, bf16[6,64,64]{2,1,0:T(8,128)(2,1)}, u32[]{:S(2)}) copy-start(bf16[6,64,64]{2,1,0:T(8,128)(2,1)} %weight_ref.1) | copy-start | bytes 147460
  1.6 4.9 %copy-start = (bf16[64,8,128]{2,1,0:T(8,128)(2,1)S(1)}, bf16[64,8,128]{2,1,0:T(8,128)(2,1)}, u32[]{:S(2)}) copy-start(bf16[64,8,128]{2,1,0:T(8,128)(2,1)} %feature_ref.1) | copy-start | bytes 393220
  1.8 5.0 %collective-permute-start = (bf16[336,128]{1,0:T(8,128)(2,1)S(1)}, bf16[336,128]{1,0:T(8,128)(2,1)S(1)}, u32[]{:S(2)}, u32[]{:S(2)}) collective-permute-start(bf16[336,128]{1,0:T(8,128)(2,1)S(1)} %get-tuple-element.22), channel_id=1, source_target_pairs={{0,1},{1,0},{2,3},{3,2},{4,5},{5,4},{6,7},{7,6},{8,16},{9,17},{10,... | collective-permute-start | bytes 258056 | tf_op jit(solution)/shard_map/ppermute | solution.py:348
  2.3 6.6 %collective-permute-start.1 = (bf16[336,128]{1,0:T(8,128)(2,1)S(1)}, bf16[336,128]{1,0:T(8,128)(2,1)S(1)}, u32[]{:S(2)}, u32[]{:S(2)}) collective-permute-start(bf16[336,128]{1,0:T(8,128)(2,1)S(1)} %get-tuple-element.23), channel_id=1, source_target_pairs={{0,8},{1,9},{2,10},{3,11},{4,12},{5,13},{6,14},{7,15},{8,0},{9,1},... | collective-permute-start | bytes 258056 | tf_op jit(solution)/shard_map/ppermute | solution.py:348
  9.0 4.4 %collective-permute-start.2 = (bf16[96,128]{1,0:T(8,128)(2,1)S(1)}, bf16[96,128]{1,0:T(8,128)(2,1)S(1)}, u32[]{:S(2)}, u32[]{:S(2)}) collective-permute-start(bf16[96,128]{1,0:T(8,128)(2,1)S(1)} %get-tuple-element.27), channel_id=1, source_target_pairs={{0,7},{1,2},{2,1},{3,4},{4,3},{5,6},{6,5},{7,0},{8,15},{9,10},{10,... | collective-permute-start | bytes 73736 | tf_op jit(solution)/shard_map/ppermute | solution.py:348
  9.8 3.6 %collective-permute-start.3 = (bf16[96,128]{1,0:T(8,128)(2,1)S(1)}, bf16[96,128]{1,0:T(8,128)(2,1)S(1)}, u32[]{:S(2)}, u32[]{:S(2)}) collective-permute-start(bf16[96,128]{1,0:T(8,128)(2,1)S(1)} %get-tuple-element.28), channel_id=1, source_target_pairs={{0,1},{1,0},{2,3},{3,2},{4,5},{5,4},{6,7},{7,6},{8,9},{9,8},{10,11... | collective-permute-start | bytes 73736 | tf_op jit(solution)/shard_map/ppermute | solution.py:348
  14.4 3.6 %collective-permute-start.4 = (f16[208,128]{1,0:T(8,128)(2,1)S(1)}, f16[208,128]{1,0:T(8,128)(2,1)S(1)}, u32[]{:S(2)}, u32[]{:S(2)}) collective-permute-start(f16[208,128]{1,0:T(8,128)(2,1)S(1)} %convert_element_type.36), channel_id=1, source_target_pairs={{0,3},{1,4},{2,7},{3,0},{4,1},{5,6},{6,5},{7,2},{8,13},{9,10},{10,... | collective-permute-start | bytes 159752 | tf_op jit(solution)/shard_map/ppermute | solution.py:348
  18.1 3.6 %collective-permute-start.5 = (f16[208,128]{1,0:T(8,128)(2,1)S(1)}, f16[208,128]{1,0:T(8,128)(2,1)S(1)}, u32[]{:S(2)}, u32[]{:S(2)}) collective-permute-start(f16[208,128]{1,0:T(8,128)(2,1)S(1)} %convert_element_type.39), channel_id=1, source_target_pairs={{0,5},{1,2},{2,1},{3,6},{4,7},{5,0},{6,3},{7,4},{8,11},{9,12},{10,... | collective-permute-start | bytes 159752 | tf_op jit(solution)/shard_map/ppermute | solution.py:348
  21.8 3.6 %collective-permute-start.6 = (f16[208,128]{1,0:T(8,128)(2,1)S(1)}, f16[208,128]{1,0:T(8,128)(2,1)S(1)}, u32[]{:S(2)}, u32[]{:S(2)}) collective-permute-start(f16[208,128]{1,0:T(8,128)(2,1)S(1)} %convert_element_type.42), channel_id=1, source_target_pairs={{0,9},{1,16},{2,19},{3,10},{4,21},{5,12},{6,15},{7,22},{8,25},{9,0... | collective-permute-start | bytes 159752 | tf_op jit(solution)/shard_map/ppermute | solution.py:348
  25.4 4.5 %collective-permute-start.7 = (f16[208,128]{1,0:T(8,128)(2,1)S(1)}, f16[208,128]{1,0:T(8,128)(2,1)S(1)}, u32[]{:S(2)}, u32[]{:S(2)}) collective-permute-start(f16[208,128]{1,0:T(8,128)(2,1)S(1)} %convert_element_type.45), channel_id=1, source_target_pairs={{0,17},{1,8},{2,11},{3,18},{4,13},{5,20},{6,23},{7,14},{8,1},{9,24... | collective-permute-start | bytes 159752 | tf_op jit(solution)/shard_map/ppermute | solution.py:348
  30.0 1.4 %collective-permute-start.8 = (f32[192,128]{1,0:T(8,128)S(1)}, f32[192,128]{1,0:T(8,128)S(1)}, u32[]{:S(2)}, u32[]{:S(2)}) collective-permute-start(f32[192,128]{1,0:T(8,128)S(1)} %shard_map.69.mine_ref), channel_id=1, source_target_pairs={{0,1},{1,0},{2,3},{3,2},{4,5},{5,4},{6,7},{7,6},{8,9},{9,8},{10,11... | collective-permute-start | bytes 294920 | tf_op jit(solution)/shard_map/ppermute | solution.py:348

commit v6 on v4

--- a/solution.py
+++ b/solution.py
@@ -108,7 +108,7 @@
     return pltpu.roll(masks, cols // 4, 1), pltpu.roll(masks, cols - cols // 4, 1)
 
 
-def strips_kernel(halo, body_ref, mask_ref, second_ref, first_ref, to_first_ref, to_second_ref):
+def strips_kernel(halo, body_ref, mask_ref, first_ref, second_ref, to_first_ref, to_second_ref):
     rows = mask_ref.shape[0] // 2
     half = body_ref.shape[0] // rows
     total = rows + 2 * halo
@@ -183,7 +183,7 @@
 
 
 def interior_kernel(
-    orders, body_ref, mask_ref, second_ref, first_ref, feature_ref, terms_ref, sums_ref, own_ref, centre_ref, even_ref, odd_ref, scale_ref, shift_ref
+    orders, body_ref, mask_ref, first_ref, second_ref, feature_ref, terms_ref, sums_ref, own_ref, centre_ref, even_ref, odd_ref, scale_ref, shift_ref
 ):
     rows, cols = mask_ref.shape[0] // 2, mask_ref.shape[1]
     half, halo, lanes = cols // 2, orders - 1, body_ref.shape[1]
@@ -413,7 +413,7 @@
     )
     sent = shape((-(-(3 * rows + total // 2 * RIM) // 16) * 16, lanes), BF16)
     west_first, west_second = call(
-        functools.partial(strips_kernel, halo), [sent, sent], [], 1 << 16, cot_body, mask16, second, first
+        functools.partial(strips_kernel, halo), [sent, sent], [], 1 << 16, cot_body, mask16, first, second
     )
     west_first, west_second = exchange_cols(west_first, west_second)
     buffer = pltpu.VMEM((total * tall, lanes), F32)
@@ -426,7 +426,7 @@
             terms, shape((orders // 2, channels, lanes), F32), shape((total * 3 * RIM, lanes), F32),
             shape((3 * rows, cols), F32),
         ],
-        [buffer, buffer, buffer, pltpu.VMEM((total * (tall + 2 * RIM), lanes), F32)], 1 << 28, cot_body, mask16, second, first, features,
+        [buffer, buffer, buffer, pltpu.VMEM((total * (tall + 2 * RIM), lanes), F32)], 1 << 28, cot_body, mask16, first, second, features,
     )
     outer, message = call(
         functools.partial(edge_kernel, orders), [rim_terms, shape((orders // 2 * channels + NOTES, lanes), F32)],

time: 32.4 us -> 33.1 us (1.022)
  starting transfers between devices: 11 us -> 15.1 us
  waiting for transfers between devices: 13.9 us -> 10.5 us
    ppermute x9, starting transfers between devices: 11 us -> 15.1 us  [swap(): return lax.ppermute(x, ('row', 'col'), [(i, partner(i)) for i in places])]
    ppermute x9, waiting for transfers between devices: 13.9 us -> 10.5 us  [swap(): return lax.ppermute(x, ('row', 'col'), [(i, partner(i)) for i in places])]
where the time goes in v6:
time: 33.1 us; the launch traced here: 32.9 us
  starting transfers between devices  15.1 us (46%)
  waiting for transfers between devices  10.5 us (32%)
  Pallas kernels  5.48 us (17%)
  local copies, waits for them, and re-layouts  0.91 us (3%)
  between operations  0.78 us (2%)
    ppermute x9, starting transfers between devices, swap(): return lax.ppermute(x, ('row', 'col'), [(i, partner(i)) for i in places])  15.1 us
    ppermute x9, waiting for transfers between devices, swap(): return lax.ppermute(x, ('row', 'col'), [(i, partner(i)) for i in places])  10.5 us
    pallas_call x12, Pallas kernels, call(): pl.pallas_call(kernel, out_shape=outs, in_specs=[pl.BlockSpec(memory_spac...  5.48 us
    unnamed x8, local copies, waits for them, and re-layouts  0.91 us
  transfers between devices with their start and end apart: 9, of which 7 were waited for; matrix products, arithmetic and copies ran while one was open for 0% of the time, Pallas kernels for 10%

profile of v6, /device:TPU:0, one launch (start us, length us, event | category | flops | bytes accessed | tf_op | source)
XLA Modules:
  0.0 32.9 jit_solution(7437351413208508043)
XLA Ops:
  0.6 0.0 copy-start.1
  0.6 0.0 copy-start.3
  0.7 0.7 %copy-done.3 = s32[8,128]{1,0:T(8,128)S(1)} copy-done((s32[8,128]{1,0:T(8,128)S(1)}, s32[8,128]{1,0:T(8,128)}, u32[]{:S(2)}) %copy-start.3) | copy-done | bytes 4120
  1.4 0.0 copy-start.2
  1.4 0.2 copy-done.1
  1.6 0.0 copy-start
  1.6 0.3 shard_map.60
  1.8 3.1 %collective-permute-start = (bf16[336,128]{1,0:T(8,128)(2,1)S(1)}, bf16[336,128]{1,0:T(8,128)(2,1)S(1)}, u32[]{:S(2)}, u32[]{:S(2)}) collective-permute-start(bf16[336,128]{1,0:T(8,128)(2,1)S(1)} %get-tuple-element.22), channel_id=1, source_target_pairs={{0,8},{1,9},{2,10},{3,11},{4,12},{5,13},{6,14},{7,15},{8,0},{9,1},... | collective-permute-start | bytes 258056 | tf_op jit(solution)/shard_map/ppermute | solution.py:348
  4.9 0.0 collective-permute-start.1
  4.9 0.0 copy-done.2
  4.9 0.0 copy-done
  4.9 0.3 %shard_map.61 = (bf16[128,512]{1,0:T(8,128)(2,1)S(1)}, bf16[128,64]{1,0:T(8,128)(2,1)S(1)}, bf16[128,768]{1,0:T(8,128)(2,1)S(1)}) custom-call(bf16[64,8,128]{2,1,0:T(8,128)(2,1)S(1)} %copy-done, bf16[6,64,64]{2,1,0:T(8,128)(2,1)S(1)} %copy-done.2), custom_call_target="tpu_custom_call" | custom-call | flops 1048576 | bytes 1048576 | tf_op jit(solution)/shard_map/pallas_call | solution.py:335
  5.3 2.2 %collective-permute-done.first_ref = bf16[336,128]{1,0:T(8,128)(2,1)S(1)} collective-permute-done((bf16[336,128]{1,0:T(8,128)(2,1)S(1)}, bf16[336,128]{1,0:T(8,128)(2,1)S(1)}, u32[]{:S(2)}, u32[]{:S(2)}) %collective-permute-start) | collective-permute-done | bytes 86048 | tf_op jit(solution)/shard_map/ppermute | solution.py:348
  7.4 0.0 collective-permute-done.1.second_ref
  7.4 0.1 shard_map.63
  7.5 1.2 %collective-permute-start.2 = (bf16[96,128]{1,0:T(8,128)(2,1)S(1)}, bf16[96,128]{1,0:T(8,128)(2,1)S(1)}, u32[]{:S(2)}, u32[]{:S(2)}) collective-permute-start(bf16[96,128]{1,0:T(8,128)(2,1)S(1)} %get-tuple-element.27), channel_id=1, source_target_pairs={{0,7},{1,2},{2,1},{3,4},{4,3},{5,6},{6,5},{7,0},{8,15},{9,10},{10,... | collective-permute-start | bytes 73736 | tf_op jit(solution)/shard_map/ppermute | solution.py:348
  8.7 0.9 %collective-permute-start.3 = (bf16[96,128]{1,0:T(8,128)(2,1)S(1)}, bf16[96,128]{1,0:T(8,128)(2,1)S(1)}, u32[]{:S(2)}, u32[]{:S(2)}) collective-permute-start(bf16[96,128]{1,0:T(8,128)(2,1)S(1)} %get-tuple-element.28), channel_id=1, source_target_pairs={{0,1},{1,0},{2,3},{3,2},{4,5},{5,4},{6,7},{7,6},{8,9},{9,8},{10,11... | collective-permute-start | bytes 73736 | tf_op jit(solution)/shard_map/ppermute | solution.py:348
  9.6 1.8 %shard_map.62 = (bf16[512,768]{1,0:T(8,128)(2,1)S(1)}, f32[3,64,128]{2,1,0:T(8,128)S(1)}, f32[432,128]{1,0:T(8,128)S(1)}, f32[24,128]{1,0:T(8,128)S(1)}) custom-call(bf16[512,128]{1,0:T(8,128)(2,1)S(1)} %get-tuple-element.21.body_ref, bf16[16,128]{1,0:T(8,128)(2,1)S(1)} %shard_map.59.mask_ref, bf16[336,128]{1,0:T(8,128)(2,1)S(1)} %collective-permute-done.first_ref, ...), custom_call_target="tpu_custom_call" | custom-call | flops 268435456 | bytes 1048576 | tf_op jit(solution)/shard_map/pallas_call | solution.py:335
  11.4 0.4 %collective-permute-done.2.second_ref = bf16[96,128]{1,0:T(8,128)(2,1)S(1)} collective-permute-done((bf16[96,128]{1,0:T(8,128)(2,1)S(1)}, bf16[96,128]{1,0:T(8,128)(2,1)S(1)}, u32[]{:S(2)}, u32[]{:S(2)}) %collective-permute-start.2) | collective-permute-done | bytes 24608 | tf_op jit(solution)/shard_map/ppermute | solution.py:348
  11.8 0.0 collective-permute-done.3.first_ref
  11.8 0.9 %shard_map.64 = (bf16[64,768]{1,0:T(8,128)(2,1)S(1)}, f32[208,128]{1,0:T(8,128)S(1)}) custom-call(f32[432,128]{1,0:T(8,128)S(1)} %get-tuple-element.25.own_ref, f32[24,128]{1,0:T(8,128)S(1)} %get-tuple-element.26.centre_ref, bf16[96,128]{1,0:T(8,128)(2,1)S(1)} %collective-permute-done.2.second_ref, bf16[96,128]{1,0:T(8,128)(2,1)S(1)} %collective-permute-done.3.first_ref, ...), custom_call_target="tpu_custom_call" | custom-call | flops 67108864 | bytes 1048576 | tf_op jit(solution)/shard_map/pallas_call | solution.py:335
  12.7 0.8 %collective-permute-start.4 = (f16[208,128]{1,0:T(8,128)(2,1)S(1)}, f16[208,128]{1,0:T(8,128)(2,1)S(1)}, u32[]{:S(2)}, u32[]{:S(2)}) collective-permute-start(f16[208,128]{1,0:T(8,128)(2,1)S(1)} %convert_element_type.36), channel_id=1, source_target_pairs={{0,3},{1,8},{2,11},{3,0},{4,13},{5,6},{6,5},{7,14},{8,1},{9,10},{1... | collective-permute-start | bytes 159752 | tf_op jit(solution)/shard_map/ppermute | solution.py:348
  13.6 1.2 %shard_map.65 = bf16[64,8,128]{2,1,0:T(8,128)(2,1)} custom-call(bf16[128,768]{1,0:T(8,128)(2,1)S(1)} %get-tuple-element.35.weight_ref, bf16[512,768]{1,0:T(8,128)(2,1)S(1)} %get-tuple-element.36.inner_ref, bf16[64,768]{1,0:T(8,128)(2,1)S(1)} %get-tuple-element.37.rim_ref), custom_call_target="tpu_custom_call" | custom-call | flops 1048576 | bytes 1048576 | tf_op jit(solution)/shard_map/pallas_call | solution.py:335
  14.7 1.6 %collective-permute-done.4 = f16[208,128]{1,0:T(8,128)(2,1)S(1)} collective-permute-done((f16[208,128]{1,0:T(8,128)(2,1)S(1)}, f16[208,128]{1,0:T(8,128)(2,1)S(1)}, u32[]{:S(2)}, u32[]{:S(2)}) %collective-permute-start.4) | collective-permute-done | bytes 53280 | tf_op jit(solution)/shard_map/ppermute | solution.py:348
  16.4 2.0 %collective-permute-start.5 = (f16[208,128]{1,0:T(8,128)(2,1)S(1)}, f16[208,128]{1,0:T(8,128)(2,1)S(1)}, u32[]{:S(2)}, u32[]{:S(2)}) collective-permute-start(f16[208,128]{1,0:T(8,128)(2,1)S(1)} %convert_element_type.39), channel_id=1, source_target_pairs={{0,9},{1,2},{2,1},{3,10},{4,7},{5,12},{6,15},{7,4},{8,11},{9,0},{1... | collective-permute-start | bytes 159752 | tf_op jit(solution)/shard_map/ppermute | solution.py:348
  18.4 1.8 %collective-permute-done.5 = f16[208,128]{1,0:T(8,128)(2,1)S(1)} collective-permute-done((f16[208,128]{1,0:T(8,128)(2,1)S(1)}, f16[208,128]{1,0:T(8,128)(2,1)S(1)}, u32[]{:S(2)}, u32[]{:S(2)}) %collective-permute-start.5) | collective-permute-done | bytes 53280 | tf_op jit(solution)/shard_map/ppermute | solution.py:348
  20.3 2.4 %collective-permute-start.6 = (f16[208,128]{1,0:T(8,128)(2,1)S(1)}, f16[208,128]{1,0:T(8,128)(2,1)S(1)}, u32[]{:S(2)}, u32[]{:S(2)}) collective-permute-start(f16[208,128]{1,0:T(8,128)(2,1)S(1)} %convert_element_type.42), channel_id=1, source_target_pairs={{0,5},{1,16},{2,19},{3,6},{4,21},{5,0},{6,3},{7,22},{8,25},{9,12},... | collective-permute-start | bytes 159752 | tf_op jit(solution)/shard_map/ppermute | solution.py:348
  22.8 1.8 %collective-permute-done.6 = f16[208,128]{1,0:T(8,128)(2,1)S(1)} collective-permute-done((f16[208,128]{1,0:T(8,128)(2,1)S(1)}, f16[208,128]{1,0:T(8,128)(2,1)S(1)}, u32[]{:S(2)}, u32[]{:S(2)}) %collective-permute-start.6) | collective-permute-done | bytes 53280 | tf_op jit(solution)/shard_map/ppermute | solution.py:348
  24.6 3.3 %collective-permute-start.7 = (f16[208,128]{1,0:T(8,128)(2,1)S(1)}, f16[208,128]{1,0:T(8,128)(2,1)S(1)}, u32[]{:S(2)}, u32[]{:S(2)}) collective-permute-start(f16[208,128]{1,0:T(8,128)(2,1)S(1)} %convert_element_type.45), channel_id=1, source_target_pairs={{0,17},{1,4},{2,7},{3,18},{4,1},{5,20},{6,23},{7,2},{8,13},{9,24},... | collective-permute-start | bytes 159752 | tf_op jit(solution)/shard_map/ppermute | solution.py:348
  27.9 1.8 %collective-permute-done.7 = f16[208,128]{1,0:T(8,128)(2,1)S(1)} collective-permute-done((f16[208,128]{1,0:T(8,128)(2,1)S(1)}, f16[208,128]{1,0:T(8,128)(2,1)S(1)}, u32[]{:S(2)}, u32[]{:S(2)}) %collective-permute-start.7) | collective-permute-done | bytes 53280 | tf_op jit(solution)/shard_map/ppermute | solution.py:348
  29.8 1.4 %collective-permute-start.8 = (f32[192,128]{1,0:T(8,128)S(1)}, f32[192,128]{1,0:T(8,128)S(1)}, u32[]{:S(2)}, u32[]{:S(2)}) collective-permute-start(f32[192,128]{1,0:T(8,128)S(1)} %shard_map.69.mine_ref), channel_id=1, source_target_pairs={{0,1},{1,0},{2,3},{3,2},{4,5},{5,4},{6,7},{7,6},{8,9},{9,8},{10,11... | collective-permute-start | bytes 294920 | tf_op jit(solution)/shard_map/ppermute | solution.py:348
  31.2 0.9 %collective-permute-done.8.other_ref = f32[192,128]{1,0:T(8,128)S(1)} collective-permute-done((f32[192,128]{1,0:T(8,128)S(1)}, f32[192,128]{1,0:T(8,128)S(1)}, u32[]{:S(2)}, u32[]{:S(2)}) %collective-permute-start.8) | collective-permute-done | bytes 98336 | tf_op jit(solution)/shard_map/ppermute | solution.py:348
  32.1 0.8 %shard_map.70 = f32[6,64,64]{2,1,0:T(8,128)} custom-call(f32[192,128]{1,0:T(8,128)S(1)} %shard_map.69.mine_ref, f32[192,128]{1,0:T(8,128)S(1)} %collective-permute-done.8.other_ref), custom_call_target="tpu_custom_call" | custom-call | flops 65536 | bytes 1048576 | tf_op jit(solution)/shard_map/pallas_call | solution.py:335
  (17 shorter events, 0.2 us)
Async XLA Ops:
  0.6 0.9 %copy-start.1 = (bf16[64,8,128]{2,1,0:T(8,128)(2,1)S(1)}, bf16[64,8,128]{2,1,0:T(8,128)(2,1)}, u32[]{:S(2)}) copy-start(bf16[64,8,128]{2,1,0:T(8,128)(2,1)} %cot_ref.1) | copy-start | bytes 393220
  0.6 0.7 %copy-start.3 = (s32[8,128]{1,0:T(8,128)S(1)}, s32[8,128]{1,0:T(8,128)}, u32[]{:S(2)}) copy-start(s32[8,128]{1,0:T(8,128)} %mask_ref.1) | copy-start | bytes 12292
  1.4 3.5 %copy-start.2 = (bf16[6,64,64]{2,1,0:T(8,128)(2,1)S(1)}, bf16[6,64,64]{2,1,0:T(8,128)(2,1)}, u32[]{:S(2)}) copy-start(bf16[6,64,64]{2,1,0:T(8,128)(2,1)} %weight_ref.1) | copy-start | bytes 147460
  1.6 3.4 %copy-start = (bf16[64,8,128]{2,1,0:T(8,128)(2,1)S(1)}, bf16[64,8,128]{2,1,0:T(8,128)(2,1)}, u32[]{:S(2)}) copy-start(bf16[64,8,128]{2,1,0:T(8,128)(2,1)} %feature_ref.1) | copy-start | bytes 393220
  1.8 5.6 %collective-permute-start = (bf16[336,128]{1,0:T(8,128)(2,1)S(1)}, bf16[336,128]{1,0:T(8,128)(2,1)S(1)}, u32[]{:S(2)}, u32[]{:S(2)}) collective-permute-start(bf16[336,128]{1,0:T(8,128)(2,1)S(1)} %get-tuple-element.22), channel_id=1, source_target_pairs={{0,8},{1,9},{2,10},{3,11},{4,12},{5,13},{6,14},{7,15},{8,0},{9,1},... | collective-permute-start | bytes 258056 | tf_op jit(solution)/shard_map/ppermute | solution.py:348
  4.9 2.5 %collective-permute-start.1 = (bf16[336,128]{1,0:T(8,128)(2,1)S(1)}, bf16[336,128]{1,0:T(8,128)(2,1)S(1)}, u32[]{:S(2)}, u32[]{:S(2)}) collective-permute-start(bf16[336,128]{1,0:T(8,128)(2,1)S(1)} %get-tuple-element.23), channel_id=1, source_target_pairs={{0,1},{1,0},{2,3},{3,2},{4,5},{5,4},{6,7},{7,6},{8,16},{9,17},{10,... | collective-permute-start | bytes 258056 | tf_op jit(solution)/shard_map/ppermute | solution.py:348
  7.5 4.2 %collective-permute-start.2 = (bf16[96,128]{1,0:T(8,128)(2,1)S(1)}, bf16[96,128]{1,0:T(8,128)(2,1)S(1)}, u32[]{:S(2)}, u32[]{:S(2)}) collective-permute-start(bf16[96,128]{1,0:T(8,128)(2,1)S(1)} %get-tuple-element.27), channel_id=1, source_target_pairs={{0,7},{1,2},{2,1},{3,4},{4,3},{5,6},{6,5},{7,0},{8,15},{9,10},{10,... | collective-permute-start | bytes 73736 | tf_op jit(solution)/shard_map/ppermute | solution.py:348
  8.7 3.0 %collective-permute-start.3 = (bf16[96,128]{1,0:T(8,128)(2,1)S(1)}, bf16[96,128]{1,0:T(8,128)(2,1)S(1)}, u32[]{:S(2)}, u32[]{:S(2)}) collective-permute-start(bf16[96,128]{1,0:T(8,128)(2,1)S(1)} %get-tuple-element.28), channel_id=1, source_target_pairs={{0,1},{1,0},{2,3},{3,2},{4,5},{5,4},{6,7},{7,6},{8,9},{9,8},{10,11... | collective-permute-start | bytes 73736 | tf_op jit(solution)/shard_map/ppermute | solution.py:348
  12.7 3.6 %collective-permute-start.4 = (f16[208,128]{1,0:T(8,128)(2,1)S(1)}, f16[208,128]{1,0:T(8,128)(2,1)S(1)}, u32[]{:S(2)}, u32[]{:S(2)}) collective-permute-start(f16[208,128]{1,0:T(8,128)(2,1)S(1)} %convert_element_type.36), channel_id=1, source_target_pairs={{0,3},{1,8},{2,11},{3,0},{4,13},{5,6},{6,5},{7,14},{8,1},{9,10},{1... | collective-permute-start | bytes 159752 | tf_op jit(solution)/shard_map/ppermute | solution.py:348
  16.4 3.8 %collective-permute-start.5 = (f16[208,128]{1,0:T(8,128)(2,1)S(1)}, f16[208,128]{1,0:T(8,128)(2,1)S(1)}, u32[]{:S(2)}, u32[]{:S(2)}) collective-permute-start(f16[208,128]{1,0:T(8,128)(2,1)S(1)} %convert_element_type.39), channel_id=1, source_target_pairs={{0,9},{1,2},{2,1},{3,10},{4,7},{5,12},{6,15},{7,4},{8,11},{9,0},{1... | collective-permute-start | bytes 159752 | tf_op jit(solution)/shard_map/ppermute | solution.py:348
  20.3 4.3 %collective-permute-start.6 = (f16[208,128]{1,0:T(8,128)(2,1)S(1)}, f16[208,128]{1,0:T(8,128)(2,1)S(1)}, u32[]{:S(2)}, u32[]{:S(2)}) collective-permute-start(f16[208,128]{1,0:T(8,128)(2,1)S(1)} %convert_element_type.42), channel_id=1, source_target_pairs={{0,5},{1,16},{2,19},{3,6},{4,21},{5,0},{6,3},{7,22},{8,25},{9,12},... | collective-permute-start | bytes 159752 | tf_op jit(solution)/shard_map/ppermute | solution.py:348
  24.6 5.1 %collective-permute-start.7 = (f16[208,128]{1,0:T(8,128)(2,1)S(1)}, f16[208,128]{1,0:T(8,128)(2,1)S(1)}, u32[]{:S(2)}, u32[]{:S(2)}) collective-permute-start(f16[208,128]{1,0:T(8,128)(2,1)S(1)} %convert_element_type.45), channel_id=1, source_target_pairs={{0,17},{1,4},{2,7},{3,18},{4,1},{5,20},{6,23},{7,2},{8,13},{9,24},... | collective-permute-start | bytes 159752 | tf_op jit(solution)/shard_map/ppermute | solution.py:348
  29.8 2.4 %collective-permute-start.8 = (f32[192,128]{1,0:T(8,128)S(1)}, f32[192,128]{1,0:T(8,128)S(1)}, u32[]{:S(2)}, u32[]{:S(2)}) collective-permute-start(f32[192,128]{1,0:T(8,128)S(1)} %shard_map.69.mine_ref), channel_id=1, source_target_pairs={{0,1},{1,0},{2,3},{3,2},{4,5},{5,4},{6,7},{7,6},{8,9},{9,8},{10,11... | collective-permute-start | bytes 294920 | tf_op jit(solution)/shard_map/ppermute | solution.py:348

commit v7 on v4

--- a/solution.py
+++ b/solution.py
@@ -149,6 +149,13 @@
         scale_ref[q * tall : (q + 1) * tall, :] = picked
 
 
+def clear_rims(tall, shift_ref):
+    whole = tall + 2 * RIM
+    for begin in range(0, shift_ref.shape[0], whole):
+        for at in (begin, begin + whole - RIM):
+            shift_ref[at : at + RIM, :] = jnp.zeros((RIM, shift_ref.shape[1]), F32)
+
+
 def next_term(k, tall, scale_ref, newer_ref, older_ref, shift_ref, visit):
     total = scale_ref.shape[0] // tall
 
@@ -208,7 +215,7 @@
         own_ref[at + RIM : at + 2 * RIM, :] = jnp.where(low, middle[:RIM], middle[tail + RIM :])
         own_ref[at + 2 * RIM : at + 3 * RIM, :] = jnp.where(low, middle[RIM : 2 * RIM], 0.0)
     terms_ref[:, :lanes] = body_ref[...]
-    shift_ref[...] = jnp.zeros_like(shift_ref)
+    clear_rims(tall, shift_ref)
     newer, older = odd_ref, even_ref
     for k in range(1, orders):
         def keep(q, fresh):
@@ -236,7 +243,7 @@
     message_ref[at:, :] = jnp.concatenate([exponent] * (NOTES // 8), axis=0)
 
 
-def add_kernel(mine_ref, received_ref, out_ref):
+def decoded_sums(mine_ref, received_ref):
     notes = mine_ref.shape[0] - NOTES
     mine, received = mine_ref[notes : notes + 8, :], received_ref[notes : notes + 8, :]
     scales = jnp.exp2(mine - 9.0), jnp.exp2(received - 9.0)
@@ -244,10 +251,11 @@
     for row in range(0, notes, 8):
         at = slice(row, row + 8)
         sums.append(mine_ref[at, :] * scales[0] + received_ref[at, :] * scales[1])
-    if out_ref.shape[0] == notes:
-        out_ref[...] = jnp.concatenate(sums, axis=0)
-    else:
-        store_sums(out_ref, sums, jnp.maximum(mine, received) + 1.0)
+    return sums, jnp.maximum(mine, received) + 1.0
+
+
+def add_kernel(mine_ref, received_ref, out_ref):
+    store_sums(out_ref, *decoded_sums(mine_ref, received_ref))
 
 
 def edge_kernel(
@@ -277,7 +285,7 @@
 
     wide_ref[:, :lanes] = jnp.zeros((rows * RIM, lanes), F32)
     blocks = []
-    shift_ref[...] = jnp.zeros_like(shift_ref)
+    clear_rims(tall, shift_ref)
     newer, older = odd_ref, even_ref
     for k in range(1, orders):
         def keep(q, fresh):
@@ -324,11 +332,12 @@
 
 def finish_kernel(divisor, mine_ref, other_ref, out_ref):
     channels = out_ref.shape[1]
-    for b in range(out_ref.shape[0] // 2):
-        at = slice(b * channels, (b + 1) * channels)
-        block = (mine_ref[at, :] + other_ref[at, :]) / divisor
-        out_ref[2 * b] = block[:, :channels]
-        out_ref[2 * b + 1] = block[:, channels:]
+    sums, _ = decoded_sums(mine_ref, other_ref)
+    for n, block in enumerate(sums):
+        b, row = n * 8 // channels, n * 8 % channels
+        block = block / divisor
+        out_ref[2 * b, row : row + 8, :] = block[:, :channels]
+        out_ref[2 * b + 1, row : row + 8, :] = block[:, channels:]
 
 
 def call(kernel, outs, scratch, cost, *args):
@@ -382,12 +391,11 @@
         if n == 0:
             _, *args = lax.optimization_barrier((message, *args))
             received, done = lax.optimization_barrier((received, work(*args)))
-        rows = part.shape[0] - (NOTES if n == len(even) - 1 else 0)
         part = call(
-            add_kernel, jax.ShapeDtypeStruct((rows, part.shape[1]), F32), [], 1 << 16,
-            message.astype(F32), received.astype(F32),
+            add_kernel, jax.ShapeDtypeStruct(part.shape, F32), [], 1 << 16, message.astype(F32), received.astype(F32)
         )
-    return part, swap(part, lambda i: i ^ 1), done
+    message = lax.optimization_barrier(part.astype(jnp.float16))
+    return message.astype(F32), swap(message, lambda i: i ^ 1).astype(F32), done
 
 
 def body(feature, cotangent, order_weight, pixel_mask):

time: 32.4 us -> 32.4 us (level)
  no operation moved by 1% of the time
where the time goes in v7:
time: 32.4 us; the launch traced here: 32.2 us
  waiting for transfers between devices  13.8 us (43%)
  starting transfers between devices  11 us (34%)
  Pallas kernels  5.49 us (17%)
  local copies, waits for them, and re-layouts  0.91 us (3%)
  between operations  0.8 us (2%)
    ppermute x9, waiting for transfers between devices, swap(): return lax.ppermute(x, ('row', 'col'), [(i, partner(i)) for i in places])  13.8 us
    ppermute x9, starting transfers between devices, swap(): return lax.ppermute(x, ('row', 'col'), [(i, partner(i)) for i in places])  11 us
    pallas_call x12, Pallas kernels, call(): pl.pallas_call(kernel, out_shape=outs, in_specs=[pl.BlockSpec(memory_spac...  5.49 us
    unnamed x8, local copies, waits for them, and re-layouts  0.91 us
  transfers between devices with their start and end apart: 9, of which 7 were waited for; matrix products, arithmetic and copies ran while one was open for 0% of the time, Pallas kernels for 10%

profile of v7, /device:TPU:0, one launch (start us, length us, event | category | flops | bytes accessed | tf_op | source)
XLA Modules:
  0.0 32.2 jit_solution(17162386838939993765)
XLA Ops:
  0.6 0.0 copy-start.1
  0.6 0.0 copy-start.3
  0.7 0.7 %copy-done.3 = s32[8,128]{1,0:T(8,128)S(1)} copy-done((s32[8,128]{1,0:T(8,128)S(1)}, s32[8,128]{1,0:T(8,128)}, u32[]{:S(2)}) %copy-start.3) | copy-done | bytes 4120
  1.4 0.0 copy-start.2
  1.4 0.2 copy-done.1
  1.6 0.0 copy-start
  1.6 0.3 shard_map.60
  1.8 0.5 %collective-permute-start = (bf16[336,128]{1,0:T(8,128)(2,1)S(1)}, bf16[336,128]{1,0:T(8,128)(2,1)S(1)}, u32[]{:S(2)}, u32[]{:S(2)}) collective-permute-start(bf16[336,128]{1,0:T(8,128)(2,1)S(1)} %get-tuple-element.22), channel_id=1, source_target_pairs={{0,1},{1,0},{2,3},{3,2},{4,5},{5,4},{6,7},{7,6},{8,16},{9,17},{10,... | collective-permute-start | bytes 258056 | tf_op jit(solution)/shard_map/ppermute | solution.py:357
  2.3 4.1 %collective-permute-start.1 = (bf16[336,128]{1,0:T(8,128)(2,1)S(1)}, bf16[336,128]{1,0:T(8,128)(2,1)S(1)}, u32[]{:S(2)}, u32[]{:S(2)}) collective-permute-start(bf16[336,128]{1,0:T(8,128)(2,1)S(1)} %get-tuple-element.23), channel_id=1, source_target_pairs={{0,8},{1,9},{2,10},{3,11},{4,12},{5,13},{6,14},{7,15},{8,0},{9,1},... | collective-permute-start | bytes 258056 | tf_op jit(solution)/shard_map/ppermute | solution.py:357
  6.5 0.0 copy-done.2
  6.5 0.0 copy-done
  6.5 0.3 %shard_map.61 = (bf16[128,512]{1,0:T(8,128)(2,1)S(1)}, bf16[128,64]{1,0:T(8,128)(2,1)S(1)}, bf16[128,768]{1,0:T(8,128)(2,1)S(1)}) custom-call(bf16[64,8,128]{2,1,0:T(8,128)(2,1)S(1)} %copy-done, bf16[6,64,64]{2,1,0:T(8,128)(2,1)S(1)} %copy-done.2), custom_call_target="tpu_custom_call" | custom-call | flops 1048576 | bytes 1048576 | tf_op jit(solution)/shard_map/pallas_call | solution.py:344
  6.8 0.0 collective-permute-done.second_ref
  6.8 2.1 %collective-permute-done.1.first_ref = bf16[336,128]{1,0:T(8,128)(2,1)S(1)} collective-permute-done((bf16[336,128]{1,0:T(8,128)(2,1)S(1)}, bf16[336,128]{1,0:T(8,128)(2,1)S(1)}, u32[]{:S(2)}, u32[]{:S(2)}) %collective-permute-start.1) | collective-permute-done | bytes 86048 | tf_op jit(solution)/shard_map/ppermute | solution.py:357
  8.9 0.1 shard_map.63
  9.0 0.8 %collective-permute-start.2 = (bf16[96,128]{1,0:T(8,128)(2,1)S(1)}, bf16[96,128]{1,0:T(8,128)(2,1)S(1)}, u32[]{:S(2)}, u32[]{:S(2)}) collective-permute-start(bf16[96,128]{1,0:T(8,128)(2,1)S(1)} %get-tuple-element.27), channel_id=1, source_target_pairs={{0,7},{1,2},{2,1},{3,4},{4,3},{5,6},{6,5},{7,0},{8,15},{9,10},{10,... | collective-permute-start | bytes 73736 | tf_op jit(solution)/shard_map/ppermute | solution.py:357
  9.8 0.9 %collective-permute-start.3 = (bf16[96,128]{1,0:T(8,128)(2,1)S(1)}, bf16[96,128]{1,0:T(8,128)(2,1)S(1)}, u32[]{:S(2)}, u32[]{:S(2)}) collective-permute-start(bf16[96,128]{1,0:T(8,128)(2,1)S(1)} %get-tuple-element.28), channel_id=1, source_target_pairs={{0,1},{1,0},{2,3},{3,2},{4,5},{5,4},{6,7},{7,6},{8,9},{9,8},{10,11... | collective-permute-start | bytes 73736 | tf_op jit(solution)/shard_map/ppermute | solution.py:357
  10.7 1.8 %shard_map.62 = (bf16[512,768]{1,0:T(8,128)(2,1)S(1)}, f32[3,64,128]{2,1,0:T(8,128)S(1)}, f32[432,128]{1,0:T(8,128)S(1)}, f32[24,128]{1,0:T(8,128)S(1)}) custom-call(bf16[512,128]{1,0:T(8,128)(2,1)S(1)} %get-tuple-element.21.body_ref, bf16[16,128]{1,0:T(8,128)(2,1)S(1)} %shard_map.59.mask_ref, bf16[336,128]{1,0:T(8,128)(2,1)S(1)} %collective-permute-done.second_ref, ...), custom_call_target="tpu_custom_call" | custom-call | flops 268435456 | bytes 1048576 | tf_op jit(solution)/shard_map/pallas_call | solution.py:344
  12.5 0.9 %collective-permute-done.2.second_ref = bf16[96,128]{1,0:T(8,128)(2,1)S(1)} collective-permute-done((bf16[96,128]{1,0:T(8,128)(2,1)S(1)}, bf16[96,128]{1,0:T(8,128)(2,1)S(1)}, u32[]{:S(2)}, u32[]{:S(2)}) %collective-permute-start.2) | collective-permute-done | bytes 24608 | tf_op jit(solution)/shard_map/ppermute | solution.py:357
  13.4 0.0 collective-permute-done.3.first_ref
  13.4 0.9 %shard_map.64 = (bf16[64,768]{1,0:T(8,128)(2,1)S(1)}, f32[208,128]{1,0:T(8,128)S(1)}) custom-call(f32[432,128]{1,0:T(8,128)S(1)} %get-tuple-element.25.own_ref, f32[24,128]{1,0:T(8,128)S(1)} %get-tuple-element.26.centre_ref, bf16[96,128]{1,0:T(8,128)(2,1)S(1)} %collective-permute-done.2.second_ref, bf16[96,128]{1,0:T(8,128)(2,1)S(1)} %collective-permute-done.3.first_ref, ...), custom_call_target="tpu_custom_call" | custom-call | flops 67108864 | bytes 1048576 | tf_op jit(solution)/shard_map/pallas_call | solution.py:344
  14.4 0.3 collective-permute-start.4
  14.7 1.2 %shard_map.65 = bf16[64,8,128]{2,1,0:T(8,128)(2,1)} custom-call(bf16[128,768]{1,0:T(8,128)(2,1)S(1)} %get-tuple-element.35.weight_ref, bf16[512,768]{1,0:T(8,128)(2,1)S(1)} %get-tuple-element.36.inner_ref, bf16[64,768]{1,0:T(8,128)(2,1)S(1)} %get-tuple-element.37.rim_ref), custom_call_target="tpu_custom_call" | custom-call | flops 1048576 | bytes 1048576 | tf_op jit(solution)/shard_map/pallas_call | solution.py:344
  15.9 2.1 %collective-permute-done.4 = f16[208,128]{1,0:T(8,128)(2,1)S(1)} collective-permute-done((f16[208,128]{1,0:T(8,128)(2,1)S(1)}, f16[208,128]{1,0:T(8,128)(2,1)S(1)}, u32[]{:S(2)}, u32[]{:S(2)}) %collective-permute-start.4) | collective-permute-done | bytes 53280 | tf_op jit(solution)/shard_map/ppermute | solution.py:357
  18.1 0.8 %collective-permute-start.5 = (f16[208,128]{1,0:T(8,128)(2,1)S(1)}, f16[208,128]{1,0:T(8,128)(2,1)S(1)}, u32[]{:S(2)}, u32[]{:S(2)}) collective-permute-start(f16[208,128]{1,0:T(8,128)(2,1)S(1)} %convert_element_type.48), channel_id=1, source_target_pairs={{0,9},{1,2},{2,1},{3,10},{4,7},{5,12},{6,15},{7,4},{8,11},{9,0},{1... | collective-permute-start | bytes 159752 | tf_op jit(solution)/shard_map/ppermute | solution.py:357
  18.9 2.8 %collective-permute-done.5 = f16[208,128]{1,0:T(8,128)(2,1)S(1)} collective-permute-done((f16[208,128]{1,0:T(8,128)(2,1)S(1)}, f16[208,128]{1,0:T(8,128)(2,1)S(1)}, u32[]{:S(2)}, u32[]{:S(2)}) %collective-permute-start.5) | collective-permute-done | bytes 53280 | tf_op jit(solution)/shard_map/ppermute | solution.py:357
  21.8 1.4 %collective-permute-start.6 = (f16[208,128]{1,0:T(8,128)(2,1)S(1)}, f16[208,128]{1,0:T(8,128)(2,1)S(1)}, u32[]{:S(2)}, u32[]{:S(2)}) collective-permute-start(f16[208,128]{1,0:T(8,128)(2,1)S(1)} %convert_element_type.51), channel_id=1, source_target_pairs={{0,5},{1,16},{2,19},{3,6},{4,21},{5,0},{6,3},{7,22},{8,25},{9,12},... | collective-permute-start | bytes 159752 | tf_op jit(solution)/shard_map/ppermute | solution.py:357
  23.2 2.2 %collective-permute-done.6 = f16[208,128]{1,0:T(8,128)(2,1)S(1)} collective-permute-done((f16[208,128]{1,0:T(8,128)(2,1)S(1)}, f16[208,128]{1,0:T(8,128)(2,1)S(1)}, u32[]{:S(2)}, u32[]{:S(2)}) %collective-permute-start.6) | collective-permute-done | bytes 53280 | tf_op jit(solution)/shard_map/ppermute | solution.py:357
  25.4 1.7 %collective-permute-start.7 = (f16[208,128]{1,0:T(8,128)(2,1)S(1)}, f16[208,128]{1,0:T(8,128)(2,1)S(1)}, u32[]{:S(2)}, u32[]{:S(2)}) collective-permute-start(f16[208,128]{1,0:T(8,128)(2,1)S(1)} %convert_element_type.54), channel_id=1, source_target_pairs={{0,17},{1,4},{2,7},{3,18},{4,1},{5,20},{6,23},{7,2},{8,13},{9,24},... | collective-permute-start | bytes 159752 | tf_op jit(solution)/shard_map/ppermute | solution.py:357
  27.2 2.8 %collective-permute-done.7 = f16[208,128]{1,0:T(8,128)(2,1)S(1)} collective-permute-done((f16[208,128]{1,0:T(8,128)(2,1)S(1)}, f16[208,128]{1,0:T(8,128)(2,1)S(1)}, u32[]{:S(2)}, u32[]{:S(2)}) %collective-permute-start.7) | collective-permute-done | bytes 53280 | tf_op jit(solution)/shard_map/ppermute | solution.py:357
  30.0 0.5 %collective-permute-start.8 = (f16[208,128]{1,0:T(8,128)(2,1)S(1)}, f16[208,128]{1,0:T(8,128)(2,1)S(1)}, u32[]{:S(2)}, u32[]{:S(2)}) collective-permute-start(f16[208,128]{1,0:T(8,128)(2,1)S(1)} %convert_element_type.57), channel_id=1, source_target_pairs={{0,1},{1,0},{2,3},{3,2},{4,5},{5,4},{6,7},{7,6},{8,9},{9,8},{10,11... | collective-permute-start | bytes 159752 | tf_op jit(solution)/shard_map/ppermute | solution.py:357
  30.5 0.9 %collective-permute-done.8 = f16[208,128]{1,0:T(8,128)(2,1)S(1)} collective-permute-done((f16[208,128]{1,0:T(8,128)(2,1)S(1)}, f16[208,128]{1,0:T(8,128)(2,1)S(1)}, u32[]{:S(2)}, u32[]{:S(2)}) %collective-permute-start.8) | collective-permute-done | bytes 53280 | tf_op jit(solution)/shard_map/ppermute | solution.py:357
  31.4 0.8 %shard_map.70 = f32[6,64,64]{2,1,0:T(8,128)} custom-call(f32[208,128]{1,0:T(8,128)S(1)} %convert_element_type.58.mine_ref, f32[208,128]{1,0:T(8,128)S(1)} %convert_element_type.59.other_ref), custom_call_target="tpu_custom_call" | custom-call | flops 65536 | bytes 1048576 | tf_op jit(solution)/shard_map/pallas_call | solution.py:344
  (20 shorter events, 0.3 us)
Async XLA Ops:
  0.6 0.9 %copy-start.1 = (bf16[64,8,128]{2,1,0:T(8,128)(2,1)S(1)}, bf16[64,8,128]{2,1,0:T(8,128)(2,1)}, u32[]{:S(2)}) copy-start(bf16[64,8,128]{2,1,0:T(8,128)(2,1)} %cot_ref.1) | copy-start | bytes 393220
  0.6 0.7 %copy-start.3 = (s32[8,128]{1,0:T(8,128)S(1)}, s32[8,128]{1,0:T(8,128)}, u32[]{:S(2)}) copy-start(s32[8,128]{1,0:T(8,128)} %mask_ref.1) | copy-start | bytes 12292
  1.4 5.1 %copy-start.2 = (bf16[6,64,64]{2,1,0:T(8,128)(2,1)S(1)}, bf16[6,64,64]{2,1,0:T(8,128)(2,1)}, u32[]{:S(2)}) copy-start(bf16[6,64,64]{2,1,0:T(8,128)(2,1)} %weight_ref.1) | copy-start | bytes 147460
  1.6 4.9 %copy-start = (bf16[64,8,128]{2,1,0:T(8,128)(2,1)S(1)}, bf16[64,8,128]{2,1,0:T(8,128)(2,1)}, u32[]{:S(2)}) copy-start(bf16[64,8,128]{2,1,0:T(8,128)(2,1)} %feature_ref.1) | copy-start | bytes 393220
  1.8 5.0 %collective-permute-start = (bf16[336,128]{1,0:T(8,128)(2,1)S(1)}, bf16[336,128]{1,0:T(8,128)(2,1)S(1)}, u32[]{:S(2)}, u32[]{:S(2)}) collective-permute-start(bf16[336,128]{1,0:T(8,128)(2,1)S(1)} %get-tuple-element.22), channel_id=1, source_target_pairs={{0,1},{1,0},{2,3},{3,2},{4,5},{5,4},{6,7},{7,6},{8,16},{9,17},{10,... | collective-permute-start | bytes 258056 | tf_op jit(solution)/shard_map/ppermute | solution.py:357
  2.3 6.6 %collective-permute-start.1 = (bf16[336,128]{1,0:T(8,128)(2,1)S(1)}, bf16[336,128]{1,0:T(8,128)(2,1)S(1)}, u32[]{:S(2)}, u32[]{:S(2)}) collective-permute-start(bf16[336,128]{1,0:T(8,128)(2,1)S(1)} %get-tuple-element.23), channel_id=1, source_target_pairs={{0,8},{1,9},{2,10},{3,11},{4,12},{5,13},{6,14},{7,15},{8,0},{9,1},... | collective-permute-start | bytes 258056 | tf_op jit(solution)/shard_map/ppermute | solution.py:357
  9.0 4.4 %collective-permute-start.2 = (bf16[96,128]{1,0:T(8,128)(2,1)S(1)}, bf16[96,128]{1,0:T(8,128)(2,1)S(1)}, u32[]{:S(2)}, u32[]{:S(2)}) collective-permute-start(bf16[96,128]{1,0:T(8,128)(2,1)S(1)} %get-tuple-element.27), channel_id=1, source_target_pairs={{0,7},{1,2},{2,1},{3,4},{4,3},{5,6},{6,5},{7,0},{8,15},{9,10},{10,... | collective-permute-start | bytes 73736 | tf_op jit(solution)/shard_map/ppermute | solution.py:357
  9.8 3.6 %collective-permute-start.3 = (bf16[96,128]{1,0:T(8,128)(2,1)S(1)}, bf16[96,128]{1,0:T(8,128)(2,1)S(1)}, u32[]{:S(2)}, u32[]{:S(2)}) collective-permute-start(bf16[96,128]{1,0:T(8,128)(2,1)S(1)} %get-tuple-element.28), channel_id=1, source_target_pairs={{0,1},{1,0},{2,3},{3,2},{4,5},{5,4},{6,7},{7,6},{8,9},{9,8},{10,11... | collective-permute-start | bytes 73736 | tf_op jit(solution)/shard_map/ppermute | solution.py:357
  14.4 3.6 %collective-permute-start.4 = (f16[208,128]{1,0:T(8,128)(2,1)S(1)}, f16[208,128]{1,0:T(8,128)(2,1)S(1)}, u32[]{:S(2)}, u32[]{:S(2)}) collective-permute-start(f16[208,128]{1,0:T(8,128)(2,1)S(1)} %convert_element_type.45), channel_id=1, source_target_pairs={{0,3},{1,8},{2,11},{3,0},{4,13},{5,6},{6,5},{7,14},{8,1},{9,10},{1... | collective-permute-start | bytes 159752 | tf_op jit(solution)/shard_map/ppermute | solution.py:357
  18.1 3.6 %collective-permute-start.5 = (f16[208,128]{1,0:T(8,128)(2,1)S(1)}, f16[208,128]{1,0:T(8,128)(2,1)S(1)}, u32[]{:S(2)}, u32[]{:S(2)}) collective-permute-start(f16[208,128]{1,0:T(8,128)(2,1)S(1)} %convert_element_type.48), channel_id=1, source_target_pairs={{0,9},{1,2},{2,1},{3,10},{4,7},{5,12},{6,15},{7,4},{8,11},{9,0},{1... | collective-permute-start | bytes 159752 | tf_op jit(solution)/shard_map/ppermute | solution.py:357
  21.8 3.6 %collective-permute-start.6 = (f16[208,128]{1,0:T(8,128)(2,1)S(1)}, f16[208,128]{1,0:T(8,128)(2,1)S(1)}, u32[]{:S(2)}, u32[]{:S(2)}) collective-permute-start(f16[208,128]{1,0:T(8,128)(2,1)S(1)} %convert_element_type.51), channel_id=1, source_target_pairs={{0,5},{1,16},{2,19},{3,6},{4,21},{5,0},{6,3},{7,22},{8,25},{9,12},... | collective-permute-start | bytes 159752 | tf_op jit(solution)/shard_map/ppermute | solution.py:357
  25.4 4.5 %collective-permute-start.7 = (f16[208,128]{1,0:T(8,128)(2,1)S(1)}, f16[208,128]{1,0:T(8,128)(2,1)S(1)}, u32[]{:S(2)}, u32[]{:S(2)}) collective-permute-start(f16[208,128]{1,0:T(8,128)(2,1)S(1)} %convert_element_type.54), channel_id=1, source_target_pairs={{0,17},{1,4},{2,7},{3,18},{4,1},{5,20},{6,23},{7,2},{8,13},{9,24},... | collective-permute-start | bytes 159752 | tf_op jit(solution)/shard_map/ppermute | solution.py:357
  30.0 1.4 %collective-permute-start.8 = (f16[208,128]{1,0:T(8,128)(2,1)S(1)}, f16[208,128]{1,0:T(8,128)(2,1)S(1)}, u32[]{:S(2)}, u32[]{:S(2)}) collective-permute-start(f16[208,128]{1,0:T(8,128)(2,1)S(1)} %convert_element_type.57), channel_id=1, source_target_pairs={{0,1},{1,0},{2,3},{3,2},{4,5},{5,4},{6,7},{7,6},{8,9},{9,8},{10,11... | collective-permute-start | bytes 159752 | tf_op jit(solution)/shard_map/ppermute | solution.py:357

commit v8 on v7

--- a/solution.py
+++ b/solution.py
@@ -384,7 +384,8 @@
     below = list(range(across.bit_length() - 1, (across * down).bit_length() - 1))
     turns = [(beside[n : n + 1], below[n : n + 1]) for n in range(max(len(beside), len(below)))]
     even = [bit for a, b in turns for bit in a + b]
-    odd = [bit for a, b in turns for bit in b + a]
+    odd = [bit for a, b in zip(beside[::-1] + [None] * len(below), below) for bit in ([b] if a is None else [b, a])]
+    odd += [bit for bit in beside if bit not in odd]
     for n, bits in enumerate(zip(even, odd)):
         message = lax.optimization_barrier(part.astype(jnp.float16))
         received = swap(message, lambda i: i ^ (1 << bits[i.bit_count() % 2]) ^ 1)

time: 32.4 us -> 32.4 us (level)
  no operation moved by 1% of the time
where the time goes in v8:
time: 32.4 us; the launch traced here: 32.2 us
  waiting for transfers between devices  13.8 us (43%)
  starting transfers between devices  11 us (34%)
  Pallas kernels  5.49 us (17%)
  local copies, waits for them, and re-layouts  0.91 us (3%)
  between operations  0.8 us (2%)
    ppermute x9, waiting for transfers between devices, swap(): return lax.ppermute(x, ('row', 'col'), [(i, partner(i)) for i in places])  13.8 us
    ppermute x9, starting transfers between devices, swap(): return lax.ppermute(x, ('row', 'col'), [(i, partner(i)) for i in places])  11 us
    pallas_call x12, Pallas kernels, call(): pl.pallas_call(kernel, out_shape=outs, in_specs=[pl.BlockSpec(memory_spac...  5.49 us
    unnamed x8, local copies, waits for them, and re-layouts  0.91 us
  transfers between devices with their start and end apart: 9, of which 7 were waited for; matrix products, arithmetic and copies ran while one was open for 0% of the time, Pallas kernels for 10%

profile of v8, /device:TPU:0, one launch (start us, length us, event | category | flops | bytes accessed | tf_op | source)
XLA Modules:
  0.0 32.2 jit_solution(8742410511346738533)
XLA Ops:
  0.6 0.0 copy-start.1
  0.6 0.0 copy-start.3
  0.7 0.7 %copy-done.3 = s32[8,128]{1,0:T(8,128)S(1)} copy-done((s32[8,128]{1,0:T(8,128)S(1)}, s32[8,128]{1,0:T(8,128)}, u32[]{:S(2)}) %copy-start.3) | copy-done | bytes 4120
  1.4 0.0 copy-start.2
  1.4 0.2 copy-done.1
  1.6 0.0 copy-start
  1.6 0.3 shard_map.60
  1.8 0.5 %collective-permute-start = (bf16[336,128]{1,0:T(8,128)(2,1)S(1)}, bf16[336,128]{1,0:T(8,128)(2,1)S(1)}, u32[]{:S(2)}, u32[]{:S(2)}) collective-permute-start(bf16[336,128]{1,0:T(8,128)(2,1)S(1)} %get-tuple-element.22), channel_id=1, source_target_pairs={{0,1},{1,0},{2,3},{3,2},{4,5},{5,4},{6,7},{7,6},{8,16},{9,17},{10,... | collective-permute-start | bytes 258056 | tf_op jit(solution)/shard_map/ppermute | solution.py:357
  2.3 4.1 %collective-permute-start.1 = (bf16[336,128]{1,0:T(8,128)(2,1)S(1)}, bf16[336,128]{1,0:T(8,128)(2,1)S(1)}, u32[]{:S(2)}, u32[]{:S(2)}) collective-permute-start(bf16[336,128]{1,0:T(8,128)(2,1)S(1)} %get-tuple-element.23), channel_id=1, source_target_pairs={{0,8},{1,9},{2,10},{3,11},{4,12},{5,13},{6,14},{7,15},{8,0},{9,1},... | collective-permute-start | bytes 258056 | tf_op jit(solution)/shard_map/ppermute | solution.py:357
  6.5 0.0 copy-done.2
  6.5 0.0 copy-done
  6.5 0.3 %shard_map.61 = (bf16[128,512]{1,0:T(8,128)(2,1)S(1)}, bf16[128,64]{1,0:T(8,128)(2,1)S(1)}, bf16[128,768]{1,0:T(8,128)(2,1)S(1)}) custom-call(bf16[64,8,128]{2,1,0:T(8,128)(2,1)S(1)} %copy-done, bf16[6,64,64]{2,1,0:T(8,128)(2,1)S(1)} %copy-done.2), custom_call_target="tpu_custom_call" | custom-call | flops 1048576 | bytes 1048576 | tf_op jit(solution)/shard_map/pallas_call | solution.py:344
  6.8 0.0 collective-permute-done.second_ref
  6.8 2.1 %collective-permute-done.1.first_ref = bf16[336,128]{1,0:T(8,128)(2,1)S(1)} collective-permute-done((bf16[336,128]{1,0:T(8,128)(2,1)S(1)}, bf16[336,128]{1,0:T(8,128)(2,1)S(1)}, u32[]{:S(2)}, u32[]{:S(2)}) %collective-permute-start.1) | collective-permute-done | bytes 86048 | tf_op jit(solution)/shard_map/ppermute | solution.py:357
  8.9 0.1 shard_map.63
  9.0 0.8 %collective-permute-start.2 = (bf16[96,128]{1,0:T(8,128)(2,1)S(1)}, bf16[96,128]{1,0:T(8,128)(2,1)S(1)}, u32[]{:S(2)}, u32[]{:S(2)}) collective-permute-start(bf16[96,128]{1,0:T(8,128)(2,1)S(1)} %get-tuple-element.27), channel_id=1, source_target_pairs={{0,7},{1,2},{2,1},{3,4},{4,3},{5,6},{6,5},{7,0},{8,15},{9,10},{10,... | collective-permute-start | bytes 73736 | tf_op jit(solution)/shard_map/ppermute | solution.py:357
  9.8 0.9 %collective-permute-start.3 = (bf16[96,128]{1,0:T(8,128)(2,1)S(1)}, bf16[96,128]{1,0:T(8,128)(2,1)S(1)}, u32[]{:S(2)}, u32[]{:S(2)}) collective-permute-start(bf16[96,128]{1,0:T(8,128)(2,1)S(1)} %get-tuple-element.28), channel_id=1, source_target_pairs={{0,1},{1,0},{2,3},{3,2},{4,5},{5,4},{6,7},{7,6},{8,9},{9,8},{10,11... | collective-permute-start | bytes 73736 | tf_op jit(solution)/shard_map/ppermute | solution.py:357
  10.7 1.8 %shard_map.62 = (bf16[512,768]{1,0:T(8,128)(2,1)S(1)}, f32[3,64,128]{2,1,0:T(8,128)S(1)}, f32[432,128]{1,0:T(8,128)S(1)}, f32[24,128]{1,0:T(8,128)S(1)}) custom-call(bf16[512,128]{1,0:T(8,128)(2,1)S(1)} %get-tuple-element.21.body_ref, bf16[16,128]{1,0:T(8,128)(2,1)S(1)} %shard_map.59.mask_ref, bf16[336,128]{1,0:T(8,128)(2,1)S(1)} %collective-permute-done.second_ref, ...), custom_call_target="tpu_custom_call" | custom-call | flops 268435456 | bytes 1048576 | tf_op jit(solution)/shard_map/pallas_call | solution.py:344
  12.5 0.9 %collective-permute-done.2.second_ref = bf16[96,128]{1,0:T(8,128)(2,1)S(1)} collective-permute-done((bf16[96,128]{1,0:T(8,128)(2,1)S(1)}, bf16[96,128]{1,0:T(8,128)(2,1)S(1)}, u32[]{:S(2)}, u32[]{:S(2)}) %collective-permute-start.2) | collective-permute-done | bytes 24608 | tf_op jit(solution)/shard_map/ppermute | solution.py:357
  13.4 0.0 collective-permute-done.3.first_ref
  13.4 0.9 %shard_map.64 = (bf16[64,768]{1,0:T(8,128)(2,1)S(1)}, f32[208,128]{1,0:T(8,128)S(1)}) custom-call(f32[432,128]{1,0:T(8,128)S(1)} %get-tuple-element.25.own_ref, f32[24,128]{1,0:T(8,128)S(1)} %get-tuple-element.26.centre_ref, bf16[96,128]{1,0:T(8,128)(2,1)S(1)} %collective-permute-done.2.second_ref, bf16[96,128]{1,0:T(8,128)(2,1)S(1)} %collective-permute-done.3.first_ref, ...), custom_call_target="tpu_custom_call" | custom-call | flops 67108864 | bytes 1048576 | tf_op jit(solution)/shard_map/pallas_call | solution.py:344
  14.4 0.3 collective-permute-start.4
  14.7 1.2 %shard_map.65 = bf16[64,8,128]{2,1,0:T(8,128)(2,1)} custom-call(bf16[128,768]{1,0:T(8,128)(2,1)S(1)} %get-tuple-element.35.weight_ref, bf16[512,768]{1,0:T(8,128)(2,1)S(1)} %get-tuple-element.36.inner_ref, bf16[64,768]{1,0:T(8,128)(2,1)S(1)} %get-tuple-element.37.rim_ref), custom_call_target="tpu_custom_call" | custom-call | flops 1048576 | bytes 1048576 | tf_op jit(solution)/shard_map/pallas_call | solution.py:344
  15.9 2.1 %collective-permute-done.4 = f16[208,128]{1,0:T(8,128)(2,1)S(1)} collective-permute-done((f16[208,128]{1,0:T(8,128)(2,1)S(1)}, f16[208,128]{1,0:T(8,128)(2,1)S(1)}, u32[]{:S(2)}, u32[]{:S(2)}) %collective-permute-start.4) | collective-permute-done | bytes 53280 | tf_op jit(solution)/shard_map/ppermute | solution.py:357
  18.1 0.8 %collective-permute-start.5 = (f16[208,128]{1,0:T(8,128)(2,1)S(1)}, f16[208,128]{1,0:T(8,128)(2,1)S(1)}, u32[]{:S(2)}, u32[]{:S(2)}) collective-permute-start(f16[208,128]{1,0:T(8,128)(2,1)S(1)} %convert_element_type.48), channel_id=1, source_target_pairs={{0,9},{1,4},{2,7},{3,10},{4,1},{5,12},{6,15},{7,2},{8,13},{9,0},{1... | collective-permute-start | bytes 159752 | tf_op jit(solution)/shard_map/ppermute | solution.py:357
  18.9 2.8 %collective-permute-done.5 = f16[208,128]{1,0:T(8,128)(2,1)S(1)} collective-permute-done((f16[208,128]{1,0:T(8,128)(2,1)S(1)}, f16[208,128]{1,0:T(8,128)(2,1)S(1)}, u32[]{:S(2)}, u32[]{:S(2)}) %collective-permute-start.5) | collective-permute-done | bytes 53280 | tf_op jit(solution)/shard_map/ppermute | solution.py:357
  21.8 1.4 %collective-permute-start.6 = (f16[208,128]{1,0:T(8,128)(2,1)S(1)}, f16[208,128]{1,0:T(8,128)(2,1)S(1)}, u32[]{:S(2)}, u32[]{:S(2)}) collective-permute-start(f16[208,128]{1,0:T(8,128)(2,1)S(1)} %convert_element_type.51), channel_id=1, source_target_pairs={{0,5},{1,16},{2,19},{3,6},{4,21},{5,0},{6,3},{7,22},{8,25},{9,12},... | collective-permute-start | bytes 159752 | tf_op jit(solution)/shard_map/ppermute | solution.py:357
  23.2 2.2 %collective-permute-done.6 = f16[208,128]{1,0:T(8,128)(2,1)S(1)} collective-permute-done((f16[208,128]{1,0:T(8,128)(2,1)S(1)}, f16[208,128]{1,0:T(8,128)(2,1)S(1)}, u32[]{:S(2)}, u32[]{:S(2)}) %collective-permute-start.6) | collective-permute-done | bytes 53280 | tf_op jit(solution)/shard_map/ppermute | solution.py:357
  25.4 1.7 %collective-permute-start.7 = (f16[208,128]{1,0:T(8,128)(2,1)S(1)}, f16[208,128]{1,0:T(8,128)(2,1)S(1)}, u32[]{:S(2)}, u32[]{:S(2)}) collective-permute-start(f16[208,128]{1,0:T(8,128)(2,1)S(1)} %convert_element_type.54), channel_id=1, source_target_pairs={{0,17},{1,2},{2,1},{3,18},{4,7},{5,20},{6,23},{7,4},{8,11},{9,24},... | collective-permute-start | bytes 159752 | tf_op jit(solution)/shard_map/ppermute | solution.py:357
  27.2 2.8 %collective-permute-done.7 = f16[208,128]{1,0:T(8,128)(2,1)S(1)} collective-permute-done((f16[208,128]{1,0:T(8,128)(2,1)S(1)}, f16[208,128]{1,0:T(8,128)(2,1)S(1)}, u32[]{:S(2)}, u32[]{:S(2)}) %collective-permute-start.7) | collective-permute-done | bytes 53280 | tf_op jit(solution)/shard_map/ppermute | solution.py:357
  30.0 0.5 %collective-permute-start.8 = (f16[208,128]{1,0:T(8,128)(2,1)S(1)}, f16[208,128]{1,0:T(8,128)(2,1)S(1)}, u32[]{:S(2)}, u32[]{:S(2)}) collective-permute-start(f16[208,128]{1,0:T(8,128)(2,1)S(1)} %convert_element_type.57), channel_id=1, source_target_pairs={{0,1},{1,0},{2,3},{3,2},{4,5},{5,4},{6,7},{7,6},{8,9},{9,8},{10,11... | collective-permute-start | bytes 159752 | tf_op jit(solution)/shard_map/ppermute | solution.py:357
  30.5 0.9 %collective-permute-done.8 = f16[208,128]{1,0:T(8,128)(2,1)S(1)} collective-permute-done((f16[208,128]{1,0:T(8,128)(2,1)S(1)}, f16[208,128]{1,0:T(8,128)(2,1)S(1)}, u32[]{:S(2)}, u32[]{:S(2)}) %collective-permute-start.8) | collective-permute-done | bytes 53280 | tf_op jit(solution)/shard_map/ppermute | solution.py:357
  31.4 0.8 %shard_map.70 = f32[6,64,64]{2,1,0:T(8,128)} custom-call(f32[208,128]{1,0:T(8,128)S(1)} %convert_element_type.58.mine_ref, f32[208,128]{1,0:T(8,128)S(1)} %convert_element_type.59.other_ref), custom_call_target="tpu_custom_call" | custom-call | flops 65536 | bytes 1048576 | tf_op jit(solution)/shard_map/pallas_call | solution.py:344
  (20 shorter events, 0.3 us)
Async XLA Ops:
  0.6 0.9 %copy-start.1 = (bf16[64,8,128]{2,1,0:T(8,128)(2,1)S(1)}, bf16[64,8,128]{2,1,0:T(8,128)(2,1)}, u32[]{:S(2)}) copy-start(bf16[64,8,128]{2,1,0:T(8,128)(2,1)} %cot_ref.1) | copy-start | bytes 393220
  0.6 0.7 %copy-start.3 = (s32[8,128]{1,0:T(8,128)S(1)}, s32[8,128]{1,0:T(8,128)}, u32[]{:S(2)}) copy-start(s32[8,128]{1,0:T(8,128)} %mask_ref.1) | copy-start | bytes 12292
  1.4 5.1 %copy-start.2 = (bf16[6,64,64]{2,1,0:T(8,128)(2,1)S(1)}, bf16[6,64,64]{2,1,0:T(8,128)(2,1)}, u32[]{:S(2)}) copy-start(bf16[6,64,64]{2,1,0:T(8,128)(2,1)} %weight_ref.1) | copy-start | bytes 147460
  1.6 4.9 %copy-start = (bf16[64,8,128]{2,1,0:T(8,128)(2,1)S(1)}, bf16[64,8,128]{2,1,0:T(8,128)(2,1)}, u32[]{:S(2)}) copy-start(bf16[64,8,128]{2,1,0:T(8,128)(2,1)} %feature_ref.1) | copy-start | bytes 393220
  1.8 5.0 %collective-permute-start = (bf16[336,128]{1,0:T(8,128)(2,1)S(1)}, bf16[336,128]{1,0:T(8,128)(2,1)S(1)}, u32[]{:S(2)}, u32[]{:S(2)}) collective-permute-start(bf16[336,128]{1,0:T(8,128)(2,1)S(1)} %get-tuple-element.22), channel_id=1, source_target_pairs={{0,1},{1,0},{2,3},{3,2},{4,5},{5,4},{6,7},{7,6},{8,16},{9,17},{10,... | collective-permute-start | bytes 258056 | tf_op jit(solution)/shard_map/ppermute | solution.py:357
  2.3 6.6 %collective-permute-start.1 = (bf16[336,128]{1,0:T(8,128)(2,1)S(1)}, bf16[336,128]{1,0:T(8,128)(2,1)S(1)}, u32[]{:S(2)}, u32[]{:S(2)}) collective-permute-start(bf16[336,128]{1,0:T(8,128)(2,1)S(1)} %get-tuple-element.23), channel_id=1, source_target_pairs={{0,8},{1,9},{2,10},{3,11},{4,12},{5,13},{6,14},{7,15},{8,0},{9,1},... | collective-permute-start | bytes 258056 | tf_op jit(solution)/shard_map/ppermute | solution.py:357
  9.0 4.4 %collective-permute-start.2 = (bf16[96,128]{1,0:T(8,128)(2,1)S(1)}, bf16[96,128]{1,0:T(8,128)(2,1)S(1)}, u32[]{:S(2)}, u32[]{:S(2)}) collective-permute-start(bf16[96,128]{1,0:T(8,128)(2,1)S(1)} %get-tuple-element.27), channel_id=1, source_target_pairs={{0,7},{1,2},{2,1},{3,4},{4,3},{5,6},{6,5},{7,0},{8,15},{9,10},{10,... | collective-permute-start | bytes 73736 | tf_op jit(solution)/shard_map/ppermute | solution.py:357
  9.8 3.6 %collective-permute-start.3 = (bf16[96,128]{1,0:T(8,128)(2,1)S(1)}, bf16[96,128]{1,0:T(8,128)(2,1)S(1)}, u32[]{:S(2)}, u32[]{:S(2)}) collective-permute-start(bf16[96,128]{1,0:T(8,128)(2,1)S(1)} %get-tuple-element.28), channel_id=1, source_target_pairs={{0,1},{1,0},{2,3},{3,2},{4,5},{5,4},{6,7},{7,6},{8,9},{9,8},{10,11... | collective-permute-start | bytes 73736 | tf_op jit(solution)/shard_map/ppermute | solution.py:357
  14.4 3.6 %collective-permute-start.4 = (f16[208,128]{1,0:T(8,128)(2,1)S(1)}, f16[208,128]{1,0:T(8,128)(2,1)S(1)}, u32[]{:S(2)}, u32[]{:S(2)}) collective-permute-start(f16[208,128]{1,0:T(8,128)(2,1)S(1)} %convert_element_type.45), channel_id=1, source_target_pairs={{0,3},{1,8},{2,11},{3,0},{4,13},{5,6},{6,5},{7,14},{8,1},{9,10},{1... | collective-permute-start | bytes 159752 | tf_op jit(solution)/shard_map/ppermute | solution.py:357
  18.1 3.6 %collective-permute-start.5 = (f16[208,128]{1,0:T(8,128)(2,1)S(1)}, f16[208,128]{1,0:T(8,128)(2,1)S(1)}, u32[]{:S(2)}, u32[]{:S(2)}) collective-permute-start(f16[208,128]{1,0:T(8,128)(2,1)S(1)} %convert_element_type.48), channel_id=1, source_target_pairs={{0,9},{1,4},{2,7},{3,10},{4,1},{5,12},{6,15},{7,2},{8,13},{9,0},{1... | collective-permute-start | bytes 159752 | tf_op jit(solution)/shard_map/ppermute | solution.py:357
  21.8 3.6 %collective-permute-start.6 = (f16[208,128]{1,0:T(8,128)(2,1)S(1)}, f16[208,128]{1,0:T(8,128)(2,1)S(1)}, u32[]{:S(2)}, u32[]{:S(2)}) collective-permute-start(f16[208,128]{1,0:T(8,128)(2,1)S(1)} %convert_element_type.51), channel_id=1, source_target_pairs={{0,5},{1,16},{2,19},{3,6},{4,21},{5,0},{6,3},{7,22},{8,25},{9,12},... | collective-permute-start | bytes 159752 | tf_op jit(solution)/shard_map/ppermute | solution.py:357
  25.4 4.5 %collective-permute-start.7 = (f16[208,128]{1,0:T(8,128)(2,1)S(1)}, f16[208,128]{1,0:T(8,128)(2,1)S(1)}, u32[]{:S(2)}, u32[]{:S(2)}) collective-permute-start(f16[208,128]{1,0:T(8,128)(2,1)S(1)} %convert_element_type.54), channel_id=1, source_target_pairs={{0,17},{1,2},{2,1},{3,18},{4,7},{5,20},{6,23},{7,4},{8,11},{9,24},... | collective-permute-start | bytes 159752 | tf_op jit(solution)/shard_map/ppermute | solution.py:357
  30.0 1.4 %collective-permute-start.8 = (f16[208,128]{1,0:T(8,128)(2,1)S(1)}, f16[208,128]{1,0:T(8,128)(2,1)S(1)}, u32[]{:S(2)}, u32[]{:S(2)}) collective-permute-start(f16[208,128]{1,0:T(8,128)(2,1)S(1)} %convert_element_type.57), channel_id=1, source_target_pairs={{0,1},{1,0},{2,3},{3,2},{4,5},{5,4},{6,7},{7,6},{8,9},{9,8},{10,11... | collective-permute-start | bytes 159752 | tf_op jit(solution)/shard_map/ppermute | solution.py:357
